TPU v7x, 256 devices: a whole 4x4x8 slice. The times are simulated.
256 devices in a mesh: group: 16 (over x, z_hi), tensor: 16 (over z_lo, y, core).
Axes of the slice: x: 4, y: 4, z: 8 (z_hi: 4, z_lo: 2; z = z_hi * 2 + z_lo), core: 2. Of those that a mesh axis runs over, the one named last changes fastest.
Arguments:
- tokens: bfloat16 [12288, 8192], P('group', 'tensor'), may hold values from -6 to 6
- base_values: bfloat16 [8192, 8192], P('tensor'), may hold values from -0.09375 to 0.09375
- base_scales: float32 [64, 64], P('tensor'), may hold values from 0.3 to 3
- shrink_factors: bfloat16 [32, 8192, 64], P('group', 'tensor'), may hold values from -0.0625 to 0.0625
- expand_factors: bfloat16 [32, 64, 8192], P('group', None, 'tensor'), may hold values from -0.75 to 0.75
- adapter_slot: int32 [32], replicated, may hold values from 0 to 31, each once
- tile_adapter: int32 [192], P('group'), may hold values from 0 to 31, as said below
- tile_count: int32 [192], P('group'), may hold values from 1 to 64, as said below
Outputs:
- mixed: bfloat16 [12288, 8192], P('group', 'tensor')
Inputs may be any that keep to these rules, and one draw needn't show every extreme that they name: `tile_adapter`: every adapter is named by at least one segment. `tile_count`: the first segment of each group's rows is full.
All inputs are finite; a program needn't handle non-finite values.
Results may differ from a plain program's by a relative error of at most 0.023.
Values may be sent and summed in bfloat16 or wider, within the bound.
No kernel may reach another device: no remote copies, remote signals or barrier semaphores. Data moves between devices by JAX's collectives and lax.ppermute only.
A program may use at most 128 MiB of HBM per device.

v0:
```python
import jax
import jax.numpy as jnp
from jax import lax
from jax.sharding import PartitionSpec as P

BLK = 128
TILE = 64


def select_slots(tile_adapter, adapter_slot):
    adapter_ids = jnp.arange(adapter_slot.shape[0], dtype=jnp.int32)
    matches = tile_adapter[:, None] == adapter_ids[None, :]
    return jnp.sum(jnp.where(matches, adapter_slot[None, :], 0), axis=1)


def body(
    tokens,
    base_values,
    base_scales,
    shrink_factors,
    expand_factors,
    adapter_slot,
    tile_adapter,
    tile_count,
):
    row_count, feat_count = tokens.shape
    col_count = base_values.shape[1]
    tile_total = row_count // TILE
    tile_slots = select_slots(tile_adapter, adapter_slot)
    tok_tiles = tokens.reshape(tile_total, TILE, feat_count)
    scaled = (
        base_values.reshape(feat_count // BLK, BLK, col_count // BLK, BLK).astype(jnp.float32)
        * base_scales[:, None, :, None]
    )
    weights = scaled.reshape(feat_count, col_count).astype(jnp.bfloat16)
    partial_sum = jnp.dot(tokens, weights, preferred_element_type=jnp.float32)
    partial_sum = lax.optimization_barrier(partial_sum.astype(jnp.bfloat16)).astype(jnp.float32)
    shrink_all, expand_all = (
        lax.all_gather(shrink_factors, "group", axis=0, tiled=True),
        lax.all_gather(expand_factors, "group", axis=0, tiled=True),
    )
    shrink_part = jnp.einsum(
        "tlf,tfr->tlr", tok_tiles, shrink_all[tile_slots], preferred_element_type=jnp.float32
    )
    shrink_part = lax.optimization_barrier(shrink_part.astype(jnp.bfloat16)).astype(jnp.float32)
    shrink_total = lax.psum(shrink_part.astype(jnp.bfloat16), "tensor")
    base_out = lax.psum_scatter(
        partial_sum.astype(jnp.bfloat16), "tensor", scatter_dimension=1, tiled=True
    ).astype(jnp.float32)
    delta = jnp.einsum(
        "tlr,trw->tlw", shrink_total, expand_all[tile_slots], preferred_element_type=jnp.float32
    )
    alive = jnp.arange(TILE, dtype=jnp.int32)[None, :] < tile_count[:, None]
    delta = jnp.where(alive[:, :, None], delta, 0.0)
    return (base_out + delta.reshape(row_count, base_out.shape[1])).astype(jnp.bfloat16)


def solution(mesh):
    in_specs = (
        P("group", "tensor"),
        P("tensor", None),
        P("tensor", None),
        P("group", "tensor", None),
        P("group", None, "tensor"),
        P(),
        P("group"),
        P("group"),
    )
    out_specs = P("group", "tensor")
    return jax.shard_map(body, mesh=mesh, in_specs=in_specs, out_specs=out_specs, check_vma=False)
```

profile of v0, /device:TPU:8, one launch (start us, length us, event | category | flops | bytes accessed | tf_op | source)
XLA Modules:
  0.0 342.1 jit_solution(14419440087264037335)
XLA Ops:
  6.5 0.0 copy-start
  6.5 0.0 all-gather.3.cloned.1.call-start
  6.5 0.7 all-gather.3.cloned.1.call-update
  7.3 0.0 all-gather.5.cloned.1.call-start
  7.3 0.7 all-gather.5.cloned.1.call-update
  8.0 0.0 all-reduce.2.cloned.1.call-start
  8.1 0.9 select_reduce_fusion
  8.9 62.9 %all-gather.3.cloned.1.call-done = bf16[32,512,64]{1,2,0:T(8,128)(2,1)} async-done(((bf16[2,512,64]{1,2,0:T(8,128)(2,1)}), bf16[32,512,64]{1,2,0:T(8,128)(2,1)}) %all-gather.3.cloned.1.call-update) | async-done | bytes 2097168 | tf_op jit(solution)/shard_map/all_gather | solution.py:39
  71.9 2.2 gather_fusion
  74.1 0.0 copy-done
  74.1 1.0 fusion.3
  75.1 0.0 all-reduce.2.cloned.1.call-update
  75.1 0.0 reduce-scatter.2.cloned.1.call-start
  75.2 8.6 %mul.11 = f32[4,128,64,128]{3,2,1,0:T(8,128)} broadcast(f32[4,64]{1,0:T(4,128)} %param.10), dimensions={0,2} | broadcast | bytes 16778240 | tf_op jit(solution)/shard_map/mul | solution.py:32
  83.8 61.8 %fusion.1 = bf16[768,8192]{0,1:T(8,128)(2,1)} fusion(bf16[768,512]{1,0:T(8,128)(2,1)S(1)} %copy-done, f32[64,8,64,128]{3,2,1,0:T(8,128)} %bitcast.23, bf16[512,8192]{1,0:T(8,128)(2,1)} %param.9), kind=kOutput, calls=%fused_computation.5 | convolution fusion | flops 6461325312 | bytes 38535168 | tf_op jit(solution)/shard_map/dot_general | solution.py:36
  145.5 0.0 copy-start.1
  145.5 0.0 reduce-scatter.2.cloned.1.call-update
  145.6 0.6 copy-done.1
  146.2 0.1 iota_compare_fusion.1
  146.3 0.0 all-gather.5.cloned.1.call-done
  146.3 2.2 gather_fusion.1
  148.5 98.9 %all-reduce.2.cloned.1.call-done = bf16[12,64,64]{1,2,0:T(8,128)(2,1)} async-done(((bf16[12,64,64]{1,2,0:T(8,128)(2,1)}), bf16[12,64,64]{1,2,0:T(8,128)(2,1)}) %all-reduce.2.cloned.1.call-update) | async-done | bytes 98320 | tf_op jit(solution)/shard_map/psum | solution.py:46
  247.4 2.5 convolution_select_fusion
  249.9 1.9 copy.17
  251.8 81.4 %reduce-scatter.2.cloned.1.call-done = bf16[768,512]{0,1:T(8,128)(2,1)} async-done(((bf16[768,8192]{0,1:T(8,128)(2,1)}), bf16[768,512]{0,1:T(8,128)(2,1)}) %reduce-scatter.2.cloned.1.call-update) | async-done | bytes 786448 | tf_op jit(solution)/shard_map/reduce_scatter | solution.py:47
  333.1 1.3 add_convert_fusion
  334.4 1.2 copy.18
  (2 shorter events, 0.0 us)
Async XLA Ops:
  6.5 67.5 %copy-start = (bf16[768,512]{1,0:T(8,128)(2,1)S(1)}, bf16[768,512]{1,0:T(8,128)(2,1)}, u32[]{:S(2)}) copy-start(bf16[768,512]{1,0:T(8,128)(2,1)} %param.8) | copy-start | bytes 2359300
  6.5 65.3 %all-gather.3.cloned.1.call-start = ((), (), s32[]{:S(2)}) async-start(), calls=%async_computation.2 | async-start | bytes 2228224 | tf_op jit(solution)/shard_map/all_gather | solution.py:39
  7.3 139.0 %all-gather.5.cloned.1.call-start = ((), (), s32[]{:S(2)}) async-start(), calls=%async_computation.4 | async-start | bytes 2228224 | tf_op jit(solution)/shard_map/all_gather | solution.py:40
  8.0 239.4 %all-reduce.2.cloned.1.call-start = ((), (), s32[]{:S(2)}) async-start(), calls=%async_computation.3 | async-start | bytes 393216 | tf_op jit(solution)/shard_map/psum | solution.py:46
  75.1 258.0 %reduce-scatter.2.cloned.1.call-start = ((), (), s32[]{:S(2)}) async-start(), calls=%async_computation.1 | async-start | bytes 13369344 | tf_op jit(solution)/shard_map/reduce_scatter | solution.py:47
  145.5 0.7 copy-start.1
Sparse Core Ops, SparseCore 0:
  9.8 62.0 all-gather.2
  74.3 57.3 all-gather.4
  134.3 112.9 all-reduce.1
  250.0 83.1 reduce-scatter.1
where the time goes:
time: 347 us; the launch traced here: 342 us
  waiting for transfers between devices  245 us (71%)
  matrix products  65.3 us (19%)
  local copies, waits for them, and re-layouts  16.7 us (5%)
  between operations  13.2 us (4%)
    psum x1, waiting for transfers between devices, body(): shrink_total = lax.psum(shrink_part.astype(jnp.bfloat16), 'tensor')  98.9 us
    reduce_scatter x1, waiting for transfers between devices, body(): lax.psum_scatter(partial_sum.astype(jnp.bfloat16), 'tensor', scatter_dime...  81.4 us
    all_gather x1, waiting for transfers between devices, body(): lax.all_gather(shrink_factors, 'group', axis=0, tiled=True)  62.9 us
    dot_general x1, matrix products, body(): partial_sum = jnp.dot(tokens, weights, preferred_element_type=jnp.float32)  61.8 us
    mul x1, local copies, waits for them, and re-layouts, body(): base_values.reshape(feat_count // BLK, BLK, col_count // BLK, BLK)  8.61 us
  transfers between devices with their start and end apart: 4, of which 3 were waited for; matrix products, arithmetic and copies ran while one was open for 24% of the time, Pallas kernels for 0%

commit v1 on v0

v1 whole, which is shorter than its diff:
```python
import functools

import jax
import jax.numpy as jnp
from jax import lax
from jax.experimental import pallas as pl
from jax.experimental.pallas import tpu as pltpu
from jax.sharding import Mesh, PartitionSpec as P

BLK = 128
TILE = 64
AXES = ("x", "zh", "zl", "y", "c")
SIZES = (4, 4, 2, 4, 2)
VMEM_LIMIT = 56 * 1024 * 1024
F32 = jnp.float32
BF16 = jnp.bfloat16

CHUNKS = (("B", 288), ("B", 288), ("A", 192))


def shift(value, axis, step):
    size = SIZES[AXES.index(axis)]
    return lax.ppermute(value, axis, [(i, (i + step) % size) for i in range(size)])


def params(**kw):
    return pltpu.CompilerParams(vmem_limit_bytes=VMEM_LIMIT, **kw)


def cost(flops, nbytes):
    return pl.CostEstimate(flops=flops, bytes_accessed=nbytes, transcendentals=0)


def scaled(w_ref, scale_ref, block):
    rows, cols = w_ref.shape
    out = []
    for i in range(rows // BLK):
        parts = [
            (
                w_ref[i * BLK : (i + 1) * BLK, j * BLK : (j + 1) * BLK].astype(F32)
                * scale_ref[i, block * (cols // BLK) + j]
            ).astype(BF16)
            for j in range(cols // BLK)
        ]
        out.append(jnp.concatenate(parts, axis=1))
    return jnp.concatenate(out, axis=0)


def prep_kernel(blocks_ref, w_ref, scale_ref, out_ref):
    out_ref[0] = scaled(w_ref, scale_ref, blocks_ref[pl.program_id(0)])


def prep(values, scales, blocks, width):
    feats = values.shape[0]
    n = blocks.shape[0]
    return pl.pallas_call(
        prep_kernel,
        out_shape=jax.ShapeDtypeStruct((n, feats, width), BF16),
        grid_spec=pltpu.PrefetchScalarGridSpec(
            num_scalar_prefetch=1,
            grid=(n,),
            in_specs=[
                pl.BlockSpec((feats, width), lambda j, b: (0, b[j])),
                pl.BlockSpec(memory_space=pltpu.SMEM),
            ],
            out_specs=pl.BlockSpec((1, feats, width), lambda j, b: (j, 0, 0)),
        ),
        compiler_params=params(),
        cost_estimate=cost(0, 4 * n * feats * width),
        name="prep",
    )(blocks, values, scales)


def partial_kernel(plan, blocks_ref, x_ref, xs_ref, w_ref, ws_ref, scale_ref, *rest):
    outs, w_scr = rest[:-1], rest[-1]
    step = pl.program_id(0)
    w_scr[...] = scaled(w_ref, scale_ref, blocks_ref[step])
    starts = {}
    for steps, out, start, rows in plan:
        starts.setdefault((start, rows), []).append((steps, out))
    for (start, rows), stores in starts.items():
        value = (
            jnp.dot(x_ref[start : start + rows], w_scr[...], preferred_element_type=F32)
            + jnp.dot(xs_ref[start : start + rows], ws_ref[0], preferred_element_type=F32)
        ).astype(BF16)
        for steps, out in stores:
            if len(steps) == pl.num_programs(0):
                outs[out][0] = value
            else:

                @pl.when((step >= steps[0]) & (step <= steps[-1]))
                def _(out=out, value=value):
                    outs[out][0] = value


def partials(tokens, other, values, others, scales, blocks, plan):
    rows, feats = tokens.shape
    width = others.shape[2]
    n = blocks.shape[0]
    stores = [
        (tuple(range(first, first + count)), i, start, size)
        for i, (first, count, start, size) in enumerate(plan)
    ]

    def out_map(first, count):
        return lambda j, b: (jnp.clip(j - first, 0, count - 1), 0, 0)

    return pl.pallas_call(
        functools.partial(partial_kernel, stores),
        out_shape=[
            jax.ShapeDtypeStruct((count, size, width), BF16)
            for _, count, _, size in plan
        ],
        grid_spec=pltpu.PrefetchScalarGridSpec(
            num_scalar_prefetch=1,
            grid=(n,),
            in_specs=[
                pl.BlockSpec((rows, feats), lambda j, b: (0, 0)),
                pl.BlockSpec((rows, feats), lambda j, b: (0, 0)),
                pl.BlockSpec((feats, width), lambda j, b: (0, b[j])),
                pl.BlockSpec((1, feats, width), lambda j, b: (j, 0, 0)),
                pl.BlockSpec(memory_space=pltpu.SMEM),
            ],
            out_specs=[
                pl.BlockSpec((1, size, width), out_map(first, count))
                for first, count, _, size in plan
            ],
            scratch_shapes=[pltpu.VMEM((feats, width), BF16)],
        ),
        compiler_params=params(),
        cost_estimate=cost(4 * n * rows * feats * width, 2 * n * width * (2 * feats + rows)),
        name="partials",
    )(blocks, tokens, other, values, others, scales)


def whole_call(kernel, shapes, *args, name, specs=None, aliases=None):
    return pl.pallas_call(
        kernel,
        out_shape=shapes,
        in_specs=specs or [pl.BlockSpec(memory_space=pltpu.VMEM)] * len(args),
        out_specs=jax.tree.map(lambda _: pl.BlockSpec(memory_space=pltpu.VMEM), shapes),
        compiler_params=params(),
        cost_estimate=cost(0, sum(2 * a.size for a in args)),
        name=name,
    )(*args)


def plus(*parts):
    total = parts[0].astype(F32)
    for part in parts[1:]:
        total = total + part.astype(F32)
    return total.astype(BF16)


def carry_kernel(up_ref, down_ref, got_up_ref, got_down_ref, up_out, down_out):
    up_out[...] = plus(up_ref[...], got_up_ref[...])
    down_out[...] = plus(down_ref[...], got_down_ref[...])


def carry(up, down, got_up, got_down):
    count, rows, width = up.shape
    half = rows // 2
    first = pl.BlockSpec((1, half, width), lambda j: (j, 0, 0))
    second = pl.BlockSpec((1, half, width), lambda j: (j, 1, 0))
    return pl.pallas_call(
        carry_kernel,
        out_shape=[jax.ShapeDtypeStruct(up.shape, BF16)] * 2,
        grid=(count,),
        in_specs=[first, second, first, first],
        out_specs=[first, second],
        input_output_aliases={0: 0, 1: 1},
        compiler_params=params(),
        cost_estimate=cost(0, 6 * count * rows * width),
        name="carry",
    )(up, down, got_up, got_down)


def locate(slot_ref, adapter_ref, place_ref, tile):
    slot = slot_ref[adapter_ref[tile]]
    dx = lax.rem(slot // 8 - place_ref[0] + 4, 4)
    dz = lax.rem(lax.rem(slot // 2, 4) - place_ref[1] + 4, 4)
    return dx, dz * 2 + lax.rem(slot, 2)


def fetch(tiles, slot_ref, adapter_ref, place_ref, buffers, held, sems):
    own, near, far_a, far_b, back = buffers
    for t in range(tiles):
        dx, at = locate(slot_ref, adapter_ref, place_ref, t)
        for cond, ref, index in (
            (dx == 0, own, at),
            (dx == 1, near, at),
            ((dx == 2) & (at < 4), far_a, at),
            ((dx == 2) & (at >= 4), far_b, at - 4),
            (dx == 3, back, at),
        ):

            @pl.when(cond)
            def _(ref=ref, index=index, t=t):
                pltpu.make_async_copy(
                    ref.at[index], held.at[pl.ds(t * TILE, TILE)], sems.at[t]
                ).start()


def wait_for(t, buffers, held, sems):
    pltpu.make_async_copy(
        buffers[0].at[0], held.at[pl.ds(t * TILE, TILE)], sems.at[t]
    ).wait()


def shrink_kernel(slot_ref, adapter_ref, place_ref, x_ref, *rest):
    buffers, out_ref, held, sems = rest[:5], rest[5], rest[6], rest[7]
    tiles = adapter_ref.shape[0]
    fetch(tiles, slot_ref, adapter_ref, place_ref, buffers, held, sems)
    left = lax.broadcasted_iota(jnp.int32, (TILE, 2 * TILE), 1) < TILE
    for t in range(0, tiles, 2):
        wait_for(t, buffers, held, sems)
        wait_for(t + 1, buffers, held, sems)
        both = lax.dot_general(
            x_ref[t * TILE : (t + 2) * TILE],
            held[t * TILE : (t + 2) * TILE],
            (((1,), (1,)), ((), ())),
            preferred_element_type=F32,
        )
        out_ref[t * TILE // 2 : (t + 2) * TILE // 2] = jnp.where(
            left, both[:TILE], both[TILE:]
        ).astype(BF16)


def expand_kernel(slot_ref, adapter_ref, place_ref, count_ref, s0, s1, s2, s3, *rest):
    buffers, out_ref, held, sems = rest[:5], rest[5], rest[6], rest[7]
    tiles = adapter_ref.shape[0]
    fetch(tiles, slot_ref, adapter_ref, place_ref, buffers, held, sems)
    left = lax.broadcasted_iota(jnp.int32, (TILE, 2 * TILE), 1) < TILE
    for t in range(0, tiles, 2):
        wait_for(t, buffers, held, sems)
        wait_for(t + 1, buffers, held, sems)
        at = pl.ds(t * TILE // 2, TILE)
        total = (
            s0[at].astype(F32) + s1[at].astype(F32) + s2[at].astype(F32) + s3[at].astype(F32)
        )
        factors = held[t * TILE : (t + 2) * TILE]
        for k in range(2):
            shrink = jnp.where(left == (k == 0), total, 0.0).astype(BF16)
            delta = jnp.dot(shrink, factors, preferred_element_type=F32)
            row = lax.broadcasted_iota(jnp.int32, delta.shape, 0)
            out_ref[(t + k) * TILE : (t + k + 1) * TILE] = jnp.where(
                row < count_ref[t + k], delta, 0.0
            )


def with_factors(kernel, shape, scalars, arrays, buffers, width, tiles, name):
    return pl.pallas_call(
        kernel,
        out_shape=shape,
        in_specs=[pl.BlockSpec(memory_space=pltpu.SMEM)] * len(scalars)
        + [pl.BlockSpec(memory_space=pltpu.VMEM)] * len(arrays)
        + [pl.BlockSpec(memory_space=pl.ANY)] * len(buffers),
        out_specs=pl.BlockSpec(memory_space=pltpu.VMEM),
        scratch_shapes=[
            pltpu.VMEM((tiles * TILE, width), BF16),
            pltpu.SemaphoreType.DMA((tiles,)),
        ],
        compiler_params=params(),
        cost_estimate=cost(2 * tiles * TILE * TILE * width, 6 * tiles * TILE * width),
        name=name,
    )(*scalars, *arrays, *buffers)


def gather_factors(mine):
    ahead = shift(mine, "zh", -1)
    behind = shift(mine, "zh", 1)
    across = shift(mine, "zh", 2)
    line = jnp.concatenate([mine, ahead, across, behind], axis=0)
    near = shift(line, "x", -1)
    back = shift(line, "x", 1)
    far_a = shift(near[:4], "x", -1)
    far_b = shift(back[4:], "x", 1)
    return line, near, far_a, far_b, back


def finish_kernel(spans, delta_ref, *rest):
    refs, out_ref = rest[:-1], rest[-1]
    for start, rows, first, count in spans:
        total = delta_ref[start : start + rows]
        for ref in refs[first : first + count]:
            total = total + ref[0].astype(F32)
        out_ref[start : start + rows] = total.astype(BF16)


def body(
    tokens,
    base_values,
    base_scales,
    shrink_factors,
    expand_factors,
    adapter_slot,
    tile_adapter,
    tile_count,
):
    rows, feats = tokens.shape
    tiles = rows // TILE
    width = base_values.shape[1] // 16
    x, zh, zl, y, c = (lax.axis_index(name).astype(jnp.int32) for name in AXES)
    place = jnp.stack([x, zh])

    def block(core, dz, dy):
        return (zl ^ dz) * 8 + ((y + dy) % 4) * 2 + core

    order_far = [(0, 2), (1, 2)]
    order_near = [(0, 1), (1, 1), (0, 3), (1, 3), (0, 0), (1, 0)]
    far_mine = jnp.stack([block(c, *o) for o in order_far])
    near_mine = jnp.stack([block(c, *o) for o in order_near])
    far_theirs = jnp.stack([block(1 - c, *o) for o in order_far])
    near_theirs = jnp.stack([block(1 - c, *o) for o in order_near])

    other = shift(tokens, "c", 1)
    down = gather_factors(jnp.swapaxes(shrink_factors, 1, 2))
    far_weights = shift(prep(base_values, base_scales, far_theirs, width), "c", 1)
    near_weights = shift(prep(base_values, base_scales, near_theirs, width), "c", 1)
    up = gather_factors(expand_factors)

    starts, at = [], 0
    for _, size in CHUNKS:
        starts.append(at)
        at += size

    plan = []
    for (kind, size), start in zip(CHUNKS, starts):
        if kind == "B":
            half = size // 2
            plan += [(0, 2, start, half), (0, 2, start + half, half)]
        else:
            plan += [(0, 1, start, size), (1, 1, start, size)]
    far = partials(tokens, other, base_values, far_weights, base_scales, far_mine, plan)
    far = [far[2 * i : 2 * i + 2] for i in range(len(CHUNKS))]

    plan = []
    for (kind, size), start in zip(CHUNKS, starts):
        if kind == "B":
            plan += [(0, 2, start, size), (2, 2, start, size), (4, 2, start, size)]
        else:
            plan += [(j, 1, start, size) for j in range(6)]
    near = partials(tokens, other, base_values, near_weights, base_scales, near_mine, plan)

    pieces = []
    at = 0
    finals = []
    for i, ((kind, size), start) in enumerate(zip(CHUNKS, starts)):
        half = size // 2
        if kind == "B":
            up_block, down_block, own = near[at : at + 3]
            at += 3
            got_up = shift(far[i][0], "y", 1)
            got_down = shift(far[i][1], "y", -1)
            up_block, down_block = carry(up_block, down_block, got_up, got_down)
            from_below = shift(up_block, "y", 1)
            from_above = shift(down_block, "y", -1)
            leaving = plus(own[1:], from_below[1:], from_above[1:])
            got = shift(leaving, "zl", 1)
            finals.append((start, size, [own, from_below, from_above, got]))
        else:
            up0, up1, down0, down1, own0, own1 = near[at : at + 6]
            at += 6
            keep2, send2 = far[i]
            got2 = shift(send2, "zl", 1)
            got = shift(jnp.concatenate([up1, down1, own1], axis=0), "zl", 1)
            far_up = plus(keep2[:, :half], got2[:, :half])
            far_down = plus(keep2[:, half:], got2[:, half:])
            got_up = shift(far_up, "y", 1)
            got_down = shift(far_down, "y", -1)
            up_block = jnp.concatenate(
                [
                    plus(up0[:, :half], got[0:1, :half], got_up),
                    plus(up0[:, half:], got[0:1, half:]),
                ],
                axis=1,
            )
            down_block = jnp.concatenate(
                [
                    plus(down0[:, :half], got[1:2, :half]),
                    plus(down0[:, half:], got[1:2, half:], got_down),
                ],
                axis=1,
            )
            from_below = shift(up_block, "y", 1)
            from_above = shift(down_block, "y", -1)
            finals.append((start, size, [own0, got[2:], from_below, from_above]))

    scalars = (adapter_slot, tile_adapter, place)
    shrink = with_factors(
        shrink_kernel,
        jax.ShapeDtypeStruct((rows // 2, 2 * TILE), BF16),
        scalars,
        (tokens,),
        down,
        feats,
        tiles,
        "shrink",
    )
    shrink = plus(shrink, shift(shrink, "c", 1))
    shrink = plus(shrink, shift(shrink, "zl", 1))
    terms = (shrink, shift(shrink, "y", 1), shift(shrink, "y", -1), shift(shrink, "y", 2))
    delta = with_factors(
        expand_kernel,
        jax.ShapeDtypeStruct((rows, width), F32),
        scalars + (tile_count,),
        terms,
        up,
        width,
        tiles,
        "expand",
    )

    spans, args = [], []
    for start, size, parts in finals:
        spans.append((start, size, len(args), len(parts)))
        args += [(p, size) for p in parts]
    return pl.pallas_call(
        functools.partial(finish_kernel, spans),
        out_shape=jax.ShapeDtypeStruct((rows, width), BF16),
        grid=(1,),
        in_specs=[pl.BlockSpec((rows, width), lambda j: (0, 0))]
        + [pl.BlockSpec((1, size, width), lambda j: (0, 0, 0)) for _, size in args],
        out_specs=pl.BlockSpec((rows, width), lambda j: (0, 0)),
        compiler_params=params(),
        cost_estimate=cost(0, 14 * rows * width),
        name="finish",
    )(delta, *(p for p, _ in args))


def solution(mesh):
    split = Mesh(mesh.devices.reshape(SIZES), AXES)
    group, tensor = ("x", "zh"), ("zl", "y", "c")
    in_specs = (
        P(group, tensor),
        P(tensor, None),
        P(tensor, None),
        P(group, tensor, None),
        P(group, None, tensor),
        P(),
        P(group),
        P(group),
    )
    return jax.shard_map(
        body, mesh=split, in_specs=in_specs, out_specs=P(group, tensor), check_vma=False
    )
```

time: 347 us -> 161 us (0.46)
  the two profiles are of different devices: /device:TPU:8 before, /device:TPU:64 now
where the time goes in v1:
time: 161 us; the launch traced here: 160 us
  starting transfers between devices  57.5 us (36%)
  waiting for transfers between devices  47.5 us (30%)
  Pallas kernels  44 us (27%)
  local copies, waits for them, and re-layouts  6.87 us (4%)
  other arithmetic  3.55 us (2%)
    ppermute x38, starting transfers between devices, shift(): lax.ppermute(value, axis, [(i, (i + step) % size) for i in range(size)])  57.5 us
    ppermute x38, waiting for transfers between devices, shift(): lax.ppermute(value, axis, [(i, (i + step) % size) for i in range(size)])  47.5 us
    pallas_call x2, Pallas kernels, partials(): pl.pallas_call(functools.partial(partial_kernel, stores), out_shape=[jax....  18.6 us
    pallas_call x2, Pallas kernels, prep(): pl.pallas_call(prep_kernel, out_shape=jax.ShapeDtypeStruct((n, feats, wid...  9.23 us
    pallas_call x2, Pallas kernels, with_factors(): pl.pallas_call(kernel, out_shape=shape, in_specs=[pl.BlockSpec(memory_spa...  8.38 us
    unnamed x77, local copies, waits for them, and re-layouts  4.82 us
    pallas_call x2, Pallas kernels, carry(): pl.pallas_call(carry_kernel, out_shape=[jax.ShapeDtypeStruct(up.shape, BF...  4.23 us
    pallas_call x1, Pallas kernels, body(): pl.pallas_call(functools.partial(finish_kernel, spans), out_shape=jax.Sha...  3.6 us
  transfers between devices with their start and end apart: 38, of which 12 were waited for; matrix products, arithmetic and copies ran while one was open for 4% of the time, Pallas kernels for 21%

profile of v1, /device:TPU:64, one launch (start us, length us, event | category | flops | bytes accessed | tf_op | source)
XLA Modules:
  0.0 160.0 jit_solution(3996323953960183992)
XLA Ops:
  0.6 6.3 %prep.2 = bf16[6,512,512]{2,1,0:T(8,128)(2,1)} custom-call(s32[6]{0:T(128)} %stack.85.blocks_ref, bf16[512,8192]{1,0:T(8,128)(2,1)} %w_ref.7, f32[4,64]{1,0:T(4,128)} %scale_ref.7), custom_call_target="tpu_custom_call" | custom-call | bytes 6291456 | tf_op jit(solution)/shard_map/prep/pallas_call | solution.py:56
  6.9 1.5 collective-permute-start
  8.4 5.5 %collective-permute-start.1 = (bf16[2,64,512]{2,1,0:T(8,128)(2,1)S(1)}, bf16[2,64,512]{2,1,0:T(8,128)(2,1)S(1)}, u32[]{:S(2)}, u32[]{:S(2)}) collective-permute-start(bf16[2,64,512]{2,1,0:T(8,128)(2,1)S(1)} %bitcast.20), channel_id=1, source_target_pairs={{0,32},{16,48},{32,0},{48,16},{1,33},{17,49},{33,1},{49,17},{2,34}... | collective-permute-start | bytes 393224 | tf_op jit(solution)/shard_map/ppermute | solution.py:23
  13.8 2.7 %collective-permute-start.2 = (bf16[2,64,512]{2,1,0:T(8,128)(2,1)S(1)}, bf16[2,64,512]{2,1,0:T(8,128)(2,1)S(1)}, u32[]{:S(2)}, u32[]{:S(2)}) collective-permute-start(bf16[2,64,512]{2,1,0:T(8,128)(2,1)S(1)} %bitcast.21), channel_id=1, source_target_pairs={{0,16},{16,32},{32,48},{48,0},{1,17},{17,33},{33,49},{49,1},{2,18}... | collective-permute-start | bytes 393224 | tf_op jit(solution)/shard_map/ppermute | solution.py:23
  16.5 2.3 %collective-permute-done = bf16[2,64,512]{2,1,0:T(8,128)(2,1)S(1)} collective-permute-done((bf16[2,64,512]{2,1,0:T(8,128)(2,1)S(1)}, bf16[2,64,512]{2,1,0:T(8,128)(2,1)S(1)}, u32[]{:S(2)}, u32[]{:S(2)}) %collective-permute-start) | collective-permute-done | bytes 131104 | tf_op jit(solution)/shard_map/ppermute | solution.py:23
  18.8 1.4 collective-permute-done.1
  20.2 5.1 %collective-permute-done.2 = bf16[2,64,512]{2,1,0:T(8,128)(2,1)S(1)} collective-permute-done((bf16[2,64,512]{2,1,0:T(8,128)(2,1)S(1)}, bf16[2,64,512]{2,1,0:T(8,128)(2,1)S(1)}, u32[]{:S(2)}, u32[]{:S(2)}) %collective-permute-start.2) | collective-permute-done | bytes 131104 | tf_op jit(solution)/shard_map/ppermute | solution.py:23
  25.4 2.8 %collective-permute-start.3 = (bf16[8,64,512]{2,1,0:T(8,128)(2,1)S(1)}, bf16[8,64,512]{2,1,0:T(8,128)(2,1)S(1)}, u32[]{:S(2)}, u32[]{:S(2)}) collective-permute-start(bf16[8,64,512]{2,1,0:T(8,128)(2,1)S(1)} %pad_maximum_fusion.1.rest_0_), channel_id=1, source_target_pairs={{0,192},{64,0},{128,64},{192,128},{1,193},{65,1},{129,65},{193,129... | collective-permute-start | bytes 1572872 | tf_op jit(solution)/shard_map/ppermute | solution.py:23
  28.2 1.2 collective-permute-start.12
  29.3 5.8 %collective-permute-start.13 = (bf16[2,64,512]{2,1,0:T(8,128)(2,1)S(1)}, bf16[2,64,512]{2,1,0:T(8,128)(2,1)}, u32[]{:S(2)}, u32[]{:S(2)}) collective-permute-start(bf16[2,64,512]{2,1,0:T(8,128)(2,1)S(1)} %copy-done.31), channel_id=1, source_target_pairs={{0,32},{16,48},{32,0},{48,16},{1,33},{17,49},{33,1},{49,17},{2,34}... | collective-permute-start | bytes 393224 | tf_op jit(solution)/shard_map/ppermute | solution.py:23
  35.8 2.9 %prep.3 = bf16[2,512,512]{2,1,0:T(8,128)(2,1)} custom-call(s32[2]{0:T(128)} %pad_add_fusion.2.blocks_ref, bf16[512,8192]{1,0:T(8,128)(2,1)} %w_ref.7, f32[4,64]{1,0:T(4,128)} %scale_ref.7), custom_call_target="tpu_custom_call" | custom-call | bytes 2097152 | tf_op jit(solution)/shard_map/prep/pallas_call | solution.py:56
  38.7 1.1 collective-permute-start.14
  39.9 2.9 %collective-permute-done.5.rest_4_ = bf16[8,64,512]{2,1,0:T(8,128)(2,1)S(1)} collective-permute-done((bf16[8,64,512]{2,1,0:T(8,128)(2,1)S(1)}, bf16[8,64,512]{2,1,0:T(8,128)(2,1)S(1)}, u32[]{:S(2)}, u32[]{:S(2)}) %collective-permute-start.5) | collective-permute-done | bytes 524320 | tf_op jit(solution)/shard_map/ppermute | solution.py:23
  43.3 1.6 %collective-permute-start.6 = (bf16[4,64,512]{2,1,0:T(8,128)(2,1)S(1)}, bf16[4,64,512]{2,1,0:T(8,128)(2,1)}, u32[]{:S(2)}, u32[]{:S(2)}) collective-permute-start(bf16[4,64,512]{2,1,0:T(8,128)(2,1)S(1)} %slice.93), channel_id=1, source_target_pairs={{0,64},{64,128},{128,192},{192,0},{1,65},{65,129},{129,193},{193,1... | collective-permute-start | bytes 786440 | tf_op jit(solution)/shard_map/ppermute | solution.py:23
  44.9 0.9 constant_dynamic-update-slice_fusion.1
  45.9 2.8 %collective-permute-start.15 = (bf16[8,64,512]{2,1,0:T(8,128)(2,1)S(1)}, bf16[8,64,512]{2,1,0:T(8,128)(2,1)S(1)}, u32[]{:S(2)}, u32[]{:S(2)}) collective-permute-start(bf16[8,64,512]{2,1,0:T(8,128)(2,1)S(1)} %constant_dynamic-update-slice_fusion.rest_0_), channel_id=1, source_target_pairs={{0,192},{64,0},{128,64},{192,128},{1,193},{65,1},{129,65},{193,129... | collective-permute-start | bytes 1572872 | tf_op jit(solution)/shard_map/ppermute | solution.py:23
  48.7 3.4 %collective-permute-done.4.rest_2_ = bf16[4,64,512]{2,1,0:T(8,128)(2,1)S(1)} collective-permute-done((bf16[4,64,512]{2,1,0:T(8,128)(2,1)S(1)}, bf16[4,64,512]{2,1,0:T(8,128)(2,1)S(1)}, u32[]{:S(2)}, u32[]{:S(2)}) %collective-permute-start.4) | collective-permute-done | bytes 262176 | tf_op jit(solution)/shard_map/ppermute | solution.py:23
  54.4 4.1 %shrink.1 = bf16[384,128]{1,0:T(8,128)(2,1)} custom-call(s32[32]{0:T(128)} %slot_ref.3, s32[12]{0:T(128)} %adapter_ref.3, s32[2]{0:T(128)} %pad_add_fusion.place_ref, bf16[768,512]{1,0:T(8,128)(2,1)} %x_ref.5, bf16[8,64,512]{2,1,0:T(8,128)(2,1)} %copy-done.1, bf16[8,64,512]{2,1,0:T(8,128)(2,1)} %copy-done.10, bf16[4,64,512]{2,1,0:T(8,128)(2,1)} %copy-done.22, ...), custom_call_target="tpu_custom_call" | custom-call | flops 50331648 | bytes 2359296 | tf_op jit(solution)/shard_map/shrink/pallas_call | solution.py:252
  58.6 2.4 %collective-permute-done.15.rest_1_ = bf16[8,64,512]{2,1,0:T(8,128)(2,1)S(1)} collective-permute-done((bf16[8,64,512]{2,1,0:T(8,128)(2,1)S(1)}, bf16[8,64,512]{2,1,0:T(8,128)(2,1)S(1)}, u32[]{:S(2)}, u32[]{:S(2)}) %collective-permute-start.15) | collective-permute-done | bytes 524320 | tf_op jit(solution)/shard_map/ppermute | solution.py:23
  61.6 6.0 %collective-permute-done.17.rest_4_ = bf16[8,64,512]{2,1,0:T(8,128)(2,1)S(1)} collective-permute-done((bf16[8,64,512]{2,1,0:T(8,128)(2,1)S(1)}, bf16[8,64,512]{2,1,0:T(8,128)(2,1)S(1)}, u32[]{:S(2)}, u32[]{:S(2)}) %collective-permute-start.17) | collective-permute-done | bytes 524320 | tf_op jit(solution)/shard_map/ppermute | solution.py:23
  67.6 1.0 add_convert_fusion.9
  68.7 3.3 %collective-permute-start.8 = (bf16[384,128]{1,0:T(8,128)(2,1)S(1)}, bf16[384,128]{1,0:T(8,128)(2,1)S(1)}, u32[]{:S(2)}, u32[]{:S(2)}) collective-permute-start(bf16[384,128]{1,0:T(8,128)(2,1)S(1)} %add_convert_fusion.9), channel_id=1, source_target_pairs={{0,8},{8,0},{1,9},{9,1},{2,10},{10,2},{3,11},{11,3},{4,12},{12,4},... | collective-permute-start | bytes 294920 | tf_op jit(solution)/shard_map/ppermute | solution.py:23
  71.9 5.5 %partials.3 = (bf16[2,144,512]{2,1,0:T(8,128)(2,1)}, bf16[2,144,512]{2,1,0:T(8,128)(2,1)}, bf16[2,144,512]{2,1,0:T(8,128)(2,1)}, bf16[2,144,512]{2,1,0:T(8,128)(...) custom-call(s32[2]{0:T(128)} %pad_add_fusion.1.blocks_ref, bf16[768,512]{1,0:T(8,128)(2,1)} %x_ref.5, ...), custom_call_target="tpu_custom_call" | custom-call | flops 1610612736 | bytes 3670016 | tf_op jit(solution)/shard_map/partials/pallas_call | solution.py:108
  77.4 1.7 %collective-permute-start.27 = (bf16[2,144,512]{2,1,0:T(8,128)(2,1)}, bf16[2,144,512]{2,1,0:T(8,128)(2,1)S(1)}, u32[]{:S(2)}, u32[]{:S(2)}) collective-permute-start(bf16[2,144,512]{2,1,0:T(8,128)(2,1)} %get-tuple-element.37), channel_id=1, source_target_pairs={{0,2},{2,4},{4,6},{6,0},{1,3},{3,5},{5,7},{7,1},{8,10},{10,12},{12... | collective-permute-start | bytes 884744 | tf_op jit(solution)/shard_map/ppermute | solution.py:23
  79.1 1.7 %collective-permute-start.28 = (bf16[2,144,512]{2,1,0:T(8,128)(2,1)}, bf16[2,144,512]{2,1,0:T(8,128)(2,1)S(1)}, u32[]{:S(2)}, u32[]{:S(2)}) collective-permute-start(bf16[2,144,512]{2,1,0:T(8,128)(2,1)} %get-tuple-element.38), channel_id=1, source_target_pairs={{0,6},{2,0},{4,2},{6,4},{1,7},{3,1},{5,3},{7,5},{8,14},{10,8},{12,... | collective-permute-start | bytes 884744 | tf_op jit(solution)/shard_map/ppermute | solution.py:23
  81.1 2.9 %collective-permute-start.23 = (bf16[2,144,512]{2,1,0:T(8,128)(2,1)}, bf16[2,144,512]{2,1,0:T(8,128)(2,1)S(1)}, u32[]{:S(2)}, u32[]{:S(2)}) collective-permute-start(bf16[2,144,512]{2,1,0:T(8,128)(2,1)} %get-tuple-element.31), channel_id=1, source_target_pairs={{0,6},{2,0},{4,2},{6,4},{1,7},{3,1},{5,3},{7,5},{8,14},{10,8},{12,... | collective-permute-start | bytes 884744 | tf_op jit(solution)/shard_map/ppermute | solution.py:23
  84.0 13.1 %partials.2 = (bf16[2,288,512]{2,1,0:T(8,128)(2,1)}, bf16[2,288,512]{2,1,0:T(8,128)(2,1)}, bf16[2,288,512]{2,1,0:T(8,128)(2,1)}, bf16[2,288,512]{2,1,0:T(8,128)(...) custom-call(s32[6]{0:T(128)} %stack.78.blocks_ref, ...), custom_call_target="tpu_custom_call" | custom-call | flops 4831838208 | bytes 11010048 | tf_op jit(solution)/shard_map/partials/pallas_call | solution.py:108
  97.2 0.9 collective-permute-start.33
  98.1 0.7 copy-done.19
  98.8 2.2 %carry.3 = (bf16[2,288,512]{2,1,0:T(8,128)(2,1)}, bf16[2,288,512]{2,1,0:T(8,128)(2,1)}) custom-call(bf16[2,288,512]{2,1,0:T(8,128)(2,1)} %get-tuple-element.35.up_ref, bf16[2,288,512]{2,1,0:T(8,128)(2,1)} %get-tuple-element.36.down_ref, bf16[2,144,512]{2,1,0:T(8,128)(2,1)} %copy-done.18, ...), custom_call_target="tpu_custom_call", output_to_operand_aliasing={{0}: (0, {}), {1}: (1, {})} | custom-call | bytes 1769472 | tf_op jit(solution)/shard_map/carry/pallas_call | solution.py:165
  101.1 3.2 %collective-permute-start.30 = (bf16[2,288,512]{2,1,0:T(8,128)(2,1)}, bf16[2,288,512]{2,1,0:T(8,128)(2,1)S(1)}, u32[]{:S(2)}, u32[]{:S(2)}) collective-permute-start(bf16[2,288,512]{2,1,0:T(8,128)(2,1)} %get-tuple-element.40), channel_id=1, source_target_pairs={{0,6},{2,0},{4,2},{6,4},{1,7},{3,1},{5,3},{7,5},{8,14},{10,8},{12,... | collective-permute-start | bytes 1769480 | tf_op jit(solution)/shard_map/ppermute | solution.py:23
  104.4 0.7 copy-done.16
  105.2 2.1 %carry.2 = (bf16[2,288,512]{2,1,0:T(8,128)(2,1)}, bf16[2,288,512]{2,1,0:T(8,128)(2,1)}) custom-call(bf16[2,288,512]{2,1,0:T(8,128)(2,1)} %get-tuple-element.28.up_ref, bf16[2,288,512]{2,1,0:T(8,128)(2,1)} %get-tuple-element.29.down_ref, bf16[2,144,512]{2,1,0:T(8,128)(2,1)} %copy-done.16, ...), custom_call_target="tpu_custom_call", output_to_operand_aliasing={{0}: (0, {}), {1}: (1, {})} | custom-call | bytes 1769472 | tf_op jit(solution)/shard_map/carry/pallas_call | solution.py:165
  107.3 3.2 %collective-permute-start.25 = (bf16[2,288,512]{2,1,0:T(8,128)(2,1)}, bf16[2,288,512]{2,1,0:T(8,128)(2,1)S(1)}, u32[]{:S(2)}, u32[]{:S(2)}) collective-permute-start(bf16[2,288,512]{2,1,0:T(8,128)(2,1)} %get-tuple-element.33), channel_id=1, source_target_pairs={{0,6},{2,0},{4,2},{6,4},{1,7},{3,1},{5,3},{7,5},{8,14},{10,8},{12,... | collective-permute-start | bytes 1769480 | tf_op jit(solution)/shard_map/ppermute | solution.py:23
  110.6 1.3 collective-permute-start.32
  111.9 6.8 %collective-permute-done.29.rest_5_ = bf16[2,288,512]{2,1,0:T(8,128)(2,1)S(1)} collective-permute-done((bf16[2,288,512]{2,1,0:T(8,128)(2,1)}, bf16[2,288,512]{2,1,0:T(8,128)(2,1)S(1)}, u32[]{:S(2)}, u32[]{:S(2)}) %collective-permute-start.29) | collective-permute-done | bytes 589856 | tf_op jit(solution)/shard_map/ppermute | solution.py:23
  118.8 2.0 %collective-permute-start.18 = (bf16[4,64,512]{2,1,0:T(8,128)(2,1)S(1)}, bf16[4,64,512]{2,1,0:T(8,128)(2,1)S(1)}, u32[]{:S(2)}, u32[]{:S(2)}) collective-permute-start(bf16[4,64,512]{2,1,0:T(8,128)(2,1)S(1)} %slice.95), channel_id=1, source_target_pairs={{0,64},{64,128},{128,192},{192,0},{1,65},{65,129},{129,193},{193,1... | collective-permute-start | bytes 786440 | tf_op jit(solution)/shard_map/ppermute | solution.py:23
  120.9 6.9 %collective-permute-done.24.rest_1_ = bf16[2,288,512]{2,1,0:T(8,128)(2,1)S(1)} collective-permute-done((bf16[2,288,512]{2,1,0:T(8,128)(2,1)}, bf16[2,288,512]{2,1,0:T(8,128)(2,1)S(1)}, u32[]{:S(2)}, u32[]{:S(2)}) %collective-permute-start.24) | collective-permute-done | bytes 589856 | tf_op jit(solution)/shard_map/ppermute | solution.py:23
  127.8 3.2 %collective-permute-start.36 = (bf16[1,96,512]{2,1,0:T(8,128)(2,1)S(1)}, bf16[1,96,512]{2,1,0:T(8,128)(2,1)S(1)}, u32[]{:S(2)}, u32[]{:S(2)}) collective-permute-start(bf16[1,96,512]{2,1,0:T(8,128)(2,1)S(1)} %get-tuple-element.55), channel_id=1, source_target_pairs={{0,6},{2,0},{4,2},{6,4},{1,7},{3,1},{5,3},{7,5},{8,14},{10,8},{12,... | collective-permute-start | bytes 294920 | tf_op jit(solution)/shard_map/ppermute | solution.py:23
  131.1 3.5 %collective-permute-done.34 = bf16[1,96,512]{2,1,0:T(8,128)(2,1)S(1)} collective-permute-done((bf16[1,96,512]{2,1,0:T(8,128)(2,1)S(1)}, bf16[1,96,512]{2,1,0:T(8,128)(2,1)S(1)}, u32[]{:S(2)}, u32[]{:S(2)}) %collective-permute-start.34) | collective-permute-done | bytes 98336 | tf_op jit(solution)/shard_map/ppermute | solution.py:23
  135.1 1.0 collective-permute-start.31
  136.3 1.1 collective-permute-start.26
  137.4 4.4 %collective-permute-start.37 = (bf16[1,192,512]{2,1,0:T(8,128)(2,1)S(1)}, bf16[1,192,512]{2,1,0:T(8,128)(2,1)S(1)}, u32[]{:S(2)}, u32[]{:S(2)}) collective-permute-start(bf16[1,192,512]{2,1,0:T(8,128)(2,1)S(1)} %pad_maximum_fusion.3), channel_id=1, source_target_pairs={{0,6},{2,0},{4,2},{6,4},{1,7},{3,1},{5,3},{7,5},{8,14},{10,8},{12,... | collective-permute-start | bytes 589832 | tf_op jit(solution)/shard_map/ppermute | solution.py:23
  141.8 1.4 collective-permute-start.9
  143.3 6.4 %collective-permute-done.9.s1 = bf16[384,128]{1,0:T(8,128)(2,1)S(1)} collective-permute-done((bf16[384,128]{1,0:T(8,128)(2,1)S(1)}, bf16[384,128]{1,0:T(8,128)(2,1)S(1)}, u32[]{:S(2)}, u32[]{:S(2)}) %collective-permute-start.9) | collective-permute-done | bytes 98336 | tf_op jit(solution)/shard_map/ppermute | solution.py:23
  150.4 4.3 %expand.1.delta_ref = f32[768,512]{1,0:T(8,128)} custom-call(s32[32]{0:T(128)} %slot_ref.3, s32[12]{0:T(128)} %adapter_ref.3, s32[2]{0:T(128)} %pad_add_fusion.place_ref, s32[12]{0:T(128)} %count_ref.1, bf16[384,128]{1,0:T(8,128)(2,1)} %copy-done.13, bf16[384,128]{1,0:T(8,128)(2,1)} %copy-done.35, bf16[384,128]{1,0:T(8,128)(2,1)} %copy-done.33, ...), custom_call_target="tpu_custom_call" | custom-call | flops 50331648 | bytes 2359296 | tf_op jit(solution)/shard_map/expand/pallas_call | solution.py:252
  154.7 0.7 slice.100.rest_9_
  156.4 3.6 %finish.1 = bf16[768,512]{1,0:T(8,128)(2,1)} custom-call(f32[768,512]{1,0:T(8,128)} %expand.1.delta_ref, bf16[2,288,512]{2,1,0:T(8,128)(2,1)} %get-tuple-element.27.rest_0_, bf16[2,288,512]{2,1,0:T(8,128)(2,1)} %copy-done.6, bf16[2,288,512]{2,1,0:T(8,128)(2,1)} %copy-done.7, bf16[1,288,512]{2,1,0:T(8,128)(2,1)} %copy-done.15, ...), custom_call_target="tpu_custom_call" | custom-call | bytes 5505024 | tf_op jit(solution)/shard_map/finish/pallas_call | solution.py:418
  (135 shorter events, 8.3 us)
Async XLA Ops:
  0.6 27.5 %copy-start.31 = (bf16[2,64,512]{2,1,0:T(8,128)(2,1)S(1)}, bf16[2,64,512]{2,1,0:T(8,128)(2,1)}, u32[]{:S(2)}) copy-start(bf16[2,64,512]{2,1,0:T(8,128)(2,1)} %param.12) | copy-start | bytes 393220
  6.9 74.2 %collective-permute-start.20 = (bf16[6,512,512]{2,1,0:T(8,128)(2,1)}, bf16[6,512,512]{2,1,0:T(8,128)(2,1)}, u32[]{:S(2)}, u32[]{:S(2)}) collective-permute-start(bf16[6,512,512]{2,1,0:T(8,128)(2,1)} %prep.2), channel_id=1, source_target_pairs={{0,1},{1,0},{2,3},{3,2},{4,5},{5,4},{6,7},{7,6},{8,9},{9,8},{10,11... | collective-permute-start | bytes 9437192 | tf_op jit(solution)/shard_map/ppermute | solution.py:23
  6.9 11.9 %collective-permute-start = (bf16[2,64,512]{2,1,0:T(8,128)(2,1)S(1)}, bf16[2,64,512]{2,1,0:T(8,128)(2,1)S(1)}, u32[]{:S(2)}, u32[]{:S(2)}) collective-permute-start(bf16[2,64,512]{2,1,0:T(8,128)(2,1)S(1)} %bitcast.19), channel_id=1, source_target_pairs={{0,48},{16,0},{32,16},{48,32},{1,49},{17,1},{33,17},{49,33},{2,50}... | collective-permute-start | bytes 393224 | tf_op jit(solution)/shard_map/ppermute | solution.py:23
  8.4 11.8 %collective-permute-start.1 = (bf16[2,64,512]{2,1,0:T(8,128)(2,1)S(1)}, bf16[2,64,512]{2,1,0:T(8,128)(2,1)S(1)}, u32[]{:S(2)}, u32[]{:S(2)}) collective-permute-start(bf16[2,64,512]{2,1,0:T(8,128)(2,1)S(1)} %bitcast.20), channel_id=1, source_target_pairs={{0,32},{16,48},{32,0},{48,16},{1,33},{17,49},{33,1},{49,17},{2,34}... | collective-permute-start | bytes 393224 | tf_op jit(solution)/shard_map/ppermute | solution.py:23
  13.8 11.5 %collective-permute-start.2 = (bf16[2,64,512]{2,1,0:T(8,128)(2,1)S(1)}, bf16[2,64,512]{2,1,0:T(8,128)(2,1)S(1)}, u32[]{:S(2)}, u32[]{:S(2)}) collective-permute-start(bf16[2,64,512]{2,1,0:T(8,128)(2,1)S(1)} %bitcast.21), channel_id=1, source_target_pairs={{0,16},{16,32},{32,48},{48,0},{1,17},{17,33},{33,49},{49,1},{2,18}... | collective-permute-start | bytes 393224 | tf_op jit(solution)/shard_map/ppermute | solution.py:23
  25.4 14.4 %collective-permute-start.3 = (bf16[8,64,512]{2,1,0:T(8,128)(2,1)S(1)}, bf16[8,64,512]{2,1,0:T(8,128)(2,1)S(1)}, u32[]{:S(2)}, u32[]{:S(2)}) collective-permute-start(bf16[8,64,512]{2,1,0:T(8,128)(2,1)S(1)} %pad_maximum_fusion.1.rest_0_), channel_id=1, source_target_pairs={{0,192},{64,0},{128,64},{192,128},{1,193},{65,1},{129,65},{193,129... | collective-permute-start | bytes 1572872 | tf_op jit(solution)/shard_map/ppermute | solution.py:23
  28.2 14.6 %collective-permute-start.5 = (bf16[8,64,512]{2,1,0:T(8,128)(2,1)S(1)}, bf16[8,64,512]{2,1,0:T(8,128)(2,1)S(1)}, u32[]{:S(2)}, u32[]{:S(2)}) collective-permute-start(bf16[8,64,512]{2,1,0:T(8,128)(2,1)S(1)} %pad_maximum_fusion.1.rest_0_), channel_id=1, source_target_pairs={{0,64},{64,128},{128,192},{192,0},{1,65},{65,129},{129,193},{193,1... | collective-permute-start | bytes 1572872 | tf_op jit(solution)/shard_map/ppermute | solution.py:23
  28.2 10.5 %collective-permute-start.12 = (bf16[2,64,512]{2,1,0:T(8,128)(2,1)S(1)}, bf16[2,64,512]{2,1,0:T(8,128)(2,1)S(1)}, u32[]{:S(2)}, u32[]{:S(2)}) collective-permute-start(bf16[2,64,512]{2,1,0:T(8,128)(2,1)S(1)} %copy-done.31), channel_id=1, source_target_pairs={{0,48},{16,0},{32,16},{48,32},{1,49},{17,1},{33,17},{49,33},{2,50}... | collective-permute-start | bytes 393224 | tf_op jit(solution)/shard_map/ppermute | solution.py:23
  29.3 13.9 %collective-permute-start.13 = (bf16[2,64,512]{2,1,0:T(8,128)(2,1)S(1)}, bf16[2,64,512]{2,1,0:T(8,128)(2,1)}, u32[]{:S(2)}, u32[]{:S(2)}) collective-permute-start(bf16[2,64,512]{2,1,0:T(8,128)(2,1)S(1)} %copy-done.31), channel_id=1, source_target_pairs={{0,32},{16,48},{32,0},{48,16},{1,33},{17,49},{33,1},{49,17},{2,34}... | collective-permute-start | bytes 393224 | tf_op jit(solution)/shard_map/ppermute | solution.py:23
  38.7 7.2 %collective-permute-start.14 = (bf16[2,64,512]{2,1,0:T(8,128)(2,1)S(1)}, bf16[2,64,512]{2,1,0:T(8,128)(2,1)S(1)}, u32[]{:S(2)}, u32[]{:S(2)}) collective-permute-start(bf16[2,64,512]{2,1,0:T(8,128)(2,1)S(1)} %copy-done.31), channel_id=1, source_target_pairs={{0,16},{16,32},{32,48},{48,0},{1,17},{17,33},{33,49},{49,1},{2,18}... | collective-permute-start | bytes 393224 | tf_op jit(solution)/shard_map/ppermute | solution.py:23
  39.8 32.2 %collective-permute-start.21 = (bf16[2,512,512]{2,1,0:T(8,128)(2,1)}, bf16[2,512,512]{2,1,0:T(8,128)(2,1)}, u32[]{:S(2)}, u32[]{:S(2)}) collective-permute-start(bf16[2,512,512]{2,1,0:T(8,128)(2,1)} %prep.3), channel_id=1, source_target_pairs={{0,1},{1,0},{2,3},{3,2},{4,5},{5,4},{6,7},{7,6},{8,9},{9,8},{10,11... | collective-permute-start | bytes 3145736 | tf_op jit(solution)/shard_map/ppermute | solution.py:23
  42.8 9.2 %collective-permute-start.4 = (bf16[4,64,512]{2,1,0:T(8,128)(2,1)S(1)}, bf16[4,64,512]{2,1,0:T(8,128)(2,1)S(1)}, u32[]{:S(2)}, u32[]{:S(2)}) collective-permute-start(bf16[4,64,512]{2,1,0:T(8,128)(2,1)S(1)} %slice.92), channel_id=1, source_target_pairs={{0,192},{64,0},{128,64},{192,128},{1,193},{65,1},{129,65},{193,129... | collective-permute-start | bytes 786440 | tf_op jit(solution)/shard_map/ppermute | solution.py:23
  43.3 9.8 %collective-permute-start.6 = (bf16[4,64,512]{2,1,0:T(8,128)(2,1)S(1)}, bf16[4,64,512]{2,1,0:T(8,128)(2,1)}, u32[]{:S(2)}, u32[]{:S(2)}) collective-permute-start(bf16[4,64,512]{2,1,0:T(8,128)(2,1)S(1)} %slice.93), channel_id=1, source_target_pairs={{0,64},{64,128},{128,192},{192,0},{1,65},{65,129},{129,193},{193,1... | collective-permute-start | bytes 786440 | tf_op jit(solution)/shard_map/ppermute | solution.py:23
  45.9 31.5 %copy-start.12 = (bf16[8,64,512]{2,1,0:T(8,128)(2,1)}, bf16[8,64,512]{2,1,0:T(8,128)(2,1)S(1)}, u32[]{:S(2)}) copy-start(bf16[8,64,512]{2,1,0:T(8,128)(2,1)S(1)} %constant_dynamic-update-slice_fusion.rest_0_) | copy-start | bytes 1572868
  45.9 15.0 %collective-permute-start.15 = (bf16[8,64,512]{2,1,0:T(8,128)(2,1)S(1)}, bf16[8,64,512]{2,1,0:T(8,128)(2,1)S(1)}, u32[]{:S(2)}, u32[]{:S(2)}) collective-permute-start(bf16[8,64,512]{2,1,0:T(8,128)(2,1)S(1)} %constant_dynamic-update-slice_fusion.rest_0_), channel_id=1, source_target_pairs={{0,192},{64,0},{128,64},{192,128},{1,193},{65,1},{129,65},{193,129... | collective-permute-start | bytes 1572872 | tf_op jit(solution)/shard_map/ppermute | solution.py:23
  52.0 19.9 %collective-permute-start.19 = (bf16[768,512]{1,0:T(8,128)(2,1)S(1)}, bf16[768,512]{1,0:T(8,128)(2,1)}, u32[]{:S(2)}, u32[]{:S(2)}) collective-permute-start(bf16[768,512]{1,0:T(8,128)(2,1)S(1)} %copy-done), channel_id=1, source_target_pairs={{0,1},{1,0},{2,3},{3,2},{4,5},{5,4},{6,7},{7,6},{8,9},{9,8},{10,11... | collective-permute-start | bytes 2359304 | tf_op jit(solution)/shard_map/ppermute | solution.py:23
  53.1 14.5 %collective-permute-start.17 = (bf16[8,64,512]{2,1,0:T(8,128)(2,1)S(1)}, bf16[8,64,512]{2,1,0:T(8,128)(2,1)S(1)}, u32[]{:S(2)}, u32[]{:S(2)}) collective-permute-start(bf16[8,64,512]{2,1,0:T(8,128)(2,1)S(1)} %constant_dynamic-update-slice_fusion.rest_0_), channel_id=1, source_target_pairs={{0,64},{64,128},{128,192},{192,0},{1,65},{65,129},{129,193},{193,1... | collective-permute-start | bytes 1572872 | tf_op jit(solution)/shard_map/ppermute | solution.py:23
  60.9 6.7 %collective-permute-start.7 = (bf16[384,128]{1,0:T(8,128)(2,1)}, bf16[384,128]{1,0:T(8,128)(2,1)S(1)}, u32[]{:S(2)}, u32[]{:S(2)}) collective-permute-start(bf16[384,128]{1,0:T(8,128)(2,1)} %shrink.1), channel_id=1, source_target_pairs={{0,1},{1,0},{2,3},{3,2},{4,5},{5,4},{6,7},{7,6},{8,9},{9,8},{10,11... | collective-permute-start | bytes 294920 | tf_op jit(solution)/shard_map/ppermute | solution.py:23
  68.7 32.4 %collective-permute-start.8 = (bf16[384,128]{1,0:T(8,128)(2,1)S(1)}, bf16[384,128]{1,0:T(8,128)(2,1)S(1)}, u32[]{:S(2)}, u32[]{:S(2)}) collective-permute-start(bf16[384,128]{1,0:T(8,128)(2,1)S(1)} %add_convert_fusion.9), channel_id=1, source_target_pairs={{0,8},{8,0},{1,9},{9,1},{2,10},{10,2},{3,11},{11,3},{4,12},{12,4},... | collective-permute-start | bytes 294920 | tf_op jit(solution)/shard_map/ppermute | solution.py:23
  77.4 19.7 %collective-permute-start.27 = (bf16[2,144,512]{2,1,0:T(8,128)(2,1)}, bf16[2,144,512]{2,1,0:T(8,128)(2,1)S(1)}, u32[]{:S(2)}, u32[]{:S(2)}) collective-permute-start(bf16[2,144,512]{2,1,0:T(8,128)(2,1)} %get-tuple-element.37), channel_id=1, source_target_pairs={{0,2},{2,4},{4,6},{6,0},{1,3},{3,5},{5,7},{7,1},{8,10},{10,12},{12... | collective-permute-start | bytes 884744 | tf_op jit(solution)/shard_map/ppermute | solution.py:23
  79.1 19.0 %collective-permute-start.28 = (bf16[2,144,512]{2,1,0:T(8,128)(2,1)}, bf16[2,144,512]{2,1,0:T(8,128)(2,1)S(1)}, u32[]{:S(2)}, u32[]{:S(2)}) collective-permute-start(bf16[2,144,512]{2,1,0:T(8,128)(2,1)} %get-tuple-element.38), channel_id=1, source_target_pairs={{0,6},{2,0},{4,2},{6,4},{1,7},{3,1},{5,3},{7,5},{8,14},{10,8},{12,... | collective-permute-start | bytes 884744 | tf_op jit(solution)/shard_map/ppermute | solution.py:23
  80.8 23.6 %collective-permute-start.22 = (bf16[2,144,512]{2,1,0:T(8,128)(2,1)}, bf16[2,144,512]{2,1,0:T(8,128)(2,1)S(1)}, u32[]{:S(2)}, u32[]{:S(2)}) collective-permute-start(bf16[2,144,512]{2,1,0:T(8,128)(2,1)} %get-tuple-element.30), channel_id=1, source_target_pairs={{0,2},{2,4},{4,6},{6,0},{1,3},{3,5},{5,7},{7,1},{8,10},{10,12},{12... | collective-permute-start | bytes 884744 | tf_op jit(solution)/shard_map/ppermute | solution.py:23
  81.1 23.2 %collective-permute-start.23 = (bf16[2,144,512]{2,1,0:T(8,128)(2,1)}, bf16[2,144,512]{2,1,0:T(8,128)(2,1)S(1)}, u32[]{:S(2)}, u32[]{:S(2)}) collective-permute-start(bf16[2,144,512]{2,1,0:T(8,128)(2,1)} %get-tuple-element.31), channel_id=1, source_target_pairs={{0,6},{2,0},{4,2},{6,4},{1,7},{3,1},{5,3},{7,5},{8,14},{10,8},{12,... | collective-permute-start | bytes 884744 | tf_op jit(solution)/shard_map/ppermute | solution.py:23
  97.2 13.4 %collective-permute-start.33 = (bf16[1,192,512]{2,1,0:T(8,128)(2,1)S(1)}, bf16[1,192,512]{2,1,0:T(8,128)(2,1)S(1)}, u32[]{:S(2)}, u32[]{:S(2)}) collective-permute-start(bf16[1,192,512]{2,1,0:T(8,128)(2,1)S(1)} %copy-done.36), channel_id=1, source_target_pairs={{0,8},{8,0},{1,9},{9,1},{2,10},{10,2},{3,11},{11,3},{4,12},{12,4},... | collective-permute-start | bytes 589832 | tf_op jit(solution)/shard_map/ppermute | solution.py:23
  98.8 32.2 %copy-start.2 = (bf16[2,288,512]{2,1,0:T(8,128)(2,1)S(1)}, bf16[2,288,512]{2,1,0:T(8,128)(2,1)}, u32[]{:S(2)}) copy-start(bf16[2,288,512]{2,1,0:T(8,128)(2,1)} %get-tuple-element.27.rest_0_) | copy-start | bytes 1769476
  101.0 35.1 %copy-start.27 = (bf16[1,192,512]{2,1,0:T(8,128)(2,1)S(1)}, bf16[1,192,512]{2,1,0:T(8,128)(2,1)}, u32[]{:S(2)}) copy-start(bf16[1,192,512]{2,1,0:T(8,128)(2,1)} %get-tuple-element.45) | copy-start | bytes 589828
  101.0 35.1 %copy-start.28 = (bf16[1,192,512]{2,1,0:T(8,128)(2,1)S(1)}, bf16[1,192,512]{2,1,0:T(8,128)(2,1)}, u32[]{:S(2)}) copy-start(bf16[1,192,512]{2,1,0:T(8,128)(2,1)} %get-tuple-element.48) | copy-start | bytes 589828
  101.0 17.8 %collective-permute-start.29 = (bf16[2,288,512]{2,1,0:T(8,128)(2,1)}, bf16[2,288,512]{2,1,0:T(8,128)(2,1)S(1)}, u32[]{:S(2)}, u32[]{:S(2)}) collective-permute-start(bf16[2,288,512]{2,1,0:T(8,128)(2,1)} %get-tuple-element.39), channel_id=1, source_target_pairs={{0,2},{2,4},{4,6},{6,0},{1,3},{3,5},{5,7},{7,1},{8,10},{10,12},{12... | collective-permute-start | bytes 1769480 | tf_op jit(solution)/shard_map/ppermute | solution.py:23
  101.1 17.7 %collective-permute-start.30 = (bf16[2,288,512]{2,1,0:T(8,128)(2,1)}, bf16[2,288,512]{2,1,0:T(8,128)(2,1)S(1)}, u32[]{:S(2)}, u32[]{:S(2)}) collective-permute-start(bf16[2,288,512]{2,1,0:T(8,128)(2,1)} %get-tuple-element.40), channel_id=1, source_target_pairs={{0,6},{2,0},{4,2},{6,4},{1,7},{3,1},{5,3},{7,5},{8,14},{10,8},{12,... | collective-permute-start | bytes 1769480 | tf_op jit(solution)/shard_map/ppermute | solution.py:23
  104.3 37.5 %copy-start.13 = (bf16[384,128]{1,0:T(8,128)(2,1)}, bf16[384,128]{1,0:T(8,128)(2,1)S(1)}, u32[]{:S(2)}) copy-start(bf16[384,128]{1,0:T(8,128)(2,1)S(1)} %add_convert_fusion.8.s0) | copy-start | bytes 294916
  107.3 20.5 %collective-permute-start.24 = (bf16[2,288,512]{2,1,0:T(8,128)(2,1)}, bf16[2,288,512]{2,1,0:T(8,128)(2,1)S(1)}, u32[]{:S(2)}, u32[]{:S(2)}) collective-permute-start(bf16[2,288,512]{2,1,0:T(8,128)(2,1)} %get-tuple-element.32), channel_id=1, source_target_pairs={{0,2},{2,4},{4,6},{6,0},{1,3},{3,5},{5,7},{7,1},{8,10},{10,12},{12... | collective-permute-start | bytes 1769480 | tf_op jit(solution)/shard_map/ppermute | solution.py:23
  107.3 20.5 %collective-permute-start.25 = (bf16[2,288,512]{2,1,0:T(8,128)(2,1)}, bf16[2,288,512]{2,1,0:T(8,128)(2,1)S(1)}, u32[]{:S(2)}, u32[]{:S(2)}) collective-permute-start(bf16[2,288,512]{2,1,0:T(8,128)(2,1)} %get-tuple-element.33), channel_id=1, source_target_pairs={{0,6},{2,0},{4,2},{6,4},{1,7},{3,1},{5,3},{7,5},{8,14},{10,8},{12,... | collective-permute-start | bytes 1769480 | tf_op jit(solution)/shard_map/ppermute | solution.py:23
  110.6 24.5 %collective-permute-start.32 = (bf16[3,192,512]{2,1,0:T(8,128)(2,1)S(1)}, bf16[3,192,512]{2,1,0:T(8,128)(2,1)S(1)}, u32[]{:S(2)}, u32[]{:S(2)}) collective-permute-start(bf16[3,192,512]{2,1,0:T(8,128)(2,1)S(1)} %pad_maximum_fusion), channel_id=1, source_target_pairs={{0,8},{8,0},{1,9},{9,1},{2,10},{10,2},{3,11},{11,3},{4,12},{12,4},... | collective-permute-start | bytes 1769480 | tf_op jit(solution)/shard_map/ppermute | solution.py:23
  118.7 35.9 %copy-start.4 = (bf16[2,288,512]{2,1,0:T(8,128)(2,1)}, bf16[2,288,512]{2,1,0:T(8,128)(2,1)S(1)}, u32[]{:S(2)}) copy-start(bf16[2,288,512]{2,1,0:T(8,128)(2,1)S(1)} %collective-permute-done.29.rest_5_) | copy-start | bytes 1769476
  118.8 17.5 %collective-permute-start.16 = (bf16[4,64,512]{2,1,0:T(8,128)(2,1)S(1)}, bf16[4,64,512]{2,1,0:T(8,128)(2,1)S(1)}, u32[]{:S(2)}, u32[]{:S(2)}) collective-permute-start(bf16[4,64,512]{2,1,0:T(8,128)(2,1)S(1)} %slice.94), channel_id=1, source_target_pairs={{0,192},{64,0},{128,64},{192,128},{1,193},{65,1},{129,65},{193,129... | collective-permute-start | bytes 786440 | tf_op jit(solution)/shard_map/ppermute | solution.py:23
  118.8 35.9 %copy-start.5 = (bf16[2,288,512]{2,1,0:T(8,128)(2,1)}, bf16[2,288,512]{2,1,0:T(8,128)(2,1)S(1)}, u32[]{:S(2)}) copy-start(bf16[2,288,512]{2,1,0:T(8,128)(2,1)S(1)} %collective-permute-done.30.rest_6_) | copy-start | bytes 1769476
  118.8 18.6 %collective-permute-start.18 = (bf16[4,64,512]{2,1,0:T(8,128)(2,1)S(1)}, bf16[4,64,512]{2,1,0:T(8,128)(2,1)S(1)}, u32[]{:S(2)}, u32[]{:S(2)}) collective-permute-start(bf16[4,64,512]{2,1,0:T(8,128)(2,1)S(1)} %slice.95), channel_id=1, source_target_pairs={{0,64},{64,128},{128,192},{192,0},{1,65},{65,129},{129,193},{193,1... | collective-permute-start | bytes 786440 | tf_op jit(solution)/shard_map/ppermute | solution.py:23
  127.8 26.9 %copy-start.6 = (bf16[2,288,512]{2,1,0:T(8,128)(2,1)}, bf16[2,288,512]{2,1,0:T(8,128)(2,1)S(1)}, u32[]{:S(2)}) copy-start(bf16[2,288,512]{2,1,0:T(8,128)(2,1)S(1)} %collective-permute-done.24.rest_1_) | copy-start | bytes 1769476
  127.8 6.9 %collective-permute-start.34 = (bf16[1,96,512]{2,1,0:T(8,128)(2,1)S(1)}, bf16[1,96,512]{2,1,0:T(8,128)(2,1)S(1)}, u32[]{:S(2)}, u32[]{:S(2)}) collective-permute-start(bf16[1,96,512]{2,1,0:T(8,128)(2,1)S(1)} %get-tuple-element.56), channel_id=1, source_target_pairs={{0,2},{2,4},{4,6},{6,0},{1,3},{3,5},{5,7},{7,1},{8,10},{10,12},{12... | collective-permute-start | bytes 294920 | tf_op jit(solution)/shard_map/ppermute | solution.py:23
  127.8 26.9 %copy-start.7 = (bf16[2,288,512]{2,1,0:T(8,128)(2,1)}, bf16[2,288,512]{2,1,0:T(8,128)(2,1)S(1)}, u32[]{:S(2)}) copy-start(bf16[2,288,512]{2,1,0:T(8,128)(2,1)S(1)} %collective-permute-done.25.rest_2_) | copy-start | bytes 1769476
  127.8 6.9 %collective-permute-start.36 = (bf16[1,96,512]{2,1,0:T(8,128)(2,1)S(1)}, bf16[1,96,512]{2,1,0:T(8,128)(2,1)S(1)}, u32[]{:S(2)}, u32[]{:S(2)}) collective-permute-start(bf16[1,96,512]{2,1,0:T(8,128)(2,1)S(1)} %get-tuple-element.55), channel_id=1, source_target_pairs={{0,6},{2,0},{4,2},{6,4},{1,7},{3,1},{5,3},{7,5},{8,14},{10,8},{12,... | collective-permute-start | bytes 294920 | tf_op jit(solution)/shard_map/ppermute | solution.py:23
  134.7 7.1 %collective-permute-start.10 = (bf16[384,128]{1,0:T(8,128)(2,1)S(1)}, bf16[384,128]{1,0:T(8,128)(2,1)S(1)}, u32[]{:S(2)}, u32[]{:S(2)}) collective-permute-start(bf16[384,128]{1,0:T(8,128)(2,1)S(1)} %add_convert_fusion.8.s0), channel_id=1, source_target_pairs={{0,6},{2,0},{4,2},{6,4},{1,7},{3,1},{5,3},{7,5},{8,14},{10,8},{12,... | collective-permute-start | bytes 294920 | tf_op jit(solution)/shard_map/ppermute | solution.py:23
  134.7 7.2 %collective-permute-start.11 = (bf16[384,128]{1,0:T(8,128)(2,1)S(1)}, bf16[384,128]{1,0:T(8,128)(2,1)S(1)}, u32[]{:S(2)}, u32[]{:S(2)}) collective-permute-start(bf16[384,128]{1,0:T(8,128)(2,1)S(1)} %add_convert_fusion.8.s0), channel_id=1, source_target_pairs={{0,4},{2,6},{4,0},{6,2},{1,5},{3,7},{5,1},{7,3},{8,12},{10,14},{12... | collective-permute-start | bytes 294920 | tf_op jit(solution)/shard_map/ppermute | solution.py:23
  135.1 20.3 %collective-permute-start.31 = (bf16[1,288,512]{2,1,0:T(8,128)(2,1)S(1)}, bf16[1,288,512]{2,1,0:T(8,128)(2,1)S(1)}, u32[]{:S(2)}, u32[]{:S(2)}) collective-permute-start(bf16[1,288,512]{2,1,0:T(8,128)(2,1)S(1)} %add_convert_fusion), channel_id=1, source_target_pairs={{0,8},{8,0},{1,9},{9,1},{2,10},{10,2},{3,11},{11,3},{4,12},{12,4},... | collective-permute-start | bytes 884744 | tf_op jit(solution)/shard_map/ppermute | solution.py:23
  136.3 19.1 %collective-permute-start.26 = (bf16[1,288,512]{2,1,0:T(8,128)(2,1)S(1)}, bf16[1,288,512]{2,1,0:T(8,128)(2,1)S(1)}, u32[]{:S(2)}, u32[]{:S(2)}) collective-permute-start(bf16[1,288,512]{2,1,0:T(8,128)(2,1)S(1)} %add_convert_fusion.1), channel_id=1, source_target_pairs={{0,8},{8,0},{1,9},{9,1},{2,10},{10,2},{3,11},{11,3},{4,12},{12,4},... | collective-permute-start | bytes 884744 | tf_op jit(solution)/shard_map/ppermute | solution.py:23
  137.4 18.0 %collective-permute-start.37 = (bf16[1,192,512]{2,1,0:T(8,128)(2,1)S(1)}, bf16[1,192,512]{2,1,0:T(8,128)(2,1)S(1)}, u32[]{:S(2)}, u32[]{:S(2)}) collective-permute-start(bf16[1,192,512]{2,1,0:T(8,128)(2,1)S(1)} %pad_maximum_fusion.3), channel_id=1, source_target_pairs={{0,6},{2,0},{4,2},{6,4},{1,7},{3,1},{5,3},{7,5},{8,14},{10,8},{12,... | collective-permute-start | bytes 589832 | tf_op jit(solution)/shard_map/ppermute | solution.py:23
  141.8 13.6 %collective-permute-start.35 = (bf16[1,192,512]{2,1,0:T(8,128)(2,1)S(1)}, bf16[1,192,512]{2,1,0:T(8,128)(2,1)S(1)}, u32[]{:S(2)}, u32[]{:S(2)}) collective-permute-start(bf16[1,192,512]{2,1,0:T(8,128)(2,1)S(1)} %pad_maximum_fusion.2), channel_id=1, source_target_pairs={{0,2},{2,4},{4,6},{6,0},{1,3},{3,5},{5,7},{7,1},{8,10},{10,12},{12... | collective-permute-start | bytes 589832 | tf_op jit(solution)/shard_map/ppermute | solution.py:23
  141.8 7.9 %collective-permute-start.9 = (bf16[384,128]{1,0:T(8,128)(2,1)S(1)}, bf16[384,128]{1,0:T(8,128)(2,1)S(1)}, u32[]{:S(2)}, u32[]{:S(2)}) collective-permute-start(bf16[384,128]{1,0:T(8,128)(2,1)S(1)} %add_convert_fusion.8.s0), channel_id=1, source_target_pairs={{0,2},{2,4},{4,6},{6,0},{1,3},{3,5},{5,7},{7,1},{8,10},{10,12},{12... | collective-permute-start | bytes 294920 | tf_op jit(solution)/shard_map/ppermute | solution.py:23
  (27 other events, 232.5 us)

commit v2 on v0

v2 whole, which is shorter than its diff:
```python
import functools

import jax
import jax.numpy as jnp
import numpy as np
from jax import lax
from jax.experimental import pallas as pl
from jax.experimental.pallas import tpu as pltpu
from jax.sharding import Mesh, PartitionSpec as P

BLK = 128
TILE = 64
AXES = ("x", "zh", "zl", "y", "c")
SIZES = (4, 4, 2, 4, 2)
MIB = 1024 * 1024
F32 = jnp.float32
BF16 = jnp.bfloat16

CHUNKS = (384, 384)

ORDER = [(dz, e) for e in (3, 2, 1, 0) for dz in (0, 1)]
MINE, THEIRS, PLACE = 0, 8, 16


def place_table():
    rows = []
    for x, zh, zl, y, c in np.ndindex(*SIZES):
        row = []
        for core in (c, 1 - c):
            for dz, e in ORDER:
                row.append((zl ^ dz) * 8 + ((y + (1 - 2 * core) * e) % 4) * 2 + core)
        rows.append(row + [x, zh, 1 - 2 * c])
    return np.array(rows, np.int32)


def shift(value, axis, step):
    size = SIZES[AXES.index(axis)]
    return lax.ppermute(value, axis, [(i, (i + step) % size) for i in range(size)])


def turn(value, axis, step):
    size = SIZES[AXES.index(axis)]
    pairs = [
        (2 * i + core, 2 * ((i + step * (1 - 2 * core)) % size) + core)
        for i in range(size)
        for core in range(2)
    ]
    return lax.ppermute(value, (axis, "c"), pairs)


def params(mib):
    return pltpu.CompilerParams(vmem_limit_bytes=mib * MIB)


def cost(flops, nbytes):
    return pl.CostEstimate(flops=flops, bytes_accessed=nbytes, transcendentals=0)


def after(value, *deps):
    return lax.optimization_barrier((value, *deps))[0]


def scale_into(out_ref, start, w, scale_ref, block):
    rows, cols = w.shape
    for i in range(rows // BLK):
        parts = [
            (
                w[i * BLK : (i + 1) * BLK, j * BLK : (j + 1) * BLK].astype(F32)
                * scale_ref[i, block * (cols // BLK) + j]
            ).astype(BF16)
            for j in range(cols // BLK)
        ]
        out_ref[start + i * BLK : start + (i + 1) * BLK] = jnp.concatenate(parts, axis=1)


def stage_kernel(skip, meta_ref, scale_ref, w_ref, out_ref, held, done, sem_in, sem_out):
    width = held.shape[2]
    arriving, leaving = [], []
    for j in range(held.shape[0]):
        columns = pl.ds(pl.multiple_of(meta_ref[skip + j] * width, width), width)
        copy = pltpu.make_async_copy(w_ref.at[:, columns], held.at[j], sem_in.at[j])
        copy.start()
        arriving.append(copy)
    for j in range(held.shape[0]):
        arriving[j].wait()
        scale_into(done.at[j], 0, held[j], scale_ref, meta_ref[skip + j])
        copy = pltpu.make_async_copy(done.at[j], out_ref.at[j], sem_out.at[j])
        copy.start()
        leaving.append(copy)
    for copy in leaving:
        copy.wait()


def stage(values, scales, meta, skip, n, width):
    feats = values.shape[0]
    return pl.pallas_call(
        functools.partial(stage_kernel, THEIRS + skip),
        out_shape=jax.ShapeDtypeStruct((n, feats, width), BF16),
        in_specs=[
            pl.BlockSpec(memory_space=pltpu.SMEM),
            pl.BlockSpec(memory_space=pltpu.SMEM),
            pl.BlockSpec(memory_space=pl.ANY),
        ],
        out_specs=pl.BlockSpec(memory_space=pl.ANY),
        scratch_shapes=[
            pltpu.VMEM((n, feats, width), BF16),
            pltpu.VMEM((n, feats, width), BF16),
            pltpu.SemaphoreType.DMA((n,)),
            pltpu.SemaphoreType.DMA((n,)),
        ],
        compiler_params=params(16),
        cost_estimate=cost(0, 4 * n * feats * width),
        name="stage",
    )(meta, scales, values)


def partial_kernel(skip, outputs, meta_ref, x_ref, xs_ref, w_ref, ws_ref, s_ref, *rest):
    outs, scr = rest[:-1], rest[-1]
    step = pl.program_id(0)
    scale_into(scr, 0, w_ref[...], s_ref, meta_ref[skip + step])
    value = (
        jnp.dot(xs_ref[...], ws_ref[0], preferred_element_type=F32)
        + jnp.dot(x_ref[...], scr[...], preferred_element_type=F32)
    ).astype(BF16)
    for first in sorted({o[0] for o in outputs}):
        stores = [(k, o) for k, o in enumerate(outputs) if o[0] == first]

        @pl.when((step >= first) & (step < first + 2))
        def _(stores=stores):
            for k, (_, start, rows) in stores:
                outs[k][0] = value[start : start + rows]


def partials(tokens, other, values, others, scales, meta, skip, outputs):
    rows, feats = tokens.shape
    n, _, width = others.shape
    whole = pl.BlockSpec((rows, feats), lambda j, m: (0, 0))
    return pl.pallas_call(
        functools.partial(partial_kernel, MINE + skip, outputs),
        out_shape=[jax.ShapeDtypeStruct((2, size, width), BF16) for _, _, size in outputs],
        grid_spec=pltpu.PrefetchScalarGridSpec(
            num_scalar_prefetch=1,
            grid=(n,),
            in_specs=[
                whole,
                whole,
                pl.BlockSpec((feats, width), lambda j, m: (0, m[MINE + skip + j])),
                pl.BlockSpec((1, feats, width), lambda j, m: (j, 0, 0)),
                pl.BlockSpec(memory_space=pltpu.SMEM),
            ],
            out_specs=[
                pl.BlockSpec((1, size, width), lambda j, m, first=first: (jnp.clip(j - first, 0, 1), 0, 0))
                for first, _, size in outputs
            ],
            scratch_shapes=[pltpu.VMEM((feats, width), BF16)],
        ),
        compiler_params=params(30),
        cost_estimate=cost(4 * n * rows * feats * width, 2 * n * width * (2 * feats + rows)),
        name="partials",
    )(meta, tokens, other, values, others, scales)


def plus(*parts):
    total = parts[0].astype(F32)
    for part in parts[1:]:
        total = total + part.astype(F32)
    return total.astype(BF16)


def locate(slot_ref, adapter_ref, place_ref, tile):
    slot = slot_ref[adapter_ref[tile]]
    dx = (place_ref[PLACE + 2] * (lax.shift_right_logical(slot, 3) - place_ref[PLACE]) + 4) & 3
    dz = (place_ref[PLACE + 2] * ((lax.shift_right_logical(slot, 1) & 3) - place_ref[PLACE + 1]) + 4) & 3
    return dx, dz * 2 + (slot & 1)


def fetch(tiles, slot_ref, adapter_ref, place_ref, buffers, held, sems):
    for t in range(tiles):
        dx, at = locate(slot_ref, adapter_ref, place_ref, t)
        for k, ref in enumerate(buffers):

            @pl.when(dx == k)
            def _(ref=ref, at=at, t=t):
                pltpu.make_async_copy(
                    ref.at[at], held.at[pl.ds(t * TILE, TILE)], sems.at[t]
                ).start()


def wait_for(t, buffers, held, sems):
    pltpu.make_async_copy(
        buffers[0].at[0], held.at[pl.ds(t * TILE, TILE)], sems.at[t]
    ).wait()


def shrink_kernel(slot_ref, adapter_ref, place_ref, x_ref, *rest):
    buffers, out_ref, held, sems = rest[:4], rest[4], rest[5], rest[6]
    tiles = adapter_ref.shape[0]
    fetch(tiles, slot_ref, adapter_ref, place_ref, buffers, held, sems)
    left = lax.broadcasted_iota(jnp.int32, (TILE, 2 * TILE), 1) < TILE
    for t in range(0, tiles, 2):
        wait_for(t, buffers, held, sems)
        wait_for(t + 1, buffers, held, sems)
        both = lax.dot_general(
            x_ref[t * TILE : (t + 2) * TILE],
            held[t * TILE : (t + 2) * TILE],
            (((1,), (1,)), ((), ())),
            preferred_element_type=F32,
        )
        out_ref[t * TILE // 2 : (t + 2) * TILE // 2] = jnp.where(
            left, both[:TILE], both[TILE:]
        ).astype(BF16)


def expand_kernel(slot_ref, adapter_ref, place_ref, count_ref, s0, s1, s2, s3, *rest):
    buffers, out_ref, held, sems = rest[:4], rest[4], rest[5], rest[6]
    tiles = adapter_ref.shape[0]
    fetch(tiles, slot_ref, adapter_ref, place_ref, buffers, held, sems)
    left = lax.broadcasted_iota(jnp.int32, (TILE, 2 * TILE), 1) < TILE
    for t in range(0, tiles, 2):
        wait_for(t, buffers, held, sems)
        wait_for(t + 1, buffers, held, sems)
        at = pl.ds(t * TILE // 2, TILE)
        total = (
            s0[at].astype(F32) + s1[at].astype(F32) + s2[at].astype(F32) + s3[at].astype(F32)
        )
        factors = held[t * TILE : (t + 2) * TILE]
        for k in range(2):
            shrink = jnp.where(left == (k == 0), total, 0.0).astype(BF16)
            delta = jnp.dot(shrink, factors, preferred_element_type=F32)
            row = lax.broadcasted_iota(jnp.int32, delta.shape, 0)
            out_ref[(t + k) * TILE : (t + k + 1) * TILE] = jnp.where(
                row < count_ref[t + k], delta, 0.0
            )


def with_factors(kernel, shape, scalars, arrays, buffers, width, tiles, name):
    return pl.pallas_call(
        kernel,
        out_shape=shape,
        in_specs=[pl.BlockSpec(memory_space=pltpu.SMEM)] * len(scalars)
        + [pl.BlockSpec(memory_space=pltpu.VMEM)] * len(arrays)
        + [pl.BlockSpec(memory_space=pl.ANY)] * len(buffers),
        out_specs=pl.BlockSpec(memory_space=pltpu.VMEM),
        scratch_shapes=[
            pltpu.VMEM((tiles * TILE, width), BF16),
            pltpu.SemaphoreType.DMA((tiles,)),
        ],
        compiler_params=params(12),
        cost_estimate=cost(2 * tiles * TILE * TILE * width, 6 * tiles * TILE * width),
        name=name,
    )(*scalars, *arrays, *buffers)


def gather_near(mine, axis):
    return turn(mine, axis, 1), turn(mine, axis, -1)


def gather_round(mine, axis):
    behind = turn(mine, axis, 1)
    across = turn(behind, axis, 1)
    return mine, turn(across, axis, 1), across, behind


def gather_all(mine, pair, axis, *deps):
    behind, ahead = pair
    return mine, ahead, turn(after(behind, *deps), axis, 1), behind


def finish_kernel(spans, delta_ref, *rest):
    refs, out_ref = rest[:-1], rest[-1]
    for start, rows, first, count in spans:
        total = delta_ref[start : start + rows]
        for ref in refs[first : first + count]:
            total = total + ref[0].astype(F32)
        out_ref[start : start + rows] = total.astype(BF16)


def body(
    tokens,
    base_values,
    base_scales,
    shrink_factors,
    expand_factors,
    adapter_slot,
    tile_adapter,
    tile_count,
):
    rows, feats = tokens.shape
    tiles = rows // TILE
    width = base_values.shape[1] // 16
    first, second = CHUNKS
    table = jnp.asarray(place_table())
    meta = lax.dynamic_index_in_dim(table, lax.axis_index(AXES), 0, keepdims=False)

    other = shift(tokens, "c", 1)
    far_w = shift(stage(base_values, base_scales, meta, 0, 2, width), "c", 1)
    near_w = stage(base_values, base_scales, meta, 2, 6, width)

    down_mine = jnp.swapaxes(shrink_factors, 1, 2)
    behind, ahead = gather_near(down_mine, "zh")
    down_line = (down_mine, ahead, turn(down_mine, "zh", 2), behind)

    def product(weights, skip, outputs):
        return partials(tokens, other, base_values, weights, base_scales, meta, skip, outputs)

    far = product(far_w, 0, [(0, 0, first), (0, first, second)])
    near_w = shift(after(near_w, far_w, other), "c", 1)
    got1, got2 = turn(far[0], "y", 1), turn(far[1], "y", 1)

    near = product(
        after(near_w, far[0]),
        2,
        [(k, start, size) for k in (0, 2, 4) for start, size in ((0, first), (first, second))],
    )
    got1 = turn(plus(near[0], got1), "y", 1)
    got2 = turn(plus(near[1], got2), "y", 1)

    down_line = lax.optimization_barrier((*down_line, near[0]))[:4]
    down_line = jnp.concatenate(down_line, axis=0)
    down_pair = gather_near(down_line, "x")
    down = gather_all(down_line, down_pair, "x")
    up_mine = after(expand_factors, down_line)
    up_line = gather_round(up_mine, "zh")
    up_line = after(jnp.concatenate(up_line, axis=0), *down_pair)
    up = gather_all(up_line, gather_near(up_line, "x"), "x")

    got1 = turn(plus(near[2], got1), "y", 1)
    got2 = turn(plus(near[3], got2), "y", 1)

    scalars = (adapter_slot, tile_adapter, meta)
    shrink = with_factors(
        shrink_kernel,
        jax.ShapeDtypeStruct((rows // 2, 2 * TILE), BF16),
        scalars,
        (tokens,),
        down,
        feats,
        tiles,
        "shrink",
    )
    shrink = plus(shrink, shift(shrink, "c", 1))
    shrink = plus(shrink, shift(shrink, "zl", 1))
    terms = (shrink, turn(shrink, "y", 1), turn(shrink, "y", -1), turn(shrink, "y", 2))

    side1 = shift(plus(near[4][1:], got1[1:]), "zl", 1)
    side2 = shift(plus(near[5][1:], got2[1:]), "zl", 1)
    finals = [
        (0, first, [near[4], got1, side1]),
        (first, second, [near[5], got2, side2]),
    ]

    delta = with_factors(
        expand_kernel,
        jax.ShapeDtypeStruct((rows, width), F32),
        scalars + (tile_count,),
        terms,
        up,
        width,
        tiles,
        "expand",
    )

    spans, args = [], []
    for start, size, parts in finals:
        spans.append((start, size, len(args), len(parts)))
        args += [(p, size) for p in parts]
    return pl.pallas_call(
        functools.partial(finish_kernel, spans),
        out_shape=jax.ShapeDtypeStruct((rows, width), BF16),
        grid=(1,),
        in_specs=[pl.BlockSpec((rows, width), lambda j: (0, 0))]
        + [pl.BlockSpec((1, size, width), lambda j: (0, 0, 0)) for _, size in args],
        out_specs=pl.BlockSpec((rows, width), lambda j: (0, 0)),
        compiler_params=params(24),
        cost_estimate=cost(0, 14 * rows * width),
        name="finish",
    )(delta, *(p for p, _ in args))


def solution(mesh):
    split = Mesh(mesh.devices.reshape(SIZES), AXES)
    group, tensor = ("x", "zh"), ("zl", "y", "c")
    in_specs = (
        P(group, tensor),
        P(tensor, None),
        P(tensor, None),
        P(group, tensor, None),
        P(group, None, tensor),
        P(),
        P(group),
        P(group),
    )
    return jax.shard_map(
        body, mesh=split, in_specs=in_specs, out_specs=P(group, tensor), check_vma=False
    )
```

time: 347 us -> 110 us (0.32)
  waiting for transfers between devices: 245 us -> 39.9 us
  matrix products: 65.3 us -> 0 us
  starting transfers between devices: 0.12 us -> 39.9 us
  Pallas kernels: 0 us -> 22 us
  between operations: 13.2 us -> 0.31 us
  local copies, waits for them, and re-layouts: 16.7 us -> 4.85 us
    psum x1 -> x0, waiting for transfers between devices: 98.9 us -> none  [body(): shrink_total = lax.psum(shrink_part.astype(jnp.bfloat16), 'tensor')]
    reduce_scatter x1 -> x0, waiting for transfers between devices: 81.4 us -> none  [body(): lax.psum_scatter(partial_sum.astype(jnp.bfloat16), 'tensor', scatter_dime...]
    dot_general x3 -> x0, matrix products: 65.3 us -> none  [the longest x1 61.8 us: body(): partial_sum = jnp.dot(tokens, weights, preferred_element_type=jnp.float32)]
    all_gather x2 -> x0, waiting for transfers between devices: 62.9 us -> none  [the longest x1 62.9 us: body(): lax.all_gather(shrink_factors, 'group', axis=0, tiled=True)]
    ppermute x0 -> x28, waiting for transfers between devices: none -> 39.9 us  [the longest x21 35.5 us: turn(): return lax.ppermute(value, (axis, 'c'), pairs)]
    ppermute x0 -> x28, starting transfers between devices: none -> 39.9 us  [the longest x21 36.8 us: turn(): return lax.ppermute(value, (axis, 'c'), pairs)]
    pallas_call x0 -> x7, Pallas kernels: none -> 22 us  [the longest x2 11.3 us: partials(): pl.pallas_call(functools.partial(partial_kernel, MINE + skip, outputs), o...]
    mul x1 -> x0, local copies, waits for them, and re-layouts: 8.61 us -> none  [body(): base_values.reshape(feat_count // BLK, BLK, col_count // BLK, BLK)]
  transfers between devices with their start and end apart: 4 -> 28, of which waited for: 3 -> 10; matrix products, arithmetic and copies ran while one was open for 24% -> 1% of each run, Pallas kernels for 0% -> 18%
where the time goes in v2:
time: 110 us; the launch traced here: 108 us
  starting transfers between devices  39.9 us (36%)
  waiting for transfers between devices  39.9 us (36%)
  Pallas kernels  22 us (20%)
  local copies, waits for them, and re-layouts  4.85 us (4%)
  other arithmetic  1.18 us (1%)
    ppermute x21, starting transfers between devices, turn(): return lax.ppermute(value, (axis, 'c'), pairs)  36.8 us
    ppermute x21, waiting for transfers between devices, turn(): return lax.ppermute(value, (axis, 'c'), pairs)  35.5 us
    pallas_call x2, Pallas kernels, partials(): pl.pallas_call(functools.partial(partial_kernel, MINE + skip, outputs), o...  11.3 us
    pallas_call x2, Pallas kernels, with_factors(): pl.pallas_call(kernel, out_shape=shape, in_specs=[pl.BlockSpec(memory_spa...  6.41 us
    ppermute x7, waiting for transfers between devices, shift(): lax.ppermute(value, axis, [(i, (i + step) % size) for i in range(size)])  4.43 us
    unnamed x25, local copies, waits for them, and re-layouts  4.15 us
    ppermute x7, starting transfers between devices, shift(): lax.ppermute(value, axis, [(i, (i + step) % size) for i in range(size)])  3.11 us
    pallas_call x2, Pallas kernels, stage(): pl.pallas_call(functools.partial(stage_kernel, THEIRS + skip), out_shape=...  3.01 us
  transfers between devices with their start and end apart: 28, of which 10 were waited for; matrix products, arithmetic and copies ran while one was open for 1% of the time, Pallas kernels for 18%

profile of v2, /device:TPU:8, one launch (start us, length us, event | category | flops | bytes accessed | tf_op | source)
XLA Modules:
  0.0 108.1 jit_solution(5027529204236469811)
XLA Ops:
  0.0 0.7 dynamic-slice_bitcast_fusion.meta_ref.place_ref
  0.7 3.4 %copy-done = bf16[512,8192]{1,0:T(8,128)(2,1)S(1)} copy-done((bf16[512,8192]{1,0:T(8,128)(2,1)S(1)}, bf16[512,8192]{1,0:T(8,128)(2,1)}, u32[]{:S(2)}) %copy-start) | copy-done | bytes 8388632
  4.1 0.7 copy-done.2
  4.8 1.0 stage.3
  6.0 0.5 collective-permute-start.3
  6.4 2.0 %stage.2 = bf16[6,512,512]{2,1,0:T(8,128)(2,1)S(1)} custom-call(s32[19]{0:T(128)S(1)} %dynamic-slice_bitcast_fusion.meta_ref.place_ref, f32[4,64]{1,0:T(4,128)S(1)} %copy-done.2, bf16[512,8192]{1,0:T(8,128)(2,1)S(1)} %copy-done), custom_call_target="tpu_custom_call" | custom-call | bytes 6291456 | tf_op jit(solution)/shard_map/stage/pallas_call | solution.py:96
  8.4 1.3 %collective-permute-done.3.xs_ref = bf16[768,512]{1,0:T(8,128)(2,1)S(1)} collective-permute-done((bf16[768,512]{1,0:T(8,128)(2,1)S(1)}, bf16[768,512]{1,0:T(8,128)(2,1)S(1)}, u32[]{:S(2)}, u32[]{:S(2)}) %collective-permute-start.3) | collective-permute-done | bytes 786464 | tf_op jit(solution)/shard_map/ppermute | solution.py:38
  9.7 0.1 collective-permute-start.5
  9.9 6.3 %collective-permute-start = (bf16[2,64,512]{2,1,0:T(8,128)(2,1)S(1)}, bf16[2,64,512]{2,1,0:T(8,128)(2,1)S(1)}, u32[]{:S(2)}, u32[]{:S(2)}) collective-permute-start(bf16[2,64,512]{2,1,0:T(8,128)(2,1)S(1)} %bitcast.5), channel_id=1, source_target_pairs={{0,48},{1,17},{16,0},{17,33},{32,16},{33,49},{48,32},{49,1},{2,50}... | collective-permute-start | bytes 393224 | tf_op jit(solution)/shard_map/ppermute | solution.py:48
  16.2 0.9 collective-permute-start.1
  17.1 2.9 %collective-permute-start.2 = (bf16[2,64,512]{2,1,0:T(8,128)(2,1)S(1)}, bf16[2,64,512]{2,1,0:T(8,128)(2,1)S(1)}, u32[]{:S(2)}, u32[]{:S(2)}) collective-permute-start(bf16[2,64,512]{2,1,0:T(8,128)(2,1)S(1)} %bitcast.7), channel_id=1, source_target_pairs={{0,16},{1,49},{16,32},{17,1},{32,48},{33,17},{48,0},{49,33},{2,18}... | collective-permute-start | bytes 393224 | tf_op jit(solution)/shard_map/ppermute | solution.py:48
  20.0 3.3 %partials.2 = (bf16[2,384,512]{2,1,0:T(8,128)(2,1)S(1)}, bf16[2,384,512]{2,1,0:T(8,128)(2,1)S(1)}) custom-call(s32[19]{0:T(128)S(1)} %dynamic-slice_bitcast_fusion.meta_ref.place_ref, bf16[768,512]{1,0:T(8,128)(2,1)S(1)} %copy-done.1, bf16[768,512]{1,0:T(8,128)(2,1)S(1)} %collective-permute-done.3.xs_ref, bf16[512,8192]{1,0:T(8,128)(2,1)S(1)} %bitcast.4, ...), custom_call_target="tpu_custom_call" | custom-call | flops 1610612736 | bytes 3670016 | tf_op jit(solution)/shard_map/partials/pallas_call | solution.py:138
  23.3 1.7 %collective-permute-start.24 = (bf16[2,384,512]{2,1,0:T(8,128)(2,1)S(1)}, bf16[2,384,512]{2,1,0:T(8,128)(2,1)S(1)}, u32[]{:S(2)}, u32[]{:S(2)}) collective-permute-start(bf16[2,384,512]{2,1,0:T(8,128)(2,1)S(1)} %get-tuple-element.36), channel_id=1, source_target_pairs={{0,2},{1,7},{2,4},{3,1},{4,6},{5,3},{6,0},{7,5},{8,10},{9,15},{10,... | collective-permute-start | bytes 2359304 | tf_op jit(solution)/shard_map/ppermute | solution.py:48
  25.0 1.3 %collective-permute-start.20 = (bf16[2,384,512]{2,1,0:T(8,128)(2,1)S(1)}, bf16[2,384,512]{2,1,0:T(8,128)(2,1)S(1)}, u32[]{:S(2)}, u32[]{:S(2)}) collective-permute-start(bf16[2,384,512]{2,1,0:T(8,128)(2,1)S(1)} %get-tuple-element.22), channel_id=1, source_target_pairs={{0,2},{1,7},{2,4},{3,1},{4,6},{5,3},{6,0},{7,5},{8,10},{9,15},{10,... | collective-permute-start | bytes 2359304 | tf_op jit(solution)/shard_map/ppermute | solution.py:48
  26.3 8.0 %partials.3 = (bf16[2,384,512]{2,1,0:T(8,128)(2,1)S(1)}, bf16[2,384,512]{2,1,0:T(8,128)(2,1)S(1)}, bf16[2,384,512]{2,1,0:T(8,128)(2,1)S(1)}, bf16[2,384,512]{2,1...) custom-call(s32[19]{0:T(128)S(1)} %dynamic-slice_bitcast_fusion.meta_ref.place_ref, ...), custom_call_target="tpu_custom_call" | custom-call | flops 4831838208 | bytes 11010048 | tf_op jit(solution)/shard_map/partials/pallas_call | solution.py:138
  34.4 2.8 %collective-permute-start.6 = (bf16[8,64,512]{2,1,0:T(8,128)(2,1)S(1)}, bf16[8,64,512]{2,1,0:T(8,128)(2,1)S(1)}, u32[]{:S(2)}, u32[]{:S(2)}) collective-permute-start(bf16[8,64,512]{2,1,0:T(8,128)(2,1)S(1)} %constant_dynamic-update-slice_fusion.rest_0_), channel_id=1, source_target_pairs={{0,192},{1,65},{64,0},{65,129},{128,64},{129,193},{192,128},{193,1... | collective-permute-start | bytes 1572872 | tf_op jit(solution)/shard_map/ppermute | solution.py:48
  37.2 0.2 add_convert_fusion.1
  37.4 0.3 collective-permute-start.25
  37.7 2.7 %collective-permute-start.14 = (bf16[2,64,512]{2,1,0:T(8,128)(2,1)S(1)}, bf16[2,64,512]{2,1,0:T(8,128)(2,1)S(1)}, u32[]{:S(2)}, u32[]{:S(2)}) collective-permute-start(bf16[2,64,512]{2,1,0:T(8,128)(2,1)S(1)} %copy-done.8), channel_id=1, source_target_pairs={{0,16},{1,49},{16,32},{17,1},{32,48},{33,17},{48,0},{49,33},{2,18}... | collective-permute-start | bytes 393224 | tf_op jit(solution)/shard_map/ppermute | solution.py:48
  40.4 3.4 %collective-permute-done.20 = bf16[2,384,512]{2,1,0:T(8,128)(2,1)S(1)} collective-permute-done((bf16[2,384,512]{2,1,0:T(8,128)(2,1)S(1)}, bf16[2,384,512]{2,1,0:T(8,128)(2,1)S(1)}, u32[]{:S(2)}, u32[]{:S(2)}) %collective-permute-start.20) | collective-permute-done | bytes 786464 | tf_op jit(solution)/shard_map/ppermute | solution.py:48
  43.8 0.2 add_convert_fusion.3
  44.0 1.8 %collective-permute-start.21 = (bf16[2,384,512]{2,1,0:T(8,128)(2,1)S(1)}, bf16[2,384,512]{2,1,0:T(8,128)(2,1)S(1)}, u32[]{:S(2)}, u32[]{:S(2)}) collective-permute-start(bf16[2,384,512]{2,1,0:T(8,128)(2,1)S(1)} %add_convert_fusion.3), channel_id=1, source_target_pairs={{0,2},{1,7},{2,4},{3,1},{4,6},{5,3},{6,0},{7,5},{8,10},{9,15},{10,... | collective-permute-start | bytes 2359304 | tf_op jit(solution)/shard_map/ppermute | solution.py:48
  45.9 0.3 collective-permute-done.14
  46.2 2.4 %collective-permute-start.15 = (bf16[2,64,512]{2,1,0:T(8,128)(2,1)S(1)}, bf16[2,64,512]{2,1,0:T(8,128)(2,1)S(1)}, u32[]{:S(2)}, u32[]{:S(2)}) collective-permute-start(bf16[2,64,512]{2,1,0:T(8,128)(2,1)S(1)} %collective-permute-done.14), channel_id=1, source_target_pairs={{0,16},{1,49},{16,32},{17,1},{32,48},{33,17},{48,0},{49,33},{2,18}... | collective-permute-start | bytes 393224 | tf_op jit(solution)/shard_map/ppermute | solution.py:48
  48.6 6.0 %collective-permute-done.15 = bf16[2,64,512]{2,1,0:T(8,128)(2,1)S(1)} collective-permute-done((bf16[2,64,512]{2,1,0:T(8,128)(2,1)S(1)}, bf16[2,64,512]{2,1,0:T(8,128)(2,1)S(1)}, u32[]{:S(2)}, u32[]{:S(2)}) %collective-permute-start.15) | collective-permute-done | bytes 131104 | tf_op jit(solution)/shard_map/ppermute | solution.py:48
  54.6 1.2 %collective-permute-start.16 = (bf16[2,64,512]{2,1,0:T(8,128)(2,1)S(1)}, bf16[2,64,512]{2,1,0:T(8,128)(2,1)S(1)}, u32[]{:S(2)}, u32[]{:S(2)}) collective-permute-start(bf16[2,64,512]{2,1,0:T(8,128)(2,1)S(1)} %collective-permute-done.15), channel_id=1, source_target_pairs={{0,16},{1,49},{16,32},{17,1},{32,48},{33,17},{48,0},{49,33},{2,18}... | collective-permute-start | bytes 393224 | tf_op jit(solution)/shard_map/ppermute | solution.py:48
  55.8 6.4 %collective-permute-done.16 = bf16[2,64,512]{2,1,0:T(8,128)(2,1)S(1)} collective-permute-done((bf16[2,64,512]{2,1,0:T(8,128)(2,1)S(1)}, bf16[2,64,512]{2,1,0:T(8,128)(2,1)S(1)}, u32[]{:S(2)}, u32[]{:S(2)}) %collective-permute-start.16) | collective-permute-done | bytes 131104 | tf_op jit(solution)/shard_map/ppermute | solution.py:48
  62.3 1.3 %collective-permute-start.18 = (bf16[8,64,512]{2,1,0:T(8,128)(2,1)S(1)}, bf16[8,64,512]{2,1,0:T(8,128)(2,1)S(1)}, u32[]{:S(2)}, u32[]{:S(2)}) collective-permute-start(bf16[8,64,512]{2,1,0:T(8,128)(2,1)S(1)} %pad_maximum_fusion.rest_0_), channel_id=1, source_target_pairs={{0,64},{1,193},{64,128},{65,1},{128,192},{129,65},{192,0},{193,129... | collective-permute-start | bytes 1572872 | tf_op jit(solution)/shard_map/ppermute | solution.py:48
  63.7 1.5 %collective-permute-start.8 = (bf16[8,64,512]{2,1,0:T(8,128)(2,1)S(1)}, bf16[8,64,512]{2,1,0:T(8,128)(2,1)S(1)}, u32[]{:S(2)}, u32[]{:S(2)}) collective-permute-start(bf16[8,64,512]{2,1,0:T(8,128)(2,1)S(1)} %collective-permute-done.7.rest_3_), channel_id=1, source_target_pairs={{0,64},{1,193},{64,128},{65,1},{128,192},{129,65},{192,0},{193,129... | collective-permute-start | bytes 1572872 | tf_op jit(solution)/shard_map/ppermute | solution.py:48
  65.2 0.2 add_convert_fusion
  65.4 1.4 %collective-permute-start.26 = (bf16[2,384,512]{2,1,0:T(8,128)(2,1)S(1)}, bf16[2,384,512]{2,1,0:T(8,128)(2,1)S(1)}, u32[]{:S(2)}, u32[]{:S(2)}) collective-permute-start(bf16[2,384,512]{2,1,0:T(8,128)(2,1)S(1)} %add_convert_fusion), channel_id=1, source_target_pairs={{0,2},{1,7},{2,4},{3,1},{4,6},{5,3},{6,0},{7,5},{8,10},{9,15},{10,... | collective-permute-start | bytes 2359304 | tf_op jit(solution)/shard_map/ppermute | solution.py:48
  66.8 0.2 add_convert_fusion.2
  67.0 1.5 %collective-permute-start.22 = (bf16[2,384,512]{2,1,0:T(8,128)(2,1)S(1)}, bf16[2,384,512]{2,1,0:T(8,128)(2,1)S(1)}, u32[]{:S(2)}, u32[]{:S(2)}) collective-permute-start(bf16[2,384,512]{2,1,0:T(8,128)(2,1)S(1)} %add_convert_fusion.2), channel_id=1, source_target_pairs={{0,2},{1,7},{2,4},{3,1},{4,6},{5,3},{6,0},{7,5},{8,10},{9,15},{10,... | collective-permute-start | bytes 2359304 | tf_op jit(solution)/shard_map/ppermute | solution.py:48
  68.5 9.9 %collective-permute-done.8.rest_2_ = bf16[8,64,512]{2,1,0:T(8,128)(2,1)S(1)} collective-permute-done((bf16[8,64,512]{2,1,0:T(8,128)(2,1)S(1)}, bf16[8,64,512]{2,1,0:T(8,128)(2,1)S(1)}, u32[]{:S(2)}, u32[]{:S(2)}) %collective-permute-start.8) | collective-permute-done | bytes 524320 | tf_op jit(solution)/shard_map/ppermute | solution.py:48
  78.4 3.3 %shrink.1 = bf16[384,128]{1,0:T(8,128)(2,1)S(1)} custom-call(s32[32]{0:T(128)S(1)} %copy-done.4, s32[12]{0:T(128)S(1)} %copy-done.5, s32[19]{0:T(128)S(1)} %dynamic-slice_bitcast_fusion.meta_ref.place_ref, bf16[768,512]{1,0:T(8,128)(2,1)S(1)} %copy-done.1, bf16[8,64,512]{2,1,0:T(8,128)(2,1)S(1)} %constant_dynamic-update-slice_fusion.rest_0_, ...), custom_call_target="tpu_custom_call" | custom-call | flops 50331648 | bytes 2359296 | tf_op jit(solution)/shard_map/shrink/pallas_call | solution.py:237
  81.9 2.0 %collective-permute-start.17 = (bf16[8,64,512]{2,1,0:T(8,128)(2,1)S(1)}, bf16[8,64,512]{2,1,0:T(8,128)(2,1)S(1)}, u32[]{:S(2)}, u32[]{:S(2)}) collective-permute-start(bf16[8,64,512]{2,1,0:T(8,128)(2,1)S(1)} %pad_maximum_fusion.rest_0_), channel_id=1, source_target_pairs={{0,192},{1,65},{64,0},{65,129},{128,64},{129,193},{192,128},{193,1... | collective-permute-start | bytes 1572872 | tf_op jit(solution)/shard_map/ppermute | solution.py:48
  83.9 0.1 collective-permute-start.19
  84.2 2.1 %collective-permute-start.27 = (bf16[1,384,512]{2,1,0:T(8,128)(2,1)S(1)}, bf16[1,384,512]{2,1,0:T(8,128)(2,1)S(1)}, u32[]{:S(2)}, u32[]{:S(2)}) collective-permute-start(bf16[1,384,512]{2,1,0:T(8,128)(2,1)S(1)} %add_convert_fusion.4), channel_id=1, source_target_pairs={{0,8},{8,0},{1,9},{9,1},{2,10},{10,2},{3,11},{11,3},{4,12},{12,4},... | collective-permute-start | bytes 1179656 | tf_op jit(solution)/shard_map/ppermute | solution.py:38
  86.4 0.1 collective-permute-start.23
  86.5 3.1 %collective-permute-done.10 = bf16[384,128]{1,0:T(8,128)(2,1)S(1)} collective-permute-done((bf16[384,128]{1,0:T(8,128)(2,1)S(1)}, bf16[384,128]{1,0:T(8,128)(2,1)S(1)}, u32[]{:S(2)}, u32[]{:S(2)}) %collective-permute-start.10) | collective-permute-done | bytes 98336 | tf_op jit(solution)/shard_map/ppermute | solution.py:38
  89.7 1.6 %collective-permute-start.11 = (bf16[384,128]{1,0:T(8,128)(2,1)S(1)}, bf16[384,128]{1,0:T(8,128)(2,1)S(1)}, u32[]{:S(2)}, u32[]{:S(2)}) collective-permute-start(bf16[384,128]{1,0:T(8,128)(2,1)S(1)} %add_convert_fusion.6.s0), channel_id=1, source_target_pairs={{0,2},{1,7},{2,4},{3,1},{4,6},{5,3},{6,0},{7,5},{8,10},{9,15},{10,... | collective-permute-start | bytes 294920 | tf_op jit(solution)/shard_map/ppermute | solution.py:48
  91.3 4.9 %collective-permute-done.17.rest_1_ = bf16[8,64,512]{2,1,0:T(8,128)(2,1)S(1)} collective-permute-done((bf16[8,64,512]{2,1,0:T(8,128)(2,1)S(1)}, bf16[8,64,512]{2,1,0:T(8,128)(2,1)S(1)}, u32[]{:S(2)}, u32[]{:S(2)}) %collective-permute-start.17) | collective-permute-done | bytes 524320 | tf_op jit(solution)/shard_map/ppermute | solution.py:48
  96.2 0.9 collective-permute-start.12
  97.1 2.2 %collective-permute-start.13 = (bf16[384,128]{1,0:T(8,128)(2,1)S(1)}, bf16[384,128]{1,0:T(8,128)(2,1)S(1)}, u32[]{:S(2)}, u32[]{:S(2)}) collective-permute-start(bf16[384,128]{1,0:T(8,128)(2,1)S(1)} %add_convert_fusion.6.s0), channel_id=1, source_target_pairs={{0,4},{1,5},{2,6},{3,7},{4,0},{5,1},{6,2},{7,3},{8,12},{9,13},{10,... | collective-permute-start | bytes 294920 | tf_op jit(solution)/shard_map/ppermute | solution.py:48
  99.2 1.9 %collective-permute-done.12.s2 = bf16[384,128]{1,0:T(8,128)(2,1)S(1)} collective-permute-done((bf16[384,128]{1,0:T(8,128)(2,1)S(1)}, bf16[384,128]{1,0:T(8,128)(2,1)S(1)}, u32[]{:S(2)}, u32[]{:S(2)}) %collective-permute-start.12) | collective-permute-done | bytes 98336 | tf_op jit(solution)/shard_map/ppermute | solution.py:48
  101.2 2.6 %collective-permute-done.13.s3 = bf16[384,128]{1,0:T(8,128)(2,1)S(1)} collective-permute-done((bf16[384,128]{1,0:T(8,128)(2,1)S(1)}, bf16[384,128]{1,0:T(8,128)(2,1)S(1)}, u32[]{:S(2)}, u32[]{:S(2)}) %collective-permute-start.13) | collective-permute-done | bytes 98336 | tf_op jit(solution)/shard_map/ppermute | solution.py:48
  103.8 3.1 %expand.1.delta_ref = f32[768,512]{1,0:T(8,128)S(1)} custom-call(s32[32]{0:T(128)S(1)} %copy-done.4, s32[12]{0:T(128)S(1)} %copy-done.5, s32[19]{0:T(128)S(1)} %dynamic-slice_bitcast_fusion.meta_ref.place_ref, s32[12]{0:T(128)S(1)} %copy-done.6, bf16[384,128]{1,0:T(8,128)(2,1)S(1)} %add_convert_fusion.6.s0, bf16[384,128]{1,0:T(8,128)(2,1)S(1)} %collective-permute-done.11.s1, ...), custom_call_target="tpu_custom_call" | custom-call | flops 50331648 | bytes 2359296 | tf_op jit(solution)/shard_map/expand/pallas_call | solution.py:237
  106.9 1.2 %finish.1 = bf16[768,512]{1,0:T(8,128)(2,1)} custom-call(f32[768,512]{1,0:T(8,128)S(1)} %expand.1.delta_ref, bf16[2,384,512]{2,1,0:T(8,128)(2,1)S(1)} %get-tuple-element.31.rest_0_, bf16[2,384,512]{2,1,0:T(8,128)(2,1)S(1)} %collective-permute-done.22.rest_1_, bf16[1,384,512]{2,1,0:T(8,128)(2,1)S(1)} %collective-permute-done.23.rest_2_, ...), custom_call_target="tpu_custom_call" | custom-call | bytes 5505024 | tf_op jit(solution)/shard_map/finish/pallas_call | solution.py:367
  (52 shorter events, 0.8 us)
Async XLA Ops:
  0.7 3.4 %copy-start = (bf16[512,8192]{1,0:T(8,128)(2,1)S(1)}, bf16[512,8192]{1,0:T(8,128)(2,1)}, u32[]{:S(2)}) copy-start(bf16[512,8192]{1,0:T(8,128)(2,1)} %w_ref.7) | copy-start | bytes 25165828
  4.1 0.7 copy-start.2
  4.8 1.2 %copy-start.1 = (bf16[768,512]{1,0:T(8,128)(2,1)S(1)}, bf16[768,512]{1,0:T(8,128)(2,1)}, u32[]{:S(2)}) copy-start(bf16[768,512]{1,0:T(8,128)(2,1)} %x_ref.5) | copy-start | bytes 2359300
  4.8 15.2 %slice-start = ((s8[8388608]{0:T(1024)(128)(4,1)}), s8[4194304]{0:T(1024)(128)(4,1)S(1)}, s32[]{:S(2)}) async-start(s8[8388608]{0:T(1024)(128)(4,1)} %bitcast.3), calls=%async_computation | async-start | bytes 8388608
  5.8 4.1 %copy-start.7 = (bf16[2,512,64]{1,2,0:T(8,128)(2,1)S(1)}, bf16[2,512,64]{1,2,0:T(8,128)(2,1)}, u32[]{:S(2)}) copy-start(bf16[2,512,64]{1,2,0:T(8,128)(2,1)} %param.12) | copy-start | bytes 393220
  5.8 14.2 %slice-start.1 = ((s8[8388608]{0:T(1024)(128)(4,1)}), s8[4194304]{0:T(1024)(128)(4,1)S(1)}, s32[]{:S(2)}) async-start(s8[8388608]{0:T(1024)(128)(4,1)} %bitcast.3), calls=%async_computation.1 | async-start | bytes 8388608
  5.8 14.2 %copy-start.3 = (f32[4,64]{1,0:T(4,128)S(1)}, f32[4,64]{1,0:T(4,128)}, u32[]{:S(2)}) copy-start(f32[4,64]{1,0:T(4,128)} %s_ref.3) | copy-start | bytes 3076
  5.8 3.9 %collective-permute-start.4 = (bf16[2,512,512]{2,1,0:T(8,128)(2,1)S(1)}, bf16[2,512,512]{2,1,0:T(8,128)(2,1)S(1)}, u32[]{:S(2)}, u32[]{:S(2)}) collective-permute-start(bf16[2,512,512]{2,1,0:T(8,128)(2,1)S(1)} %stage.3), channel_id=1, source_target_pairs={{0,1},{1,0},{2,3},{3,2},{4,5},{5,4},{6,7},{7,6},{8,9},{9,8},{10,11... | collective-permute-start | bytes 3145736 | tf_op jit(solution)/shard_map/ppermute | solution.py:38
  6.0 3.8 %collective-permute-start.3 = (bf16[768,512]{1,0:T(8,128)(2,1)S(1)}, bf16[768,512]{1,0:T(8,128)(2,1)S(1)}, u32[]{:S(2)}, u32[]{:S(2)}) collective-permute-start(bf16[768,512]{1,0:T(8,128)(2,1)S(1)} %copy-done.1), channel_id=1, source_target_pairs={{0,1},{1,0},{2,3},{3,2},{4,5},{5,4},{6,7},{7,6},{8,9},{9,8},{10,11... | collective-permute-start | bytes 2359304 | tf_op jit(solution)/shard_map/ppermute | solution.py:38
  9.7 15.3 %collective-permute-start.5 = (bf16[6,512,512]{2,1,0:T(8,128)(2,1)S(1)}, bf16[6,512,512]{2,1,0:T(8,128)(2,1)S(1)}, u32[]{:S(2)}, u32[]{:S(2)}) collective-permute-start(bf16[6,512,512]{2,1,0:T(8,128)(2,1)S(1)} %stage.2), channel_id=1, source_target_pairs={{0,1},{1,0},{2,3},{3,2},{4,5},{5,4},{6,7},{7,6},{8,9},{9,8},{10,11... | collective-permute-start | bytes 9437192 | tf_op jit(solution)/shard_map/ppermute | solution.py:38
  9.9 24.4 %collective-permute-start = (bf16[2,64,512]{2,1,0:T(8,128)(2,1)S(1)}, bf16[2,64,512]{2,1,0:T(8,128)(2,1)S(1)}, u32[]{:S(2)}, u32[]{:S(2)}) collective-permute-start(bf16[2,64,512]{2,1,0:T(8,128)(2,1)S(1)} %bitcast.5), channel_id=1, source_target_pairs={{0,48},{1,17},{16,0},{17,33},{32,16},{33,49},{48,32},{49,1},{2,50}... | collective-permute-start | bytes 393224 | tf_op jit(solution)/shard_map/ppermute | solution.py:48
  16.2 18.1 %collective-permute-start.1 = (bf16[2,64,512]{2,1,0:T(8,128)(2,1)S(1)}, bf16[2,64,512]{2,1,0:T(8,128)(2,1)S(1)}, u32[]{:S(2)}, u32[]{:S(2)}) collective-permute-start(bf16[2,64,512]{2,1,0:T(8,128)(2,1)S(1)} %bitcast.6), channel_id=1, source_target_pairs={{0,32},{1,33},{16,48},{17,49},{32,0},{33,1},{48,16},{49,17},{2,34}... | collective-permute-start | bytes 393224 | tf_op jit(solution)/shard_map/ppermute | solution.py:48
  17.1 17.2 %collective-permute-start.2 = (bf16[2,64,512]{2,1,0:T(8,128)(2,1)S(1)}, bf16[2,64,512]{2,1,0:T(8,128)(2,1)S(1)}, u32[]{:S(2)}, u32[]{:S(2)}) collective-permute-start(bf16[2,64,512]{2,1,0:T(8,128)(2,1)S(1)} %bitcast.7), channel_id=1, source_target_pairs={{0,16},{1,49},{16,32},{17,1},{32,48},{33,17},{48,0},{49,33},{2,18}... | collective-permute-start | bytes 393224 | tf_op jit(solution)/shard_map/ppermute | solution.py:48
  23.3 13.9 %collective-permute-start.24 = (bf16[2,384,512]{2,1,0:T(8,128)(2,1)S(1)}, bf16[2,384,512]{2,1,0:T(8,128)(2,1)S(1)}, u32[]{:S(2)}, u32[]{:S(2)}) collective-permute-start(bf16[2,384,512]{2,1,0:T(8,128)(2,1)S(1)} %get-tuple-element.36), channel_id=1, source_target_pairs={{0,2},{1,7},{2,4},{3,1},{4,6},{5,3},{6,0},{7,5},{8,10},{9,15},{10,... | collective-permute-start | bytes 2359304 | tf_op jit(solution)/shard_map/ppermute | solution.py:48
  25.0 18.8 %collective-permute-start.20 = (bf16[2,384,512]{2,1,0:T(8,128)(2,1)S(1)}, bf16[2,384,512]{2,1,0:T(8,128)(2,1)S(1)}, u32[]{:S(2)}, u32[]{:S(2)}) collective-permute-start(bf16[2,384,512]{2,1,0:T(8,128)(2,1)S(1)} %get-tuple-element.22), channel_id=1, source_target_pairs={{0,2},{1,7},{2,4},{3,1},{4,6},{5,3},{6,0},{7,5},{8,10},{9,15},{10,... | collective-permute-start | bytes 2359304 | tf_op jit(solution)/shard_map/ppermute | solution.py:48
  34.3 3.4 %copy-start.8 = (bf16[2,64,512]{2,1,0:T(8,128)(2,1)S(1)}, bf16[2,64,512]{2,1,0:T(8,128)(2,1)}, u32[]{:S(2)}) copy-start(bf16[2,64,512]{2,1,0:T(8,128)(2,1)} %param.13) | copy-start | bytes 393220
  34.4 27.9 %collective-permute-start.6 = (bf16[8,64,512]{2,1,0:T(8,128)(2,1)S(1)}, bf16[8,64,512]{2,1,0:T(8,128)(2,1)S(1)}, u32[]{:S(2)}, u32[]{:S(2)}) collective-permute-start(bf16[8,64,512]{2,1,0:T(8,128)(2,1)S(1)} %constant_dynamic-update-slice_fusion.rest_0_), channel_id=1, source_target_pairs={{0,192},{1,65},{64,0},{65,129},{128,64},{129,193},{192,128},{193,1... | collective-permute-start | bytes 1572872 | tf_op jit(solution)/shard_map/ppermute | solution.py:48
  37.2 25.1 %collective-permute-start.7 = (bf16[8,64,512]{2,1,0:T(8,128)(2,1)S(1)}, bf16[8,64,512]{2,1,0:T(8,128)(2,1)S(1)}, u32[]{:S(2)}, u32[]{:S(2)}) collective-permute-start(bf16[8,64,512]{2,1,0:T(8,128)(2,1)S(1)} %constant_dynamic-update-slice_fusion.rest_0_), channel_id=1, source_target_pairs={{0,64},{1,193},{64,128},{65,1},{128,192},{129,65},{192,0},{193,129... | collective-permute-start | bytes 1572872 | tf_op jit(solution)/shard_map/ppermute | solution.py:48
  37.4 27.8 %collective-permute-start.25 = (bf16[2,384,512]{2,1,0:T(8,128)(2,1)S(1)}, bf16[2,384,512]{2,1,0:T(8,128)(2,1)S(1)}, u32[]{:S(2)}, u32[]{:S(2)}) collective-permute-start(bf16[2,384,512]{2,1,0:T(8,128)(2,1)S(1)} %add_convert_fusion.1), channel_id=1, source_target_pairs={{0,2},{1,7},{2,4},{3,1},{4,6},{5,3},{6,0},{7,5},{8,10},{9,15},{10,... | collective-permute-start | bytes 2359304 | tf_op jit(solution)/shard_map/ppermute | solution.py:48
  37.7 8.4 %collective-permute-start.14 = (bf16[2,64,512]{2,1,0:T(8,128)(2,1)S(1)}, bf16[2,64,512]{2,1,0:T(8,128)(2,1)S(1)}, u32[]{:S(2)}, u32[]{:S(2)}) collective-permute-start(bf16[2,64,512]{2,1,0:T(8,128)(2,1)S(1)} %copy-done.8), channel_id=1, source_target_pairs={{0,16},{1,49},{16,32},{17,1},{32,48},{33,17},{48,0},{49,33},{2,18}... | collective-permute-start | bytes 393224 | tf_op jit(solution)/shard_map/ppermute | solution.py:48
  44.0 22.7 %collective-permute-start.21 = (bf16[2,384,512]{2,1,0:T(8,128)(2,1)S(1)}, bf16[2,384,512]{2,1,0:T(8,128)(2,1)S(1)}, u32[]{:S(2)}, u32[]{:S(2)}) collective-permute-start(bf16[2,384,512]{2,1,0:T(8,128)(2,1)S(1)} %add_convert_fusion.3), channel_id=1, source_target_pairs={{0,2},{1,7},{2,4},{3,1},{4,6},{5,3},{6,0},{7,5},{8,10},{9,15},{10,... | collective-permute-start | bytes 2359304 | tf_op jit(solution)/shard_map/ppermute | solution.py:48
  46.2 8.4 %collective-permute-start.15 = (bf16[2,64,512]{2,1,0:T(8,128)(2,1)S(1)}, bf16[2,64,512]{2,1,0:T(8,128)(2,1)S(1)}, u32[]{:S(2)}, u32[]{:S(2)}) collective-permute-start(bf16[2,64,512]{2,1,0:T(8,128)(2,1)S(1)} %collective-permute-done.14), channel_id=1, source_target_pairs={{0,16},{1,49},{16,32},{17,1},{32,48},{33,17},{48,0},{49,33},{2,18}... | collective-permute-start | bytes 393224 | tf_op jit(solution)/shard_map/ppermute | solution.py:48
  54.6 7.7 %collective-permute-start.16 = (bf16[2,64,512]{2,1,0:T(8,128)(2,1)S(1)}, bf16[2,64,512]{2,1,0:T(8,128)(2,1)S(1)}, u32[]{:S(2)}, u32[]{:S(2)}) collective-permute-start(bf16[2,64,512]{2,1,0:T(8,128)(2,1)S(1)} %collective-permute-done.15), channel_id=1, source_target_pairs={{0,16},{1,49},{16,32},{17,1},{32,48},{33,17},{48,0},{49,33},{2,18}... | collective-permute-start | bytes 393224 | tf_op jit(solution)/shard_map/ppermute | solution.py:48
  62.3 21.5 %collective-permute-start.18 = (bf16[8,64,512]{2,1,0:T(8,128)(2,1)S(1)}, bf16[8,64,512]{2,1,0:T(8,128)(2,1)S(1)}, u32[]{:S(2)}, u32[]{:S(2)}) collective-permute-start(bf16[8,64,512]{2,1,0:T(8,128)(2,1)S(1)} %pad_maximum_fusion.rest_0_), channel_id=1, source_target_pairs={{0,64},{1,193},{64,128},{65,1},{128,192},{129,65},{192,0},{193,129... | collective-permute-start | bytes 1572872 | tf_op jit(solution)/shard_map/ppermute | solution.py:48
  63.7 14.7 %collective-permute-start.8 = (bf16[8,64,512]{2,1,0:T(8,128)(2,1)S(1)}, bf16[8,64,512]{2,1,0:T(8,128)(2,1)S(1)}, u32[]{:S(2)}, u32[]{:S(2)}) collective-permute-start(bf16[8,64,512]{2,1,0:T(8,128)(2,1)S(1)} %collective-permute-done.7.rest_3_), channel_id=1, source_target_pairs={{0,64},{1,193},{64,128},{65,1},{128,192},{129,65},{192,0},{193,129... | collective-permute-start | bytes 1572872 | tf_op jit(solution)/shard_map/ppermute | solution.py:48
  65.4 13.0 %copy-start.4 = (s32[32]{0:T(128)S(1)}, s32[32]{0:T(128)}, u32[]{:S(2)}) copy-start(s32[32]{0:T(128)} %slot_ref.3) | copy-start | bytes 388
  65.4 13.0 %copy-start.5 = (s32[12]{0:T(128)S(1)}, s32[12]{0:T(128)}, u32[]{:S(2)}) copy-start(s32[12]{0:T(128)} %adapter_ref.3) | copy-start | bytes 148
  65.4 18.7 %collective-permute-start.26 = (bf16[2,384,512]{2,1,0:T(8,128)(2,1)S(1)}, bf16[2,384,512]{2,1,0:T(8,128)(2,1)S(1)}, u32[]{:S(2)}, u32[]{:S(2)}) collective-permute-start(bf16[2,384,512]{2,1,0:T(8,128)(2,1)S(1)} %add_convert_fusion), channel_id=1, source_target_pairs={{0,2},{1,7},{2,4},{3,1},{4,6},{5,3},{6,0},{7,5},{8,10},{9,15},{10,... | collective-permute-start | bytes 2359304 | tf_op jit(solution)/shard_map/ppermute | solution.py:48
  67.0 19.3 %collective-permute-start.22 = (bf16[2,384,512]{2,1,0:T(8,128)(2,1)S(1)}, bf16[2,384,512]{2,1,0:T(8,128)(2,1)S(1)}, u32[]{:S(2)}, u32[]{:S(2)}) collective-permute-start(bf16[2,384,512]{2,1,0:T(8,128)(2,1)S(1)} %add_convert_fusion.2), channel_id=1, source_target_pairs={{0,2},{1,7},{2,4},{3,1},{4,6},{5,3},{6,0},{7,5},{8,10},{9,15},{10,... | collective-permute-start | bytes 2359304 | tf_op jit(solution)/shard_map/ppermute | solution.py:48
  81.8 22.0 %copy-start.6 = (s32[12]{0:T(128)S(1)}, s32[12]{0:T(128)}, u32[]{:S(2)}) copy-start(s32[12]{0:T(128)} %count_ref.1) | copy-start | bytes 148
  81.8 2.2 %collective-permute-start.9 = (bf16[384,128]{1,0:T(8,128)(2,1)S(1)}, bf16[384,128]{1,0:T(8,128)(2,1)S(1)}, u32[]{:S(2)}, u32[]{:S(2)}) collective-permute-start(bf16[384,128]{1,0:T(8,128)(2,1)S(1)} %shrink.1), channel_id=1, source_target_pairs={{0,1},{1,0},{2,3},{3,2},{4,5},{5,4},{6,7},{7,6},{8,9},{9,8},{10,11... | collective-permute-start | bytes 294920 | tf_op jit(solution)/shard_map/ppermute | solution.py:38
  81.9 14.3 %collective-permute-start.17 = (bf16[8,64,512]{2,1,0:T(8,128)(2,1)S(1)}, bf16[8,64,512]{2,1,0:T(8,128)(2,1)S(1)}, u32[]{:S(2)}, u32[]{:S(2)}) collective-permute-start(bf16[8,64,512]{2,1,0:T(8,128)(2,1)S(1)} %pad_maximum_fusion.rest_0_), channel_id=1, source_target_pairs={{0,192},{1,65},{64,0},{65,129},{128,64},{129,193},{192,128},{193,1... | collective-permute-start | bytes 1572872 | tf_op jit(solution)/shard_map/ppermute | solution.py:48
  83.9 19.9 %collective-permute-start.19 = (bf16[8,64,512]{2,1,0:T(8,128)(2,1)S(1)}, bf16[8,64,512]{2,1,0:T(8,128)(2,1)S(1)}, u32[]{:S(2)}, u32[]{:S(2)}) collective-permute-start(bf16[8,64,512]{2,1,0:T(8,128)(2,1)S(1)} %collective-permute-done.18.rest_3_), channel_id=1, source_target_pairs={{0,64},{1,193},{64,128},{65,1},{128,192},{129,65},{192,0},{193,129... | collective-permute-start | bytes 1572872 | tf_op jit(solution)/shard_map/ppermute | solution.py:48
  84.0 5.7 %collective-permute-start.10 = (bf16[384,128]{1,0:T(8,128)(2,1)S(1)}, bf16[384,128]{1,0:T(8,128)(2,1)S(1)}, u32[]{:S(2)}, u32[]{:S(2)}) collective-permute-start(bf16[384,128]{1,0:T(8,128)(2,1)S(1)} %add_convert_fusion.7), channel_id=1, source_target_pairs={{0,8},{8,0},{1,9},{9,1},{2,10},{10,2},{3,11},{11,3},{4,12},{12,4},... | collective-permute-start | bytes 294920 | tf_op jit(solution)/shard_map/ppermute | solution.py:38
  84.2 22.7 %collective-permute-start.27 = (bf16[1,384,512]{2,1,0:T(8,128)(2,1)S(1)}, bf16[1,384,512]{2,1,0:T(8,128)(2,1)S(1)}, u32[]{:S(2)}, u32[]{:S(2)}) collective-permute-start(bf16[1,384,512]{2,1,0:T(8,128)(2,1)S(1)} %add_convert_fusion.4), channel_id=1, source_target_pairs={{0,8},{8,0},{1,9},{9,1},{2,10},{10,2},{3,11},{11,3},{4,12},{12,4},... | collective-permute-start | bytes 1179656 | tf_op jit(solution)/shard_map/ppermute | solution.py:38
  86.4 20.5 %collective-permute-start.23 = (bf16[1,384,512]{2,1,0:T(8,128)(2,1)S(1)}, bf16[1,384,512]{2,1,0:T(8,128)(2,1)S(1)}, u32[]{:S(2)}, u32[]{:S(2)}) collective-permute-start(bf16[1,384,512]{2,1,0:T(8,128)(2,1)S(1)} %add_convert_fusion.5), channel_id=1, source_target_pairs={{0,8},{8,0},{1,9},{9,1},{2,10},{10,2},{3,11},{11,3},{4,12},{12,4},... | collective-permute-start | bytes 1179656 | tf_op jit(solution)/shard_map/ppermute | solution.py:38
  89.7 7.4 %collective-permute-start.11 = (bf16[384,128]{1,0:T(8,128)(2,1)S(1)}, bf16[384,128]{1,0:T(8,128)(2,1)S(1)}, u32[]{:S(2)}, u32[]{:S(2)}) collective-permute-start(bf16[384,128]{1,0:T(8,128)(2,1)S(1)} %add_convert_fusion.6.s0), channel_id=1, source_target_pairs={{0,2},{1,7},{2,4},{3,1},{4,6},{5,3},{6,0},{7,5},{8,10},{9,15},{10,... | collective-permute-start | bytes 294920 | tf_op jit(solution)/shard_map/ppermute | solution.py:48
  96.2 5.0 %collective-permute-start.12 = (bf16[384,128]{1,0:T(8,128)(2,1)S(1)}, bf16[384,128]{1,0:T(8,128)(2,1)S(1)}, u32[]{:S(2)}, u32[]{:S(2)}) collective-permute-start(bf16[384,128]{1,0:T(8,128)(2,1)S(1)} %add_convert_fusion.6.s0), channel_id=1, source_target_pairs={{0,6},{1,3},{2,0},{3,5},{4,2},{5,7},{6,4},{7,1},{8,14},{9,11},{10,... | collective-permute-start | bytes 294920 | tf_op jit(solution)/shard_map/ppermute | solution.py:48
  97.1 6.7 %collective-permute-start.13 = (bf16[384,128]{1,0:T(8,128)(2,1)S(1)}, bf16[384,128]{1,0:T(8,128)(2,1)S(1)}, u32[]{:S(2)}, u32[]{:S(2)}) collective-permute-start(bf16[384,128]{1,0:T(8,128)(2,1)S(1)} %add_convert_fusion.6.s0), channel_id=1, source_target_pairs={{0,4},{1,5},{2,6},{3,7},{4,0},{5,1},{6,2},{7,3},{8,12},{9,13},{10,... | collective-permute-start | bytes 294920 | tf_op jit(solution)/shard_map/ppermute | solution.py:48

commit v3 on v2

--- a/solution.py
+++ b/solution.py
@@ -36,6 +36,11 @@
 def shift(value, axis, step):
     size = SIZES[AXES.index(axis)]
     return lax.ppermute(value, axis, [(i, (i + step) % size) for i in range(size)])
+
+
+def swap(value, axis, bit):
+    size = SIZES[AXES.index(axis)]
+    return lax.ppermute(value, axis, [(i, i ^ bit) for i in range(size)])
 
 
 def turn(value, axis, step):
@@ -211,7 +216,7 @@
         ).astype(BF16)
 
 
-def expand_kernel(slot_ref, adapter_ref, place_ref, count_ref, s0, s1, s2, s3, *rest):
+def expand_kernel(slot_ref, adapter_ref, place_ref, count_ref, s0, s1, *rest):
     buffers, out_ref, held, sems = rest[:4], rest[4], rest[5], rest[6]
     tiles = adapter_ref.shape[0]
     fetch(tiles, slot_ref, adapter_ref, place_ref, buffers, held, sems)
@@ -220,9 +225,7 @@
         wait_for(t, buffers, held, sems)
         wait_for(t + 1, buffers, held, sems)
         at = pl.ds(t * TILE // 2, TILE)
-        total = (
-            s0[at].astype(F32) + s1[at].astype(F32) + s2[at].astype(F32) + s3[at].astype(F32)
-        )
+        total = s0[at].astype(F32) + s1[at].astype(F32)
         factors = held[t * TILE : (t + 2) * TILE]
         for k in range(2):
             shrink = jnp.where(left == (k == 0), total, 0.0).astype(BF16)
@@ -255,12 +258,6 @@
     return turn(mine, axis, 1), turn(mine, axis, -1)
 
 
-def gather_round(mine, axis):
-    behind = turn(mine, axis, 1)
-    across = turn(behind, axis, 1)
-    return mine, turn(across, axis, 1), across, behind
-
-
 def gather_all(mine, pair, axis, *deps):
     behind, ahead = pair
     return mine, ahead, turn(after(behind, *deps), axis, 1), behind
@@ -305,27 +302,26 @@
 
     far = product(far_w, 0, [(0, 0, first), (0, first, second)])
     near_w = shift(after(near_w, far_w, other), "c", 1)
-    got1, got2 = turn(far[0], "y", 1), turn(far[1], "y", 1)
-
     near = product(
         after(near_w, far[0]),
         2,
         [(k, start, size) for k in (0, 2, 4) for start, size in ((0, first), (first, second))],
     )
-    got1 = turn(plus(near[0], got1), "y", 1)
-    got2 = turn(plus(near[1], got2), "y", 1)
-
-    down_line = lax.optimization_barrier((*down_line, near[0]))[:4]
+
+    behind = turn(after(expand_factors, far[0]), "zh", 1)
+    down_line = lax.optimization_barrier((*down_line, near[0], behind))[:4]
     down_line = jnp.concatenate(down_line, axis=0)
     down_pair = gather_near(down_line, "x")
     down = gather_all(down_line, down_pair, "x")
-    up_mine = after(expand_factors, down_line)
-    up_line = gather_round(up_mine, "zh")
-    up_line = after(jnp.concatenate(up_line, axis=0), *down_pair)
-    up = gather_all(up_line, gather_near(up_line, "x"), "x")
-
-    got1 = turn(plus(near[2], got1), "y", 1)
-    got2 = turn(plus(near[3], got2), "y", 1)
+
+    got1 = turn(far[0], "y", 1)
+    got2 = turn(after(far[1], near[0]), "y", 1)
+    got1 = turn(plus(near[0], got1), "y", 1)
+    across = turn(after(behind, near[0]), "zh", 1)
+    got2 = turn(plus(after(near[1], across), got2), "y", 1)
+    ahead = turn(across, "zh", 1)
+    got1 = turn(plus(after(near[2], ahead, *down_pair), got1), "y", 1)
+    got2 = turn(plus(after(near[3], down[2]), got2), "y", 1)
 
     scalars = (adapter_slot, tile_adapter, meta)
     shrink = with_factors(
@@ -338,9 +334,14 @@
         tiles,
         "shrink",
     )
+    up_line = jnp.concatenate([expand_factors, ahead, across, behind], axis=0)
+    up_line = after(up_line, down[2])
+    up = gather_all(up_line, gather_near(up_line, "x"), "x", got1)
+
     shrink = plus(shrink, shift(shrink, "c", 1))
     shrink = plus(shrink, shift(shrink, "zl", 1))
-    terms = (shrink, turn(shrink, "y", 1), turn(shrink, "y", -1), turn(shrink, "y", 2))
+    shrink = plus(shrink, swap(shrink, "y", 1))
+    terms = (shrink, swap(shrink, "y", 2))
 
     side1 = shift(plus(near[4][1:], got1[1:]), "zl", 1)
     side2 = shift(plus(near[5][1:], got2[1:]), "zl", 1)

time: 110 us -> 101 us (0.918); the launches traced: 108 us -> 101 us
  waiting for transfers between devices: 39.9 us -> 29.2 us
  starting transfers between devices: 39.9 us -> 43.6 us
    ppermute x21 -> x18, waiting for transfers between devices: 35.5 us -> 23.8 us  [turn(): return lax.ppermute(value, (axis, 'c'), pairs)]
    ppermute x0 -> x2, starting transfers between devices: none -> 4.29 us  [swap(): return lax.ppermute(value, axis, [(i, i ^ bit) for i in range(size)])]
    ppermute x0 -> x2, waiting for transfers between devices: none -> 3.9 us  [swap(): return lax.ppermute(value, axis, [(i, i ^ bit) for i in range(size)])]
    ppermute x21 -> x18, starting transfers between devices: 36.8 us -> 33.4 us  [turn(): return lax.ppermute(value, (axis, 'c'), pairs)]
    ppermute x7, waiting for transfers between devices: 4.43 us -> 1.48 us  [shift(): lax.ppermute(value, axis, [(i, (i + step) % size) for i in range(size)])]
    ppermute x7, starting transfers between devices: 3.11 us -> 5.83 us  [shift(): lax.ppermute(value, axis, [(i, (i + step) % size) for i in range(size)])]
  transfers between devices with their start and end apart: 28 -> 27, of which waited for: 10 -> 8; matrix products, arithmetic and copies ran while one was open for 1% -> 1% of each run, Pallas kernels for 18% -> 19%
where the time goes in v3:
time: 101 us
  starting transfers between devices  43.6 us (43%)
  waiting for transfers between devices  29.2 us (29%)
  Pallas kernels  22 us (22%)
  local copies, waits for them, and re-layouts  4.85 us (5%)
  other arithmetic  1.19 us (1%)
    ppermute x18, starting transfers between devices, turn(): return lax.ppermute(value, (axis, 'c'), pairs)  33.4 us
    ppermute x18, waiting for transfers between devices, turn(): return lax.ppermute(value, (axis, 'c'), pairs)  23.8 us
    pallas_call x2, Pallas kernels, partials(): pl.pallas_call(functools.partial(partial_kernel, MINE + skip, outputs), o...  11.3 us
    pallas_call x2, Pallas kernels, with_factors(): pl.pallas_call(kernel, out_shape=shape, in_specs=[pl.BlockSpec(memory_spa...  6.41 us
    ppermute x7, starting transfers between devices, shift(): lax.ppermute(value, axis, [(i, (i + step) % size) for i in range(size)])  5.83 us
    ppermute x2, starting transfers between devices, swap(): return lax.ppermute(value, axis, [(i, i ^ bit) for i in range(size)])  4.29 us
    unnamed x25, local copies, waits for them, and re-layouts  4.15 us
    ppermute x2, waiting for transfers between devices, swap(): return lax.ppermute(value, axis, [(i, i ^ bit) for i in range(size)])  3.9 us
  transfers between devices with their start and end apart: 27, of which 8 were waited for; matrix products, arithmetic and copies ran while one was open for 1% of the time, Pallas kernels for 19%

profile of v3, /device:TPU:8, one launch (start us, length us, event | category | flops | bytes accessed | tf_op | source)
XLA Modules:
  0.0 101.0 jit_solution(1934054337404383465)
XLA Ops:
  0.0 0.7 dynamic-slice_bitcast_fusion.meta_ref.place_ref
  0.7 3.4 %copy-done = bf16[512,8192]{1,0:T(8,128)(2,1)S(1)} copy-done((bf16[512,8192]{1,0:T(8,128)(2,1)S(1)}, bf16[512,8192]{1,0:T(8,128)(2,1)}, u32[]{:S(2)}) %copy-start) | copy-done | bytes 8388632
  4.1 0.7 copy-done.2
  4.8 1.0 %stage.3 = bf16[2,512,512]{2,1,0:T(8,128)(2,1)S(1)} custom-call(s32[19]{0:T(128)S(1)} %dynamic-slice_bitcast_fusion.meta_ref.place_ref, f32[4,64]{1,0:T(4,128)S(1)} %copy-done.2, bf16[512,8192]{1,0:T(8,128)(2,1)S(1)} %copy-done), custom_call_target="tpu_custom_call" | custom-call | bytes 2097152 | tf_op jit(solution)/shard_map/stage/pallas_call | solution.py:101
  5.9 0.5 collective-permute-start.3
  6.4 2.0 %stage.2 = bf16[6,512,512]{2,1,0:T(8,128)(2,1)S(1)} custom-call(s32[19]{0:T(128)S(1)} %dynamic-slice_bitcast_fusion.meta_ref.place_ref, f32[4,64]{1,0:T(4,128)S(1)} %copy-done.2, bf16[512,8192]{1,0:T(8,128)(2,1)S(1)} %copy-done), custom_call_target="tpu_custom_call" | custom-call | bytes 6291456 | tf_op jit(solution)/shard_map/stage/pallas_call | solution.py:101
  8.4 1.3 %collective-permute-done.3.xs_ref = bf16[768,512]{1,0:T(8,128)(2,1)S(1)} collective-permute-done((bf16[768,512]{1,0:T(8,128)(2,1)S(1)}, bf16[768,512]{1,0:T(8,128)(2,1)S(1)}, u32[]{:S(2)}, u32[]{:S(2)}) %collective-permute-start.3) | collective-permute-done | bytes 786464 | tf_op jit(solution)/shard_map/ppermute | solution.py:38
  9.7 0.1 collective-permute-start.5
  9.9 3.3 %partials.2 = (bf16[2,384,512]{2,1,0:T(8,128)(2,1)S(1)}, bf16[2,384,512]{2,1,0:T(8,128)(2,1)S(1)}) custom-call(s32[19]{0:T(128)S(1)} %dynamic-slice_bitcast_fusion.meta_ref.place_ref, bf16[768,512]{1,0:T(8,128)(2,1)S(1)} %copy-done.1, bf16[768,512]{1,0:T(8,128)(2,1)S(1)} %collective-permute-done.3.xs_ref, bf16[512,8192]{1,0:T(8,128)(2,1)S(1)} %bitcast.4, ...), custom_call_target="tpu_custom_call" | custom-call | flops 1610612736 | bytes 3670016 | tf_op jit(solution)/shard_map/partials/pallas_call | solution.py:143
  13.2 1.7 %collective-permute-start.18 = (bf16[2,384,512]{2,1,0:T(8,128)(2,1)S(1)}, bf16[2,384,512]{2,1,0:T(8,128)(2,1)S(1)}, u32[]{:S(2)}, u32[]{:S(2)}) collective-permute-start(bf16[2,384,512]{2,1,0:T(8,128)(2,1)S(1)} %get-tuple-element.28), channel_id=1, source_target_pairs={{0,2},{1,7},{2,4},{3,1},{4,6},{5,3},{6,0},{7,5},{8,10},{9,15},{10,... | collective-permute-start | bytes 2359304 | tf_op jit(solution)/shard_map/ppermute | solution.py:53
  14.9 6.3 %collective-permute-start = (bf16[2,64,512]{2,1,0:T(8,128)(2,1)S(1)}, bf16[2,64,512]{2,1,0:T(8,128)(2,1)S(1)}, u32[]{:S(2)}, u32[]{:S(2)}) collective-permute-start(bf16[2,64,512]{2,1,0:T(8,128)(2,1)S(1)} %bitcast.5), channel_id=1, source_target_pairs={{0,48},{1,17},{16,0},{17,33},{32,16},{33,49},{48,32},{49,1},{2,50}... | collective-permute-start | bytes 393224 | tf_op jit(solution)/shard_map/ppermute | solution.py:53
  21.2 0.9 collective-permute-start.1
  22.0 2.9 %collective-permute-start.2 = (bf16[2,64,512]{2,1,0:T(8,128)(2,1)S(1)}, bf16[2,64,512]{2,1,0:T(8,128)(2,1)S(1)}, u32[]{:S(2)}, u32[]{:S(2)}) collective-permute-start(bf16[2,64,512]{2,1,0:T(8,128)(2,1)S(1)} %bitcast.7), channel_id=1, source_target_pairs={{0,16},{1,49},{16,32},{17,1},{32,48},{33,17},{48,0},{49,33},{2,18}... | collective-permute-start | bytes 393224 | tf_op jit(solution)/shard_map/ppermute | solution.py:53
  25.0 2.7 %collective-permute-start.6 = (bf16[2,64,512]{2,1,0:T(8,128)(2,1)S(1)}, bf16[2,64,512]{2,1,0:T(8,128)(2,1)S(1)}, u32[]{:S(2)}, u32[]{:S(2)}) collective-permute-start(bf16[2,64,512]{2,1,0:T(8,128)(2,1)S(1)} %copy-done.8), channel_id=1, source_target_pairs={{0,16},{1,49},{16,32},{17,1},{32,48},{33,17},{48,0},{49,33},{2,18}... | collective-permute-start | bytes 393224 | tf_op jit(solution)/shard_map/ppermute | solution.py:53
  27.7 8.0 %partials.3 = (bf16[2,384,512]{2,1,0:T(8,128)(2,1)S(1)}, bf16[2,384,512]{2,1,0:T(8,128)(2,1)S(1)}, bf16[2,384,512]{2,1,0:T(8,128)(2,1)S(1)}, bf16[2,384,512]{2,1...) custom-call(s32[19]{0:T(128)S(1)} %dynamic-slice_bitcast_fusion.meta_ref.place_ref, ...), custom_call_target="tpu_custom_call" | custom-call | flops 4831838208 | bytes 11010048 | tf_op jit(solution)/shard_map/partials/pallas_call | solution.py:143
  35.7 1.4 %collective-permute-start.23 = (bf16[2,384,512]{2,1,0:T(8,128)(2,1)S(1)}, bf16[2,384,512]{2,1,0:T(8,128)(2,1)S(1)}, u32[]{:S(2)}, u32[]{:S(2)}) collective-permute-start(bf16[2,384,512]{2,1,0:T(8,128)(2,1)S(1)} %get-tuple-element.48), channel_id=1, source_target_pairs={{0,2},{1,7},{2,4},{3,1},{4,6},{5,3},{6,0},{7,5},{8,10},{9,15},{10,... | collective-permute-start | bytes 2359304 | tf_op jit(solution)/shard_map/ppermute | solution.py:53
  37.0 0.2 collective-permute-start.14
  37.2 0.2 add_convert_fusion.3
  37.4 0.3 collective-permute-start.19
  37.8 1.6 %collective-permute-start.8 = (bf16[8,64,512]{2,1,0:T(8,128)(2,1)S(1)}, bf16[8,64,512]{2,1,0:T(8,128)(2,1)S(1)}, u32[]{:S(2)}, u32[]{:S(2)}) collective-permute-start(bf16[8,64,512]{2,1,0:T(8,128)(2,1)S(1)} %constant_dynamic-update-slice_fusion.rest_0_), channel_id=1, source_target_pairs={{0,64},{1,193},{64,128},{65,1},{128,192},{129,65},{192,0},{193,129... | collective-permute-start | bytes 1572872 | tf_op jit(solution)/shard_map/ppermute | solution.py:53
  39.4 1.7 %collective-permute-start.7 = (bf16[8,64,512]{2,1,0:T(8,128)(2,1)S(1)}, bf16[8,64,512]{2,1,0:T(8,128)(2,1)S(1)}, u32[]{:S(2)}, u32[]{:S(2)}) collective-permute-start(bf16[8,64,512]{2,1,0:T(8,128)(2,1)S(1)} %constant_dynamic-update-slice_fusion.rest_0_), channel_id=1, source_target_pairs={{0,192},{1,65},{64,0},{65,129},{128,64},{129,193},{192,128},{193,1... | collective-permute-start | bytes 1572872 | tf_op jit(solution)/shard_map/ppermute | solution.py:53
  41.1 3.2 %collective-permute-done.14 = bf16[2,64,512]{2,1,0:T(8,128)(2,1)S(1)} collective-permute-done((bf16[2,64,512]{2,1,0:T(8,128)(2,1)S(1)}, bf16[2,64,512]{2,1,0:T(8,128)(2,1)S(1)}, u32[]{:S(2)}, u32[]{:S(2)}) %collective-permute-start.14) | collective-permute-done | bytes 131104 | tf_op jit(solution)/shard_map/ppermute | solution.py:53
  44.3 3.4 %collective-permute-done.23 = bf16[2,384,512]{2,1,0:T(8,128)(2,1)S(1)} collective-permute-done((bf16[2,384,512]{2,1,0:T(8,128)(2,1)S(1)}, bf16[2,384,512]{2,1,0:T(8,128)(2,1)S(1)}, u32[]{:S(2)}, u32[]{:S(2)}) %collective-permute-start.23) | collective-permute-done | bytes 786464 | tf_op jit(solution)/shard_map/ppermute | solution.py:53
  47.7 0.2 add_convert_fusion.1
  48.0 1.4 %collective-permute-start.24 = (bf16[2,384,512]{2,1,0:T(8,128)(2,1)S(1)}, bf16[2,384,512]{2,1,0:T(8,128)(2,1)S(1)}, u32[]{:S(2)}, u32[]{:S(2)}) collective-permute-start(bf16[2,384,512]{2,1,0:T(8,128)(2,1)S(1)} %add_convert_fusion.1), channel_id=1, source_target_pairs={{0,2},{1,7},{2,4},{3,1},{4,6},{5,3},{6,0},{7,5},{8,10},{9,15},{10,... | collective-permute-start | bytes 2359304 | tf_op jit(solution)/shard_map/ppermute | solution.py:53
  49.3 1.5 %collective-permute-start.9 = (bf16[8,64,512]{2,1,0:T(8,128)(2,1)S(1)}, bf16[8,64,512]{2,1,0:T(8,128)(2,1)S(1)}, u32[]{:S(2)}, u32[]{:S(2)}) collective-permute-start(bf16[8,64,512]{2,1,0:T(8,128)(2,1)S(1)} %collective-permute-done.8.rest_3_), channel_id=1, source_target_pairs={{0,64},{1,193},{64,128},{65,1},{128,192},{129,65},{192,0},{193,129... | collective-permute-start | bytes 1572872 | tf_op jit(solution)/shard_map/ppermute | solution.py:53
  50.8 6.4 %collective-permute-start.15 = (bf16[2,64,512]{2,1,0:T(8,128)(2,1)S(1)}, bf16[2,64,512]{2,1,0:T(8,128)(2,1)S(1)}, u32[]{:S(2)}, u32[]{:S(2)}) collective-permute-start(bf16[2,64,512]{2,1,0:T(8,128)(2,1)S(1)} %collective-permute-done.14), channel_id=1, source_target_pairs={{0,16},{1,49},{16,32},{17,1},{32,48},{33,17},{48,0},{49,33},{2,18}... | collective-permute-start | bytes 393224 | tf_op jit(solution)/shard_map/ppermute | solution.py:53
  57.2 5.3 %collective-permute-done.15 = bf16[2,64,512]{2,1,0:T(8,128)(2,1)S(1)} collective-permute-done((bf16[2,64,512]{2,1,0:T(8,128)(2,1)S(1)}, bf16[2,64,512]{2,1,0:T(8,128)(2,1)S(1)}, u32[]{:S(2)}, u32[]{:S(2)}) %collective-permute-start.15) | collective-permute-done | bytes 131104 | tf_op jit(solution)/shard_map/ppermute | solution.py:53
  62.5 0.2 add_convert_fusion.2
  62.8 3.3 %shrink.1 = bf16[384,128]{1,0:T(8,128)(2,1)S(1)} custom-call(s32[32]{0:T(128)S(1)} %copy-done.4, s32[12]{0:T(128)S(1)} %copy-done.5, s32[19]{0:T(128)S(1)} %dynamic-slice_bitcast_fusion.meta_ref.place_ref, bf16[768,512]{1,0:T(8,128)(2,1)S(1)} %copy-done.1, bf16[8,64,512]{2,1,0:T(8,128)(2,1)S(1)} %constant_dynamic-update-slice_fusion.rest_0_, ...), custom_call_target="tpu_custom_call" | custom-call | flops 50331648 | bytes 2359296 | tf_op jit(solution)/shard_map/shrink/pallas_call | solution.py:240
  66.1 1.1 %collective-permute-start.10 = (bf16[384,128]{1,0:T(8,128)(2,1)S(1)}, bf16[384,128]{1,0:T(8,128)(2,1)S(1)}, u32[]{:S(2)}, u32[]{:S(2)}) collective-permute-start(bf16[384,128]{1,0:T(8,128)(2,1)S(1)} %shrink.1), channel_id=1, source_target_pairs={{0,1},{1,0},{2,3},{3,2},{4,5},{5,4},{6,7},{7,6},{8,9},{9,8},{10,11... | collective-permute-start | bytes 294920 | tf_op jit(solution)/shard_map/ppermute | solution.py:38
  67.2 0.2 add_convert_fusion
  67.4 0.8 collective-permute-start.25
  68.3 2.5 %collective-permute-start.11 = (bf16[384,128]{1,0:T(8,128)(2,1)S(1)}, bf16[384,128]{1,0:T(8,128)(2,1)S(1)}, u32[]{:S(2)}, u32[]{:S(2)}) collective-permute-start(bf16[384,128]{1,0:T(8,128)(2,1)S(1)} %add_convert_fusion.8), channel_id=1, source_target_pairs={{0,8},{8,0},{1,9},{9,1},{2,10},{10,2},{3,11},{11,3},{4,12},{12,4},... | collective-permute-start | bytes 294920 | tf_op jit(solution)/shard_map/ppermute | solution.py:38
  70.8 2.0 %collective-permute-start.17 = (bf16[8,64,512]{2,1,0:T(8,128)(2,1)S(1)}, bf16[8,64,512]{2,1,0:T(8,128)(2,1)S(1)}, u32[]{:S(2)}, u32[]{:S(2)}) collective-permute-start(bf16[8,64,512]{2,1,0:T(8,128)(2,1)S(1)} %pad_maximum_fusion.rest_0_), channel_id=1, source_target_pairs={{0,64},{1,193},{64,128},{65,1},{128,192},{129,65},{192,0},{193,129... | collective-permute-start | bytes 1572872 | tf_op jit(solution)/shard_map/ppermute | solution.py:53
  72.8 1.3 %collective-permute-start.16 = (bf16[8,64,512]{2,1,0:T(8,128)(2,1)S(1)}, bf16[8,64,512]{2,1,0:T(8,128)(2,1)S(1)}, u32[]{:S(2)}, u32[]{:S(2)}) collective-permute-start(bf16[8,64,512]{2,1,0:T(8,128)(2,1)S(1)} %pad_maximum_fusion.rest_0_), channel_id=1, source_target_pairs={{0,192},{1,65},{64,0},{65,129},{128,64},{129,193},{192,128},{193,1... | collective-permute-start | bytes 1572872 | tf_op jit(solution)/shard_map/ppermute | solution.py:53
  74.1 0.2 collective-permute-done.11
  74.4 1.7 %collective-permute-start.12 = (bf16[384,128]{1,0:T(8,128)(2,1)S(1)}, bf16[384,128]{1,0:T(8,128)(2,1)S(1)}, u32[]{:S(2)}, u32[]{:S(2)}) collective-permute-start(bf16[384,128]{1,0:T(8,128)(2,1)S(1)} %add_convert_fusion.7), channel_id=1, source_target_pairs={{0,2},{2,0},{4,6},{6,4},{1,3},{3,1},{5,7},{7,5},{8,10},{10,8},{12,... | collective-permute-start | bytes 294920 | tf_op jit(solution)/shard_map/ppermute | solution.py:43
  76.1 0.1 add_convert_fusion.5
  76.2 0.8 collective-permute-start.22
  77.0 9.3 %collective-permute-done.17.rest_3_ = bf16[8,64,512]{2,1,0:T(8,128)(2,1)S(1)} collective-permute-done((bf16[8,64,512]{2,1,0:T(8,128)(2,1)S(1)}, bf16[8,64,512]{2,1,0:T(8,128)(2,1)S(1)}, u32[]{:S(2)}, u32[]{:S(2)}) %collective-permute-start.17) | collective-permute-done | bytes 524320 | tf_op jit(solution)/shard_map/ppermute | solution.py:53
  86.3 0.4 collective-permute-start.21
  86.8 0.8 collective-permute-start.26
  87.6 2.6 %collective-permute-start.13 = (bf16[384,128]{1,0:T(8,128)(2,1)S(1)}, bf16[384,128]{1,0:T(8,128)(2,1)S(1)}, u32[]{:S(2)}, u32[]{:S(2)}) collective-permute-start(bf16[384,128]{1,0:T(8,128)(2,1)S(1)} %add_convert_fusion.6.s0), channel_id=1, source_target_pairs={{0,4},{2,6},{4,0},{6,2},{1,5},{3,7},{5,1},{7,3},{8,12},{10,14},{12... | collective-permute-start | bytes 294920 | tf_op jit(solution)/shard_map/ppermute | solution.py:43
  90.2 3.9 %collective-permute-done.13.s1 = bf16[384,128]{1,0:T(8,128)(2,1)S(1)} collective-permute-done((bf16[384,128]{1,0:T(8,128)(2,1)S(1)}, bf16[384,128]{1,0:T(8,128)(2,1)S(1)}, u32[]{:S(2)}, u32[]{:S(2)}) %collective-permute-start.13) | collective-permute-done | bytes 98336 | tf_op jit(solution)/shard_map/ppermute | solution.py:43
  94.1 2.6 %collective-permute-done.21.rest_2_ = bf16[8,64,512]{2,1,0:T(8,128)(2,1)S(1)} collective-permute-done((bf16[8,64,512]{2,1,0:T(8,128)(2,1)S(1)}, bf16[8,64,512]{2,1,0:T(8,128)(2,1)S(1)}, u32[]{:S(2)}, u32[]{:S(2)}) %collective-permute-start.21) | collective-permute-done | bytes 524320 | tf_op jit(solution)/shard_map/ppermute | solution.py:53
  96.7 3.1 %expand.1.delta_ref = f32[768,512]{1,0:T(8,128)S(1)} custom-call(s32[32]{0:T(128)S(1)} %copy-done.4, s32[12]{0:T(128)S(1)} %copy-done.5, s32[19]{0:T(128)S(1)} %dynamic-slice_bitcast_fusion.meta_ref.place_ref, s32[12]{0:T(128)S(1)} %copy-done.6, bf16[384,128]{1,0:T(8,128)(2,1)S(1)} %add_convert_fusion.6.s0, bf16[384,128]{1,0:T(8,128)(2,1)S(1)} %collective-permute-done.13.s1, ...), custom_call_target="tpu_custom_call" | custom-call | flops 50331648 | bytes 2359296 | tf_op jit(solution)/shard_map/expand/pallas_call | solution.py:240
  99.8 1.2 %finish.1 = bf16[768,512]{1,0:T(8,128)(2,1)} custom-call(f32[768,512]{1,0:T(8,128)S(1)} %expand.1.delta_ref, bf16[2,384,512]{2,1,0:T(8,128)(2,1)S(1)} %get-tuple-element.41.rest_0_, bf16[2,384,512]{2,1,0:T(8,128)(2,1)S(1)} %collective-permute-done.20.rest_1_, bf16[1,384,512]{2,1,0:T(8,128)(2,1)S(1)} %collective-permute-done.22.rest_2_, ...), custom_call_target="tpu_custom_call" | custom-call | bytes 5505024 | tf_op jit(solution)/shard_map/finish/pallas_call | solution.py:368
  (51 shorter events, 0.6 us)
Async XLA Ops:
  0.7 3.4 %copy-start = (bf16[512,8192]{1,0:T(8,128)(2,1)S(1)}, bf16[512,8192]{1,0:T(8,128)(2,1)}, u32[]{:S(2)}) copy-start(bf16[512,8192]{1,0:T(8,128)(2,1)} %w_ref.7) | copy-start | bytes 25165828
  4.1 0.7 copy-start.2
  4.8 1.2 %copy-start.1 = (bf16[768,512]{1,0:T(8,128)(2,1)S(1)}, bf16[768,512]{1,0:T(8,128)(2,1)}, u32[]{:S(2)}) copy-start(bf16[768,512]{1,0:T(8,128)(2,1)} %x_ref.5) | copy-start | bytes 2359300
  4.8 5.1 %slice-start = ((s8[8388608]{0:T(1024)(128)(4,1)}), s8[4194304]{0:T(1024)(128)(4,1)S(1)}, s32[]{:S(2)}) async-start(s8[8388608]{0:T(1024)(128)(4,1)} %bitcast.3), calls=%async_computation | async-start | bytes 8388608
  5.8 4.0 %slice-start.1 = ((s8[8388608]{0:T(1024)(128)(4,1)}), s8[4194304]{0:T(1024)(128)(4,1)S(1)}, s32[]{:S(2)}) async-start(s8[8388608]{0:T(1024)(128)(4,1)} %bitcast.3), calls=%async_computation.1 | async-start | bytes 8388608
  5.8 4.0 %copy-start.3 = (f32[4,64]{1,0:T(4,128)S(1)}, f32[4,64]{1,0:T(4,128)}, u32[]{:S(2)}) copy-start(f32[4,64]{1,0:T(4,128)} %s_ref.3) | copy-start | bytes 3076
  5.8 3.9 %collective-permute-start.4 = (bf16[2,512,512]{2,1,0:T(8,128)(2,1)S(1)}, bf16[2,512,512]{2,1,0:T(8,128)(2,1)S(1)}, u32[]{:S(2)}, u32[]{:S(2)}) collective-permute-start(bf16[2,512,512]{2,1,0:T(8,128)(2,1)S(1)} %stage.3), channel_id=1, source_target_pairs={{0,1},{1,0},{2,3},{3,2},{4,5},{5,4},{6,7},{7,6},{8,9},{9,8},{10,11... | collective-permute-start | bytes 3145736 | tf_op jit(solution)/shard_map/ppermute | solution.py:38
  5.9 3.8 %collective-permute-start.3 = (bf16[768,512]{1,0:T(8,128)(2,1)S(1)}, bf16[768,512]{1,0:T(8,128)(2,1)S(1)}, u32[]{:S(2)}, u32[]{:S(2)}) collective-permute-start(bf16[768,512]{1,0:T(8,128)(2,1)S(1)} %copy-done.1), channel_id=1, source_target_pairs={{0,1},{1,0},{2,3},{3,2},{4,5},{5,4},{6,7},{7,6},{8,9},{9,8},{10,11... | collective-permute-start | bytes 2359304 | tf_op jit(solution)/shard_map/ppermute | solution.py:38
  8.4 6.4 %copy-start.7 = (bf16[2,512,64]{1,2,0:T(8,128)(2,1)S(1)}, bf16[2,512,64]{1,2,0:T(8,128)(2,1)}, u32[]{:S(2)}) copy-start(bf16[2,512,64]{1,2,0:T(8,128)(2,1)} %param.12) | copy-start | bytes 393220
  8.4 16.5 %copy-start.8 = (bf16[2,64,512]{2,1,0:T(8,128)(2,1)S(1)}, bf16[2,64,512]{2,1,0:T(8,128)(2,1)}, u32[]{:S(2)}) copy-start(bf16[2,64,512]{2,1,0:T(8,128)(2,1)} %param.13) | copy-start | bytes 393220
  9.7 15.3 %collective-permute-start.5 = (bf16[6,512,512]{2,1,0:T(8,128)(2,1)S(1)}, bf16[6,512,512]{2,1,0:T(8,128)(2,1)S(1)}, u32[]{:S(2)}, u32[]{:S(2)}) collective-permute-start(bf16[6,512,512]{2,1,0:T(8,128)(2,1)S(1)} %stage.2), channel_id=1, source_target_pairs={{0,1},{1,0},{2,3},{3,2},{4,5},{5,4},{6,7},{7,6},{8,9},{9,8},{10,11... | collective-permute-start | bytes 9437192 | tf_op jit(solution)/shard_map/ppermute | solution.py:38
  13.2 24.0 %collective-permute-start.18 = (bf16[2,384,512]{2,1,0:T(8,128)(2,1)S(1)}, bf16[2,384,512]{2,1,0:T(8,128)(2,1)S(1)}, u32[]{:S(2)}, u32[]{:S(2)}) collective-permute-start(bf16[2,384,512]{2,1,0:T(8,128)(2,1)S(1)} %get-tuple-element.28), channel_id=1, source_target_pairs={{0,2},{1,7},{2,4},{3,1},{4,6},{5,3},{6,0},{7,5},{8,10},{9,15},{10,... | collective-permute-start | bytes 2359304 | tf_op jit(solution)/shard_map/ppermute | solution.py:53
  14.9 20.8 %collective-permute-start = (bf16[2,64,512]{2,1,0:T(8,128)(2,1)S(1)}, bf16[2,64,512]{2,1,0:T(8,128)(2,1)S(1)}, u32[]{:S(2)}, u32[]{:S(2)}) collective-permute-start(bf16[2,64,512]{2,1,0:T(8,128)(2,1)S(1)} %bitcast.5), channel_id=1, source_target_pairs={{0,48},{1,17},{16,0},{17,33},{32,16},{33,49},{48,32},{49,1},{2,50}... | collective-permute-start | bytes 393224 | tf_op jit(solution)/shard_map/ppermute | solution.py:53
  21.2 15.9 %collective-permute-start.1 = (bf16[2,64,512]{2,1,0:T(8,128)(2,1)S(1)}, bf16[2,64,512]{2,1,0:T(8,128)(2,1)S(1)}, u32[]{:S(2)}, u32[]{:S(2)}) collective-permute-start(bf16[2,64,512]{2,1,0:T(8,128)(2,1)S(1)} %bitcast.6), channel_id=1, source_target_pairs={{0,32},{1,33},{16,48},{17,49},{32,0},{33,1},{48,16},{49,17},{2,34}... | collective-permute-start | bytes 393224 | tf_op jit(solution)/shard_map/ppermute | solution.py:53
  22.0 15.0 %collective-permute-start.2 = (bf16[2,64,512]{2,1,0:T(8,128)(2,1)S(1)}, bf16[2,64,512]{2,1,0:T(8,128)(2,1)S(1)}, u32[]{:S(2)}, u32[]{:S(2)}) collective-permute-start(bf16[2,64,512]{2,1,0:T(8,128)(2,1)S(1)} %bitcast.7), channel_id=1, source_target_pairs={{0,16},{1,49},{16,32},{17,1},{32,48},{33,17},{48,0},{49,33},{2,18}... | collective-permute-start | bytes 393224 | tf_op jit(solution)/shard_map/ppermute | solution.py:53
  25.0 12.1 %collective-permute-start.6 = (bf16[2,64,512]{2,1,0:T(8,128)(2,1)S(1)}, bf16[2,64,512]{2,1,0:T(8,128)(2,1)S(1)}, u32[]{:S(2)}, u32[]{:S(2)}) collective-permute-start(bf16[2,64,512]{2,1,0:T(8,128)(2,1)S(1)} %copy-done.8), channel_id=1, source_target_pairs={{0,16},{1,49},{16,32},{17,1},{32,48},{33,17},{48,0},{49,33},{2,18}... | collective-permute-start | bytes 393224 | tf_op jit(solution)/shard_map/ppermute | solution.py:53
  35.7 12.1 %collective-permute-start.23 = (bf16[2,384,512]{2,1,0:T(8,128)(2,1)S(1)}, bf16[2,384,512]{2,1,0:T(8,128)(2,1)S(1)}, u32[]{:S(2)}, u32[]{:S(2)}) collective-permute-start(bf16[2,384,512]{2,1,0:T(8,128)(2,1)S(1)} %get-tuple-element.48), channel_id=1, source_target_pairs={{0,2},{1,7},{2,4},{3,1},{4,6},{5,3},{6,0},{7,5},{8,10},{9,15},{10,... | collective-permute-start | bytes 2359304 | tf_op jit(solution)/shard_map/ppermute | solution.py:53
  37.0 7.3 %collective-permute-start.14 = (bf16[2,64,512]{2,1,0:T(8,128)(2,1)S(1)}, bf16[2,64,512]{2,1,0:T(8,128)(2,1)S(1)}, u32[]{:S(2)}, u32[]{:S(2)}) collective-permute-start(bf16[2,64,512]{2,1,0:T(8,128)(2,1)S(1)} %collective-permute-done.6), channel_id=1, source_target_pairs={{0,16},{1,49},{16,32},{17,1},{32,48},{33,17},{48,0},{49,33},{2,18}... | collective-permute-start | bytes 393224 | tf_op jit(solution)/shard_map/ppermute | solution.py:53
  37.4 25.1 %collective-permute-start.19 = (bf16[2,384,512]{2,1,0:T(8,128)(2,1)S(1)}, bf16[2,384,512]{2,1,0:T(8,128)(2,1)S(1)}, u32[]{:S(2)}, u32[]{:S(2)}) collective-permute-start(bf16[2,384,512]{2,1,0:T(8,128)(2,1)S(1)} %add_convert_fusion.3), channel_id=1, source_target_pairs={{0,2},{1,7},{2,4},{3,1},{4,6},{5,3},{6,0},{7,5},{8,10},{9,15},{10,... | collective-permute-start | bytes 2359304 | tf_op jit(solution)/shard_map/ppermute | solution.py:53
  37.8 11.5 %collective-permute-start.8 = (bf16[8,64,512]{2,1,0:T(8,128)(2,1)S(1)}, bf16[8,64,512]{2,1,0:T(8,128)(2,1)S(1)}, u32[]{:S(2)}, u32[]{:S(2)}) collective-permute-start(bf16[8,64,512]{2,1,0:T(8,128)(2,1)S(1)} %constant_dynamic-update-slice_fusion.rest_0_), channel_id=1, source_target_pairs={{0,64},{1,193},{64,128},{65,1},{128,192},{129,65},{192,0},{193,129... | collective-permute-start | bytes 1572872 | tf_op jit(solution)/shard_map/ppermute | solution.py:53
  39.4 23.1 %collective-permute-start.7 = (bf16[8,64,512]{2,1,0:T(8,128)(2,1)S(1)}, bf16[8,64,512]{2,1,0:T(8,128)(2,1)S(1)}, u32[]{:S(2)}, u32[]{:S(2)}) collective-permute-start(bf16[8,64,512]{2,1,0:T(8,128)(2,1)S(1)} %constant_dynamic-update-slice_fusion.rest_0_), channel_id=1, source_target_pairs={{0,192},{1,65},{64,0},{65,129},{128,64},{129,193},{192,128},{193,1... | collective-permute-start | bytes 1572872 | tf_op jit(solution)/shard_map/ppermute | solution.py:53
  47.9 14.9 %copy-start.4 = (s32[32]{0:T(128)S(1)}, s32[32]{0:T(128)}, u32[]{:S(2)}) copy-start(s32[32]{0:T(128)} %slot_ref.3) | copy-start | bytes 388
  47.9 14.9 %copy-start.5 = (s32[12]{0:T(128)S(1)}, s32[12]{0:T(128)}, u32[]{:S(2)}) copy-start(s32[12]{0:T(128)} %adapter_ref.3) | copy-start | bytes 148
  48.0 19.3 %collective-permute-start.24 = (bf16[2,384,512]{2,1,0:T(8,128)(2,1)S(1)}, bf16[2,384,512]{2,1,0:T(8,128)(2,1)S(1)}, u32[]{:S(2)}, u32[]{:S(2)}) collective-permute-start(bf16[2,384,512]{2,1,0:T(8,128)(2,1)S(1)} %add_convert_fusion.1), channel_id=1, source_target_pairs={{0,2},{1,7},{2,4},{3,1},{4,6},{5,3},{6,0},{7,5},{8,10},{9,15},{10,... | collective-permute-start | bytes 2359304 | tf_op jit(solution)/shard_map/ppermute | solution.py:53
  49.3 13.5 %collective-permute-start.9 = (bf16[8,64,512]{2,1,0:T(8,128)(2,1)S(1)}, bf16[8,64,512]{2,1,0:T(8,128)(2,1)S(1)}, u32[]{:S(2)}, u32[]{:S(2)}) collective-permute-start(bf16[8,64,512]{2,1,0:T(8,128)(2,1)S(1)} %collective-permute-done.8.rest_3_), channel_id=1, source_target_pairs={{0,64},{1,193},{64,128},{65,1},{128,192},{129,65},{192,0},{193,129... | collective-permute-start | bytes 1572872 | tf_op jit(solution)/shard_map/ppermute | solution.py:53
  50.8 11.7 %collective-permute-start.15 = (bf16[2,64,512]{2,1,0:T(8,128)(2,1)S(1)}, bf16[2,64,512]{2,1,0:T(8,128)(2,1)S(1)}, u32[]{:S(2)}, u32[]{:S(2)}) collective-permute-start(bf16[2,64,512]{2,1,0:T(8,128)(2,1)S(1)} %collective-permute-done.14), channel_id=1, source_target_pairs={{0,16},{1,49},{16,32},{17,1},{32,48},{33,17},{48,0},{49,33},{2,18}... | collective-permute-start | bytes 393224 | tf_op jit(solution)/shard_map/ppermute | solution.py:53
  62.7 13.4 %collective-permute-start.20 = (bf16[2,384,512]{2,1,0:T(8,128)(2,1)S(1)}, bf16[2,384,512]{2,1,0:T(8,128)(2,1)S(1)}, u32[]{:S(2)}, u32[]{:S(2)}) collective-permute-start(bf16[2,384,512]{2,1,0:T(8,128)(2,1)S(1)} %add_convert_fusion.2), channel_id=1, source_target_pairs={{0,2},{1,7},{2,4},{3,1},{4,6},{5,3},{6,0},{7,5},{8,10},{9,15},{10,... | collective-permute-start | bytes 2359304 | tf_op jit(solution)/shard_map/ppermute | solution.py:53
  66.1 2.1 %collective-permute-start.10 = (bf16[384,128]{1,0:T(8,128)(2,1)S(1)}, bf16[384,128]{1,0:T(8,128)(2,1)S(1)}, u32[]{:S(2)}, u32[]{:S(2)}) collective-permute-start(bf16[384,128]{1,0:T(8,128)(2,1)S(1)} %shrink.1), channel_id=1, source_target_pairs={{0,1},{1,0},{2,3},{3,2},{4,5},{5,4},{6,7},{7,6},{8,9},{9,8},{10,11... | collective-permute-start | bytes 294920 | tf_op jit(solution)/shard_map/ppermute | solution.py:38
  67.4 19.2 %collective-permute-start.25 = (bf16[2,384,512]{2,1,0:T(8,128)(2,1)S(1)}, bf16[2,384,512]{2,1,0:T(8,128)(2,1)S(1)}, u32[]{:S(2)}, u32[]{:S(2)}) collective-permute-start(bf16[2,384,512]{2,1,0:T(8,128)(2,1)S(1)} %add_convert_fusion), channel_id=1, source_target_pairs={{0,2},{1,7},{2,4},{3,1},{4,6},{5,3},{6,0},{7,5},{8,10},{9,15},{10,... | collective-permute-start | bytes 2359304 | tf_op jit(solution)/shard_map/ppermute | solution.py:53
  68.3 6.1 %collective-permute-start.11 = (bf16[384,128]{1,0:T(8,128)(2,1)S(1)}, bf16[384,128]{1,0:T(8,128)(2,1)S(1)}, u32[]{:S(2)}, u32[]{:S(2)}) collective-permute-start(bf16[384,128]{1,0:T(8,128)(2,1)S(1)} %add_convert_fusion.8), channel_id=1, source_target_pairs={{0,8},{8,0},{1,9},{9,1},{2,10},{10,2},{3,11},{11,3},{4,12},{12,4},... | collective-permute-start | bytes 294920 | tf_op jit(solution)/shard_map/ppermute | solution.py:38
  70.8 25.9 %copy-start.6 = (s32[12]{0:T(128)S(1)}, s32[12]{0:T(128)}, u32[]{:S(2)}) copy-start(s32[12]{0:T(128)} %count_ref.1) | copy-start | bytes 148
  70.8 15.5 %collective-permute-start.17 = (bf16[8,64,512]{2,1,0:T(8,128)(2,1)S(1)}, bf16[8,64,512]{2,1,0:T(8,128)(2,1)S(1)}, u32[]{:S(2)}, u32[]{:S(2)}) collective-permute-start(bf16[8,64,512]{2,1,0:T(8,128)(2,1)S(1)} %pad_maximum_fusion.rest_0_), channel_id=1, source_target_pairs={{0,64},{1,193},{64,128},{65,1},{128,192},{129,65},{192,0},{193,129... | collective-permute-start | bytes 1572872 | tf_op jit(solution)/shard_map/ppermute | solution.py:53
  72.8 21.3 %collective-permute-start.16 = (bf16[8,64,512]{2,1,0:T(8,128)(2,1)S(1)}, bf16[8,64,512]{2,1,0:T(8,128)(2,1)S(1)}, u32[]{:S(2)}, u32[]{:S(2)}) collective-permute-start(bf16[8,64,512]{2,1,0:T(8,128)(2,1)S(1)} %pad_maximum_fusion.rest_0_), channel_id=1, source_target_pairs={{0,192},{1,65},{64,0},{65,129},{128,64},{129,193},{192,128},{193,1... | collective-permute-start | bytes 1572872 | tf_op jit(solution)/shard_map/ppermute | solution.py:53
  74.4 13.2 %collective-permute-start.12 = (bf16[384,128]{1,0:T(8,128)(2,1)S(1)}, bf16[384,128]{1,0:T(8,128)(2,1)S(1)}, u32[]{:S(2)}, u32[]{:S(2)}) collective-permute-start(bf16[384,128]{1,0:T(8,128)(2,1)S(1)} %add_convert_fusion.7), channel_id=1, source_target_pairs={{0,2},{2,0},{4,6},{6,4},{1,3},{3,1},{5,7},{7,5},{8,10},{10,8},{12,... | collective-permute-start | bytes 294920 | tf_op jit(solution)/shard_map/ppermute | solution.py:43
  76.2 23.6 %collective-permute-start.22 = (bf16[1,384,512]{2,1,0:T(8,128)(2,1)S(1)}, bf16[1,384,512]{2,1,0:T(8,128)(2,1)S(1)}, u32[]{:S(2)}, u32[]{:S(2)}) collective-permute-start(bf16[1,384,512]{2,1,0:T(8,128)(2,1)S(1)} %add_convert_fusion.5), channel_id=1, source_target_pairs={{0,8},{8,0},{1,9},{9,1},{2,10},{10,2},{3,11},{11,3},{4,12},{12,4},... | collective-permute-start | bytes 1179656 | tf_op jit(solution)/shard_map/ppermute | solution.py:38
  86.3 10.4 %collective-permute-start.21 = (bf16[8,64,512]{2,1,0:T(8,128)(2,1)S(1)}, bf16[8,64,512]{2,1,0:T(8,128)(2,1)S(1)}, u32[]{:S(2)}, u32[]{:S(2)}) collective-permute-start(bf16[8,64,512]{2,1,0:T(8,128)(2,1)S(1)} %collective-permute-done.17.rest_3_), channel_id=1, source_target_pairs={{0,64},{1,193},{64,128},{65,1},{128,192},{129,65},{192,0},{193,129... | collective-permute-start | bytes 1572872 | tf_op jit(solution)/shard_map/ppermute | solution.py:53
  86.8 13.0 %collective-permute-start.26 = (bf16[1,384,512]{2,1,0:T(8,128)(2,1)S(1)}, bf16[1,384,512]{2,1,0:T(8,128)(2,1)S(1)}, u32[]{:S(2)}, u32[]{:S(2)}) collective-permute-start(bf16[1,384,512]{2,1,0:T(8,128)(2,1)S(1)} %add_convert_fusion.4), channel_id=1, source_target_pairs={{0,8},{8,0},{1,9},{9,1},{2,10},{10,2},{3,11},{11,3},{4,12},{12,4},... | collective-permute-start | bytes 1179656 | tf_op jit(solution)/shard_map/ppermute | solution.py:38
  87.6 6.5 %collective-permute-start.13 = (bf16[384,128]{1,0:T(8,128)(2,1)S(1)}, bf16[384,128]{1,0:T(8,128)(2,1)S(1)}, u32[]{:S(2)}, u32[]{:S(2)}) collective-permute-start(bf16[384,128]{1,0:T(8,128)(2,1)S(1)} %add_convert_fusion.6.s0), channel_id=1, source_target_pairs={{0,4},{2,6},{4,0},{6,2},{1,5},{3,7},{5,1},{7,3},{8,12},{10,14},{12... | collective-permute-start | bytes 294920 | tf_op jit(solution)/shard_map/ppermute | solution.py:43

commit v4 on v3

--- a/solution.py
+++ b/solution.py
@@ -16,7 +16,7 @@
 F32 = jnp.float32
 BF16 = jnp.bfloat16
 
-CHUNKS = (384, 384)
+CHUNKS = (416, 352)
 
 ORDER = [(dz, e) for e in (3, 2, 1, 0) for dz in (0, 1)]
 MINE, THEIRS, PLACE = 0, 8, 16
@@ -294,13 +294,13 @@
     near_w = stage(base_values, base_scales, meta, 2, 6, width)
 
     down_mine = jnp.swapaxes(shrink_factors, 1, 2)
+    def product(weights, skip, outputs):
+        return partials(tokens, other, base_values, weights, base_scales, meta, skip, outputs)
+
+    far = product(far_w, 0, [(0, 0, first), (0, first, second)])
+    down_mine = after(down_mine, far[0])
     behind, ahead = gather_near(down_mine, "zh")
     down_line = (down_mine, ahead, turn(down_mine, "zh", 2), behind)
-
-    def product(weights, skip, outputs):
-        return partials(tokens, other, base_values, weights, base_scales, meta, skip, outputs)
-
-    far = product(far_w, 0, [(0, 0, first), (0, first, second)])
     near_w = shift(after(near_w, far_w, other), "c", 1)
     near = product(
         after(near_w, far[0]),
@@ -312,16 +312,15 @@
     down_line = lax.optimization_barrier((*down_line, near[0], behind))[:4]
     down_line = jnp.concatenate(down_line, axis=0)
     down_pair = gather_near(down_line, "x")
+
+    first1 = turn(far[0], "y", 1)
+    first2 = turn(far[1], "y", 1)
+    mid1 = turn(plus(near[0], first1), "y", 1)
+    across = turn(behind, "zh", 1)
+    mid2 = turn(plus(after(near[1], across, *down_pair), first2), "y", 1)
+    ahead = turn(after(across, *down_pair), "zh", 1)
     down = gather_all(down_line, down_pair, "x")
-
-    got1 = turn(far[0], "y", 1)
-    got2 = turn(after(far[1], near[0]), "y", 1)
-    got1 = turn(plus(near[0], got1), "y", 1)
-    across = turn(after(behind, near[0]), "zh", 1)
-    got2 = turn(plus(after(near[1], across), got2), "y", 1)
-    ahead = turn(across, "zh", 1)
-    got1 = turn(plus(after(near[2], ahead, *down_pair), got1), "y", 1)
-    got2 = turn(plus(after(near[3], down[2]), got2), "y", 1)
+    got1 = turn(plus(near[2], mid1), "y", 1)
 
     scalars = (adapter_slot, tile_adapter, meta)
     shrink = with_factors(
@@ -335,13 +334,18 @@
         "shrink",
     )
     up_line = jnp.concatenate([expand_factors, ahead, across, behind], axis=0)
-    up_line = after(up_line, down[2])
-    up = gather_all(up_line, gather_near(up_line, "x"), "x", got1)
+    up_line = after(up_line, shrink)
+    up_pair = [turn(up_line, "x", 1), 0]
+    up_pair[1] = turn(up_line, "x", -1)
+    up = gather_all(up_line, up_pair, "x", got1)
+    got2 = turn(plus(near[3], mid2), "y", 1)
 
     shrink = plus(shrink, shift(shrink, "c", 1))
     shrink = plus(shrink, shift(shrink, "zl", 1))
+    zsum = shrink
     shrink = plus(shrink, swap(shrink, "y", 1))
     terms = (shrink, swap(shrink, "y", 2))
+    ysum = shrink
 
     side1 = shift(plus(near[4][1:], got1[1:]), "zl", 1)
     side2 = shift(plus(near[5][1:], got2[1:]), "zl", 1)

time: 101 us -> 98.7 us (0.977)
  starting transfers between devices: 43.6 us -> 36.1 us
  waiting for transfers between devices: 29.2 us -> 33.6 us
    ppermute x18, starting transfers between devices: 33.4 us -> 28.6 us  [turn(): return lax.ppermute(value, (axis, 'c'), pairs)]
    ppermute x18, waiting for transfers between devices: 23.8 us -> 26.6 us  [turn(): return lax.ppermute(value, (axis, 'c'), pairs)]
    ppermute x7, starting transfers between devices: 5.83 us -> 4.26 us  [shift(): lax.ppermute(value, axis, [(i, (i + step) % size) for i in range(size)])]
    ppermute x2, starting transfers between devices: 4.29 us -> 3.18 us  [swap(): return lax.ppermute(value, axis, [(i, i ^ bit) for i in range(size)])]
  transfers between devices with their start and end apart: 27 -> 27, of which waited for: 8 -> 9; matrix products, arithmetic and copies ran while one was open for 1% -> 1% of each run, Pallas kernels for 19% -> 20%
where the time goes in v4:
time: 98.7 us; the launch traced here: 98 us
  starting transfers between devices  36.1 us (37%)
  waiting for transfers between devices  33.6 us (34%)
  Pallas kernels  21.9 us (22%)
  local copies, waits for them, and re-layouts  4.85 us (5%)
  other arithmetic  1.2 us (1%)
    ppermute x18, starting transfers between devices, turn(): return lax.ppermute(value, (axis, 'c'), pairs)  28.6 us
    ppermute x18, waiting for transfers between devices, turn(): return lax.ppermute(value, (axis, 'c'), pairs)  26.6 us
    pallas_call x2, Pallas kernels, partials(): pl.pallas_call(functools.partial(partial_kernel, MINE + skip, outputs), o...  11.3 us
    pallas_call x2, Pallas kernels, with_factors(): pl.pallas_call(kernel, out_shape=shape, in_specs=[pl.BlockSpec(memory_spa...  6.41 us
    ppermute x2, waiting for transfers between devices, swap(): return lax.ppermute(value, axis, [(i, i ^ bit) for i in range(size)])  4.84 us
    ppermute x7, starting transfers between devices, shift(): lax.ppermute(value, axis, [(i, (i + step) % size) for i in range(size)])  4.26 us
    unnamed x25, local copies, waits for them, and re-layouts  4.15 us
    ppermute x2, starting transfers between devices, swap(): return lax.ppermute(value, axis, [(i, i ^ bit) for i in range(size)])  3.18 us
  transfers between devices with their start and end apart: 27, of which 9 were waited for; matrix products, arithmetic and copies ran while one was open for 1% of the time, Pallas kernels for 20%

profile of v4, /device:TPU:8, one launch (start us, length us, event | category | flops | bytes accessed | tf_op | source)
XLA Modules:
  0.0 98.0 jit_solution(11170875060065909255)
XLA Ops:
  0.0 0.7 dynamic-slice_bitcast_fusion.meta_ref.place_ref
  0.7 3.4 %copy-done = bf16[512,8192]{1,0:T(8,128)(2,1)S(1)} copy-done((bf16[512,8192]{1,0:T(8,128)(2,1)S(1)}, bf16[512,8192]{1,0:T(8,128)(2,1)}, u32[]{:S(2)}) %copy-start) | copy-done | bytes 8388632
  4.1 0.7 copy-done.2
  4.8 1.0 %stage.2 = bf16[2,512,512]{2,1,0:T(8,128)(2,1)S(1)} custom-call(s32[19]{0:T(128)S(1)} %dynamic-slice_bitcast_fusion.meta_ref.place_ref, f32[4,64]{1,0:T(4,128)S(1)} %copy-done.2, bf16[512,8192]{1,0:T(8,128)(2,1)S(1)} %copy-done), custom_call_target="tpu_custom_call" | custom-call | bytes 2097152 | tf_op jit(solution)/shard_map/stage/pallas_call | solution.py:101
  5.9 0.5 collective-permute-start
  6.4 2.0 %stage.3 = bf16[6,512,512]{2,1,0:T(8,128)(2,1)S(1)} custom-call(s32[19]{0:T(128)S(1)} %dynamic-slice_bitcast_fusion.meta_ref.place_ref, f32[4,64]{1,0:T(4,128)S(1)} %copy-done.2, bf16[512,8192]{1,0:T(8,128)(2,1)S(1)} %copy-done), custom_call_target="tpu_custom_call" | custom-call | bytes 6291456 | tf_op jit(solution)/shard_map/stage/pallas_call | solution.py:101
  8.4 1.3 %collective-permute-done.xs_ref = bf16[768,512]{1,0:T(8,128)(2,1)S(1)} collective-permute-done((bf16[768,512]{1,0:T(8,128)(2,1)S(1)}, bf16[768,512]{1,0:T(8,128)(2,1)S(1)}, u32[]{:S(2)}, u32[]{:S(2)}) %collective-permute-start) | collective-permute-done | bytes 786464 | tf_op jit(solution)/shard_map/ppermute | solution.py:38
  9.7 0.1 collective-permute-start.5
  9.9 3.3 %partials.2 = (bf16[2,416,512]{2,1,0:T(8,128)(2,1)S(1)}, bf16[2,352,512]{2,1,0:T(8,128)(2,1)S(1)}) custom-call(s32[19]{0:T(128)S(1)} %dynamic-slice_bitcast_fusion.meta_ref.place_ref, bf16[768,512]{1,0:T(8,128)(2,1)S(1)} %copy-done.1, bf16[768,512]{1,0:T(8,128)(2,1)S(1)} %collective-permute-done.xs_ref, bf16[512,8192]{1,0:T(8,128)(2,1)S(1)} %bitcast.4, ...), custom_call_target="tpu_custom_call" | custom-call | flops 1610612736 | bytes 3670016 | tf_op jit(solution)/shard_map/partials/pallas_call | solution.py:143
  13.2 6.4 %collective-permute-start.2 = (bf16[2,64,512]{2,1,0:T(8,128)(2,1)S(1)}, bf16[2,64,512]{2,1,0:T(8,128)(2,1)S(1)}, u32[]{:S(2)}, u32[]{:S(2)}) collective-permute-start(bf16[2,64,512]{2,1,0:T(8,128)(2,1)S(1)} %bitcast.5), channel_id=1, source_target_pairs={{0,48},{1,17},{16,0},{17,33},{32,16},{33,49},{48,32},{49,1},{2,50}... | collective-permute-start | bytes 393224 | tf_op jit(solution)/shard_map/ppermute | solution.py:53
  19.6 1.0 %collective-permute-start.3 = (bf16[2,64,512]{2,1,0:T(8,128)(2,1)S(1)}, bf16[2,64,512]{2,1,0:T(8,128)(2,1)S(1)}, u32[]{:S(2)}, u32[]{:S(2)}) collective-permute-start(bf16[2,64,512]{2,1,0:T(8,128)(2,1)S(1)} %bitcast.6), channel_id=1, source_target_pairs={{0,32},{1,33},{16,48},{17,49},{32,0},{33,1},{48,16},{49,17},{2,34}... | collective-permute-start | bytes 393224 | tf_op jit(solution)/shard_map/ppermute | solution.py:53
  20.6 2.8 %collective-permute-start.4 = (bf16[2,64,512]{2,1,0:T(8,128)(2,1)S(1)}, bf16[2,64,512]{2,1,0:T(8,128)(2,1)S(1)}, u32[]{:S(2)}, u32[]{:S(2)}) collective-permute-start(bf16[2,64,512]{2,1,0:T(8,128)(2,1)S(1)} %bitcast.7), channel_id=1, source_target_pairs={{0,16},{1,49},{16,32},{17,1},{32,48},{33,17},{48,0},{49,33},{2,18}... | collective-permute-start | bytes 393224 | tf_op jit(solution)/shard_map/ppermute | solution.py:53
  23.4 1.6 %collective-permute-start.18 = (bf16[2,416,512]{2,1,0:T(8,128)(2,1)S(1)}, bf16[2,416,512]{2,1,0:T(8,128)(2,1)S(1)}, u32[]{:S(2)}, u32[]{:S(2)}) collective-permute-start(bf16[2,416,512]{2,1,0:T(8,128)(2,1)S(1)} %get-tuple-element.25), channel_id=1, source_target_pairs={{0,2},{1,7},{2,4},{3,1},{4,6},{5,3},{6,0},{7,5},{8,10},{9,15},{10,... | collective-permute-start | bytes 2555912 | tf_op jit(solution)/shard_map/ppermute | solution.py:53
  25.0 2.7 %collective-permute-start.6 = (bf16[2,64,512]{2,1,0:T(8,128)(2,1)S(1)}, bf16[2,64,512]{2,1,0:T(8,128)(2,1)S(1)}, u32[]{:S(2)}, u32[]{:S(2)}) collective-permute-start(bf16[2,64,512]{2,1,0:T(8,128)(2,1)S(1)} %copy-done.8), channel_id=1, source_target_pairs={{0,16},{1,49},{16,32},{17,1},{32,48},{33,17},{48,0},{49,33},{2,18}... | collective-permute-start | bytes 393224 | tf_op jit(solution)/shard_map/ppermute | solution.py:53
  27.7 8.0 %partials.3 = (bf16[2,416,512]{2,1,0:T(8,128)(2,1)S(1)}, bf16[2,352,512]{2,1,0:T(8,128)(2,1)S(1)}, bf16[2,416,512]{2,1,0:T(8,128)(2,1)S(1)}, bf16[2,352,512]{2,1...) custom-call(s32[19]{0:T(128)S(1)} %dynamic-slice_bitcast_fusion.meta_ref.place_ref, ...), custom_call_target="tpu_custom_call" | custom-call | flops 4831838208 | bytes 11010048 | tf_op jit(solution)/shard_map/partials/pallas_call | solution.py:143
  35.6 1.4 %collective-permute-start.23 = (bf16[2,352,512]{2,1,0:T(8,128)(2,1)S(1)}, bf16[2,352,512]{2,1,0:T(8,128)(2,1)S(1)}, u32[]{:S(2)}, u32[]{:S(2)}) collective-permute-start(bf16[2,352,512]{2,1,0:T(8,128)(2,1)S(1)} %get-tuple-element.44), channel_id=1, source_target_pairs={{0,2},{1,7},{2,4},{3,1},{4,6},{5,3},{6,0},{7,5},{8,10},{9,15},{10,... | collective-permute-start | bytes 2162696 | tf_op jit(solution)/shard_map/ppermute | solution.py:53
  37.1 2.8 %collective-permute-start.7 = (bf16[8,64,512]{2,1,0:T(8,128)(2,1)S(1)}, bf16[8,64,512]{2,1,0:T(8,128)(2,1)S(1)}, u32[]{:S(2)}, u32[]{:S(2)}) collective-permute-start(bf16[8,64,512]{2,1,0:T(8,128)(2,1)S(1)} %constant_dynamic-update-slice_fusion.rest_0_), channel_id=1, source_target_pairs={{0,192},{1,65},{64,0},{65,129},{128,64},{129,193},{192,128},{193,1... | collective-permute-start | bytes 1572872 | tf_op jit(solution)/shard_map/ppermute | solution.py:53
  39.9 0.2 add_convert_fusion.1
  40.2 0.3 collective-permute-start.19
  40.5 0.2 collective-permute-start.14
  40.7 8.1 %collective-permute-done.14 = bf16[2,64,512]{2,1,0:T(8,128)(2,1)S(1)} collective-permute-done((bf16[2,64,512]{2,1,0:T(8,128)(2,1)S(1)}, bf16[2,64,512]{2,1,0:T(8,128)(2,1)S(1)}, u32[]{:S(2)}, u32[]{:S(2)}) %collective-permute-start.14) | collective-permute-done | bytes 131104 | tf_op jit(solution)/shard_map/ppermute | solution.py:53
  48.8 1.5 %collective-permute-done.7.rest_1_ = bf16[8,64,512]{2,1,0:T(8,128)(2,1)S(1)} collective-permute-done((bf16[8,64,512]{2,1,0:T(8,128)(2,1)S(1)}, bf16[8,64,512]{2,1,0:T(8,128)(2,1)S(1)}, u32[]{:S(2)}, u32[]{:S(2)}) %collective-permute-start.7) | collective-permute-done | bytes 524320 | tf_op jit(solution)/shard_map/ppermute | solution.py:53
  50.3 0.2 add_convert_fusion.3
  50.5 1.3 %collective-permute-start.24 = (bf16[2,352,512]{2,1,0:T(8,128)(2,1)S(1)}, bf16[2,352,512]{2,1,0:T(8,128)(2,1)S(1)}, u32[]{:S(2)}, u32[]{:S(2)}) collective-permute-start(bf16[2,352,512]{2,1,0:T(8,128)(2,1)S(1)} %add_convert_fusion.3), channel_id=1, source_target_pairs={{0,2},{1,7},{2,4},{3,1},{4,6},{5,3},{6,0},{7,5},{8,10},{9,15},{10,... | collective-permute-start | bytes 2162696 | tf_op jit(solution)/shard_map/ppermute | solution.py:53
  51.9 1.5 %collective-permute-start.9 = (bf16[8,64,512]{2,1,0:T(8,128)(2,1)S(1)}, bf16[8,64,512]{2,1,0:T(8,128)(2,1)S(1)}, u32[]{:S(2)}, u32[]{:S(2)}) collective-permute-start(bf16[8,64,512]{2,1,0:T(8,128)(2,1)S(1)} %collective-permute-done.8.rest_3_), channel_id=1, source_target_pairs={{0,64},{1,193},{64,128},{65,1},{128,192},{129,65},{192,0},{193,129... | collective-permute-start | bytes 1572872 | tf_op jit(solution)/shard_map/ppermute | solution.py:53
  53.4 0.6 collective-permute-start.15
  54.0 2.1 %collective-permute-done.19 = bf16[2,416,512]{2,1,0:T(8,128)(2,1)S(1)} collective-permute-done((bf16[2,416,512]{2,1,0:T(8,128)(2,1)S(1)}, bf16[2,416,512]{2,1,0:T(8,128)(2,1)S(1)}, u32[]{:S(2)}, u32[]{:S(2)}) %collective-permute-start.19) | collective-permute-done | bytes 852000 | tf_op jit(solution)/shard_map/ppermute | solution.py:53
  56.1 0.2 add_convert_fusion
  56.4 1.4 %collective-permute-start.20 = (bf16[2,416,512]{2,1,0:T(8,128)(2,1)S(1)}, bf16[2,416,512]{2,1,0:T(8,128)(2,1)S(1)}, u32[]{:S(2)}, u32[]{:S(2)}) collective-permute-start(bf16[2,416,512]{2,1,0:T(8,128)(2,1)S(1)} %add_convert_fusion), channel_id=1, source_target_pairs={{0,2},{1,7},{2,4},{3,1},{4,6},{5,3},{6,0},{7,5},{8,10},{9,15},{10,... | collective-permute-start | bytes 2555912 | tf_op jit(solution)/shard_map/ppermute | solution.py:53
  57.7 4.6 %collective-permute-done.9.rest_2_ = bf16[8,64,512]{2,1,0:T(8,128)(2,1)S(1)} collective-permute-done((bf16[8,64,512]{2,1,0:T(8,128)(2,1)S(1)}, bf16[8,64,512]{2,1,0:T(8,128)(2,1)S(1)}, u32[]{:S(2)}, u32[]{:S(2)}) %collective-permute-start.9) | collective-permute-done | bytes 524320 | tf_op jit(solution)/shard_map/ppermute | solution.py:53
  62.3 3.3 %shrink.1 = bf16[384,128]{1,0:T(8,128)(2,1)S(1)} custom-call(s32[32]{0:T(128)S(1)} %copy-done.4, s32[12]{0:T(128)S(1)} %copy-done.5, s32[19]{0:T(128)S(1)} %dynamic-slice_bitcast_fusion.meta_ref.place_ref, bf16[768,512]{1,0:T(8,128)(2,1)S(1)} %copy-done.1, bf16[8,64,512]{2,1,0:T(8,128)(2,1)S(1)} %constant_dynamic-update-slice_fusion.rest_0_, ...), custom_call_target="tpu_custom_call" | custom-call | flops 50331648 | bytes 2359296 | tf_op jit(solution)/shard_map/shrink/pallas_call | solution.py:240
  65.7 0.2 add_convert_fusion.2
  65.9 1.4 %collective-permute-start.25 = (bf16[2,352,512]{2,1,0:T(8,128)(2,1)S(1)}, bf16[2,352,512]{2,1,0:T(8,128)(2,1)S(1)}, u32[]{:S(2)}, u32[]{:S(2)}) collective-permute-start(bf16[2,352,512]{2,1,0:T(8,128)(2,1)S(1)} %add_convert_fusion.2), channel_id=1, source_target_pairs={{0,2},{1,7},{2,4},{3,1},{4,6},{5,3},{6,0},{7,5},{8,10},{9,15},{10,... | collective-permute-start | bytes 2162696 | tf_op jit(solution)/shard_map/ppermute | solution.py:53
  67.3 0.3 collective-permute-start.11
  67.8 0.4 collective-permute-start.17
  68.2 2.9 %collective-permute-start.16 = (bf16[8,64,512]{2,1,0:T(8,128)(2,1)S(1)}, bf16[8,64,512]{2,1,0:T(8,128)(2,1)S(1)}, u32[]{:S(2)}, u32[]{:S(2)}) collective-permute-start(bf16[8,64,512]{2,1,0:T(8,128)(2,1)S(1)} %pad_maximum_fusion.rest_0_), channel_id=1, source_target_pairs={{0,192},{1,65},{64,0},{65,129},{128,64},{129,193},{192,128},{193,1... | collective-permute-start | bytes 1572872 | tf_op jit(solution)/shard_map/ppermute | solution.py:53
  71.1 1.0 collective-permute-done.11
  72.1 1.8 %collective-permute-start.12 = (bf16[384,128]{1,0:T(8,128)(2,1)S(1)}, bf16[384,128]{1,0:T(8,128)(2,1)S(1)}, u32[]{:S(2)}, u32[]{:S(2)}) collective-permute-start(bf16[384,128]{1,0:T(8,128)(2,1)S(1)} %add_convert_fusion.7), channel_id=1, source_target_pairs={{0,2},{2,0},{4,6},{6,4},{1,3},{3,1},{5,7},{7,5},{8,10},{10,8},{12,... | collective-permute-start | bytes 294920 | tf_op jit(solution)/shard_map/ppermute | solution.py:43
  73.9 0.1 add_convert_fusion.4
  74.0 0.7 collective-permute-start.22
  74.7 8.5 %collective-permute-done.17.rest_3_ = bf16[8,64,512]{2,1,0:T(8,128)(2,1)S(1)} collective-permute-done((bf16[8,64,512]{2,1,0:T(8,128)(2,1)S(1)}, bf16[8,64,512]{2,1,0:T(8,128)(2,1)S(1)}, u32[]{:S(2)}, u32[]{:S(2)}) %collective-permute-start.17) | collective-permute-done | bytes 524320 | tf_op jit(solution)/shard_map/ppermute | solution.py:53
  83.3 0.1 add_convert_fusion.5
  83.4 2.4 %collective-permute-start.26 = (bf16[1,352,512]{2,1,0:T(8,128)(2,1)S(1)}, bf16[1,352,512]{2,1,0:T(8,128)(2,1)S(1)}, u32[]{:S(2)}, u32[]{:S(2)}) collective-permute-start(bf16[1,352,512]{2,1,0:T(8,128)(2,1)S(1)} %add_convert_fusion.5), channel_id=1, source_target_pairs={{0,8},{8,0},{1,9},{9,1},{2,10},{10,2},{3,11},{11,3},{4,12},{12,4},... | collective-permute-start | bytes 1081352 | tf_op jit(solution)/shard_map/ppermute | solution.py:38
  85.8 1.4 %collective-permute-start.13 = (bf16[384,128]{1,0:T(8,128)(2,1)S(1)}, bf16[384,128]{1,0:T(8,128)(2,1)S(1)}, u32[]{:S(2)}, u32[]{:S(2)}) collective-permute-start(bf16[384,128]{1,0:T(8,128)(2,1)S(1)} %add_convert_fusion.6.s0), channel_id=1, source_target_pairs={{0,4},{2,6},{4,0},{6,2},{1,5},{3,7},{5,1},{7,3},{8,12},{10,14},{12... | collective-permute-start | bytes 294920 | tf_op jit(solution)/shard_map/ppermute | solution.py:43
  87.1 4.8 %collective-permute-done.13.s1 = bf16[384,128]{1,0:T(8,128)(2,1)S(1)} collective-permute-done((bf16[384,128]{1,0:T(8,128)(2,1)S(1)}, bf16[384,128]{1,0:T(8,128)(2,1)S(1)}, u32[]{:S(2)}, u32[]{:S(2)}) %collective-permute-start.13) | collective-permute-done | bytes 98336 | tf_op jit(solution)/shard_map/ppermute | solution.py:43
  92.0 1.7 %collective-permute-done.21.rest_2_ = bf16[8,64,512]{2,1,0:T(8,128)(2,1)S(1)} collective-permute-done((bf16[8,64,512]{2,1,0:T(8,128)(2,1)S(1)}, bf16[8,64,512]{2,1,0:T(8,128)(2,1)S(1)}, u32[]{:S(2)}, u32[]{:S(2)}) %collective-permute-start.21) | collective-permute-done | bytes 524320 | tf_op jit(solution)/shard_map/ppermute | solution.py:53
  93.6 3.1 %expand.1.delta_ref = f32[768,512]{1,0:T(8,128)S(1)} custom-call(s32[32]{0:T(128)S(1)} %copy-done.4, s32[12]{0:T(128)S(1)} %copy-done.5, s32[19]{0:T(128)S(1)} %dynamic-slice_bitcast_fusion.meta_ref.place_ref, s32[12]{0:T(128)S(1)} %copy-done.6, bf16[384,128]{1,0:T(8,128)(2,1)S(1)} %add_convert_fusion.6.s0, bf16[384,128]{1,0:T(8,128)(2,1)S(1)} %collective-permute-done.13.s1, ...), custom_call_target="tpu_custom_call" | custom-call | flops 50331648 | bytes 2359296 | tf_op jit(solution)/shard_map/expand/pallas_call | solution.py:240
  96.8 1.2 %finish.1 = bf16[768,512]{1,0:T(8,128)(2,1)} custom-call(f32[768,512]{1,0:T(8,128)S(1)} %expand.1.delta_ref, bf16[2,416,512]{2,1,0:T(8,128)(2,1)S(1)} %get-tuple-element.39.rest_0_, bf16[2,416,512]{2,1,0:T(8,128)(2,1)S(1)} %collective-permute-done.20.rest_1_, bf16[1,416,512]{2,1,0:T(8,128)(2,1)S(1)} %collective-permute-done.22.rest_2_, ...), custom_call_target="tpu_custom_call" | custom-call | bytes 5505024 | tf_op jit(solution)/shard_map/finish/pallas_call | solution.py:372
  (51 shorter events, 0.5 us)
Async XLA Ops:
  0.7 3.4 %copy-start = (bf16[512,8192]{1,0:T(8,128)(2,1)S(1)}, bf16[512,8192]{1,0:T(8,128)(2,1)}, u32[]{:S(2)}) copy-start(bf16[512,8192]{1,0:T(8,128)(2,1)} %w_ref.7) | copy-start | bytes 25165828
  4.1 0.7 copy-start.2
  4.8 1.2 %copy-start.1 = (bf16[768,512]{1,0:T(8,128)(2,1)S(1)}, bf16[768,512]{1,0:T(8,128)(2,1)}, u32[]{:S(2)}) copy-start(bf16[768,512]{1,0:T(8,128)(2,1)} %x_ref.5) | copy-start | bytes 2359300
  4.8 5.1 %slice-start = ((s8[8388608]{0:T(1024)(128)(4,1)}), s8[4194304]{0:T(1024)(128)(4,1)S(1)}, s32[]{:S(2)}) async-start(s8[8388608]{0:T(1024)(128)(4,1)} %bitcast.3), calls=%async_computation | async-start | bytes 8388608
  5.8 4.0 %slice-start.1 = ((s8[8388608]{0:T(1024)(128)(4,1)}), s8[4194304]{0:T(1024)(128)(4,1)S(1)}, s32[]{:S(2)}) async-start(s8[8388608]{0:T(1024)(128)(4,1)} %bitcast.3), calls=%async_computation.1 | async-start | bytes 8388608
  5.8 4.0 %copy-start.3 = (f32[4,64]{1,0:T(4,128)S(1)}, f32[4,64]{1,0:T(4,128)}, u32[]{:S(2)}) copy-start(f32[4,64]{1,0:T(4,128)} %s_ref.3) | copy-start | bytes 3076
  5.8 3.9 %collective-permute-start.1 = (bf16[2,512,512]{2,1,0:T(8,128)(2,1)S(1)}, bf16[2,512,512]{2,1,0:T(8,128)(2,1)S(1)}, u32[]{:S(2)}, u32[]{:S(2)}) collective-permute-start(bf16[2,512,512]{2,1,0:T(8,128)(2,1)S(1)} %stage.2), channel_id=1, source_target_pairs={{0,1},{1,0},{2,3},{3,2},{4,5},{5,4},{6,7},{7,6},{8,9},{9,8},{10,11... | collective-permute-start | bytes 3145736 | tf_op jit(solution)/shard_map/ppermute | solution.py:38
  5.9 3.8 %collective-permute-start = (bf16[768,512]{1,0:T(8,128)(2,1)S(1)}, bf16[768,512]{1,0:T(8,128)(2,1)S(1)}, u32[]{:S(2)}, u32[]{:S(2)}) collective-permute-start(bf16[768,512]{1,0:T(8,128)(2,1)S(1)} %copy-done.1), channel_id=1, source_target_pairs={{0,1},{1,0},{2,3},{3,2},{4,5},{5,4},{6,7},{7,6},{8,9},{9,8},{10,11... | collective-permute-start | bytes 2359304 | tf_op jit(solution)/shard_map/ppermute | solution.py:38
  8.4 4.8 %copy-start.7 = (bf16[2,512,64]{1,2,0:T(8,128)(2,1)S(1)}, bf16[2,512,64]{1,2,0:T(8,128)(2,1)}, u32[]{:S(2)}) copy-start(bf16[2,512,64]{1,2,0:T(8,128)(2,1)} %param.12) | copy-start | bytes 393220
  8.4 16.6 %copy-start.8 = (bf16[2,64,512]{2,1,0:T(8,128)(2,1)S(1)}, bf16[2,64,512]{2,1,0:T(8,128)(2,1)}, u32[]{:S(2)}) copy-start(bf16[2,64,512]{2,1,0:T(8,128)(2,1)} %param.13) | copy-start | bytes 393220
  9.7 15.3 %collective-permute-start.5 = (bf16[6,512,512]{2,1,0:T(8,128)(2,1)S(1)}, bf16[6,512,512]{2,1,0:T(8,128)(2,1)S(1)}, u32[]{:S(2)}, u32[]{:S(2)}) collective-permute-start(bf16[6,512,512]{2,1,0:T(8,128)(2,1)S(1)} %stage.3), channel_id=1, source_target_pairs={{0,1},{1,0},{2,3},{3,2},{4,5},{5,4},{6,7},{7,6},{8,9},{9,8},{10,11... | collective-permute-start | bytes 9437192 | tf_op jit(solution)/shard_map/ppermute | solution.py:38
  13.2 22.4 %collective-permute-start.2 = (bf16[2,64,512]{2,1,0:T(8,128)(2,1)S(1)}, bf16[2,64,512]{2,1,0:T(8,128)(2,1)S(1)}, u32[]{:S(2)}, u32[]{:S(2)}) collective-permute-start(bf16[2,64,512]{2,1,0:T(8,128)(2,1)S(1)} %bitcast.5), channel_id=1, source_target_pairs={{0,48},{1,17},{16,0},{17,33},{32,16},{33,49},{48,32},{49,1},{2,50}... | collective-permute-start | bytes 393224 | tf_op jit(solution)/shard_map/ppermute | solution.py:53
  19.6 17.4 %collective-permute-start.3 = (bf16[2,64,512]{2,1,0:T(8,128)(2,1)S(1)}, bf16[2,64,512]{2,1,0:T(8,128)(2,1)S(1)}, u32[]{:S(2)}, u32[]{:S(2)}) collective-permute-start(bf16[2,64,512]{2,1,0:T(8,128)(2,1)S(1)} %bitcast.6), channel_id=1, source_target_pairs={{0,32},{1,33},{16,48},{17,49},{32,0},{33,1},{48,16},{49,17},{2,34}... | collective-permute-start | bytes 393224 | tf_op jit(solution)/shard_map/ppermute | solution.py:53
  20.6 16.4 %collective-permute-start.4 = (bf16[2,64,512]{2,1,0:T(8,128)(2,1)S(1)}, bf16[2,64,512]{2,1,0:T(8,128)(2,1)S(1)}, u32[]{:S(2)}, u32[]{:S(2)}) collective-permute-start(bf16[2,64,512]{2,1,0:T(8,128)(2,1)S(1)} %bitcast.7), channel_id=1, source_target_pairs={{0,16},{1,49},{16,32},{17,1},{32,48},{33,17},{48,0},{49,33},{2,18}... | collective-permute-start | bytes 393224 | tf_op jit(solution)/shard_map/ppermute | solution.py:53
  23.4 16.5 %collective-permute-start.18 = (bf16[2,416,512]{2,1,0:T(8,128)(2,1)S(1)}, bf16[2,416,512]{2,1,0:T(8,128)(2,1)S(1)}, u32[]{:S(2)}, u32[]{:S(2)}) collective-permute-start(bf16[2,416,512]{2,1,0:T(8,128)(2,1)S(1)} %get-tuple-element.25), channel_id=1, source_target_pairs={{0,2},{1,7},{2,4},{3,1},{4,6},{5,3},{6,0},{7,5},{8,10},{9,15},{10,... | collective-permute-start | bytes 2555912 | tf_op jit(solution)/shard_map/ppermute | solution.py:53
  25.0 12.0 %collective-permute-start.6 = (bf16[2,64,512]{2,1,0:T(8,128)(2,1)S(1)}, bf16[2,64,512]{2,1,0:T(8,128)(2,1)S(1)}, u32[]{:S(2)}, u32[]{:S(2)}) collective-permute-start(bf16[2,64,512]{2,1,0:T(8,128)(2,1)S(1)} %copy-done.8), channel_id=1, source_target_pairs={{0,16},{1,49},{16,32},{17,1},{32,48},{33,17},{48,0},{49,33},{2,18}... | collective-permute-start | bytes 393224 | tf_op jit(solution)/shard_map/ppermute | solution.py:53
  35.6 14.7 %collective-permute-start.23 = (bf16[2,352,512]{2,1,0:T(8,128)(2,1)S(1)}, bf16[2,352,512]{2,1,0:T(8,128)(2,1)S(1)}, u32[]{:S(2)}, u32[]{:S(2)}) collective-permute-start(bf16[2,352,512]{2,1,0:T(8,128)(2,1)S(1)} %get-tuple-element.44), channel_id=1, source_target_pairs={{0,2},{1,7},{2,4},{3,1},{4,6},{5,3},{6,0},{7,5},{8,10},{9,15},{10,... | collective-permute-start | bytes 2162696 | tf_op jit(solution)/shard_map/ppermute | solution.py:53
  37.1 13.2 %collective-permute-start.7 = (bf16[8,64,512]{2,1,0:T(8,128)(2,1)S(1)}, bf16[8,64,512]{2,1,0:T(8,128)(2,1)S(1)}, u32[]{:S(2)}, u32[]{:S(2)}) collective-permute-start(bf16[8,64,512]{2,1,0:T(8,128)(2,1)S(1)} %constant_dynamic-update-slice_fusion.rest_0_), channel_id=1, source_target_pairs={{0,192},{1,65},{64,0},{65,129},{128,64},{129,193},{192,128},{193,1... | collective-permute-start | bytes 1572872 | tf_op jit(solution)/shard_map/ppermute | solution.py:53
  39.9 10.4 %collective-permute-start.8 = (bf16[8,64,512]{2,1,0:T(8,128)(2,1)S(1)}, bf16[8,64,512]{2,1,0:T(8,128)(2,1)S(1)}, u32[]{:S(2)}, u32[]{:S(2)}) collective-permute-start(bf16[8,64,512]{2,1,0:T(8,128)(2,1)S(1)} %constant_dynamic-update-slice_fusion.rest_0_), channel_id=1, source_target_pairs={{0,64},{1,193},{64,128},{65,1},{128,192},{129,65},{192,0},{193,129... | collective-permute-start | bytes 1572872 | tf_op jit(solution)/shard_map/ppermute | solution.py:53
  40.2 16.0 %collective-permute-start.19 = (bf16[2,416,512]{2,1,0:T(8,128)(2,1)S(1)}, bf16[2,416,512]{2,1,0:T(8,128)(2,1)S(1)}, u32[]{:S(2)}, u32[]{:S(2)}) collective-permute-start(bf16[2,416,512]{2,1,0:T(8,128)(2,1)S(1)} %add_convert_fusion.1), channel_id=1, source_target_pairs={{0,2},{1,7},{2,4},{3,1},{4,6},{5,3},{6,0},{7,5},{8,10},{9,15},{10,... | collective-permute-start | bytes 2555912 | tf_op jit(solution)/shard_map/ppermute | solution.py:53
  40.5 8.3 %collective-permute-start.14 = (bf16[2,64,512]{2,1,0:T(8,128)(2,1)S(1)}, bf16[2,64,512]{2,1,0:T(8,128)(2,1)S(1)}, u32[]{:S(2)}, u32[]{:S(2)}) collective-permute-start(bf16[2,64,512]{2,1,0:T(8,128)(2,1)S(1)} %collective-permute-done.6), channel_id=1, source_target_pairs={{0,16},{1,49},{16,32},{17,1},{32,48},{33,17},{48,0},{49,33},{2,18}... | collective-permute-start | bytes 393224 | tf_op jit(solution)/shard_map/ppermute | solution.py:53
  50.5 11.8 %copy-start.4 = (s32[32]{0:T(128)S(1)}, s32[32]{0:T(128)}, u32[]{:S(2)}) copy-start(s32[32]{0:T(128)} %slot_ref.3) | copy-start | bytes 388
  50.5 11.8 %copy-start.5 = (s32[12]{0:T(128)S(1)}, s32[12]{0:T(128)}, u32[]{:S(2)}) copy-start(s32[12]{0:T(128)} %adapter_ref.3) | copy-start | bytes 148
  50.5 15.2 %collective-permute-start.24 = (bf16[2,352,512]{2,1,0:T(8,128)(2,1)S(1)}, bf16[2,352,512]{2,1,0:T(8,128)(2,1)S(1)}, u32[]{:S(2)}, u32[]{:S(2)}) collective-permute-start(bf16[2,352,512]{2,1,0:T(8,128)(2,1)S(1)} %add_convert_fusion.3), channel_id=1, source_target_pairs={{0,2},{1,7},{2,4},{3,1},{4,6},{5,3},{6,0},{7,5},{8,10},{9,15},{10,... | collective-permute-start | bytes 2162696 | tf_op jit(solution)/shard_map/ppermute | solution.py:53
  51.9 10.4 %collective-permute-start.9 = (bf16[8,64,512]{2,1,0:T(8,128)(2,1)S(1)}, bf16[8,64,512]{2,1,0:T(8,128)(2,1)S(1)}, u32[]{:S(2)}, u32[]{:S(2)}) collective-permute-start(bf16[8,64,512]{2,1,0:T(8,128)(2,1)S(1)} %collective-permute-done.8.rest_3_), channel_id=1, source_target_pairs={{0,64},{1,193},{64,128},{65,1},{128,192},{129,65},{192,0},{193,129... | collective-permute-start | bytes 1572872 | tf_op jit(solution)/shard_map/ppermute | solution.py:53
  53.4 14.3 %collective-permute-start.15 = (bf16[2,64,512]{2,1,0:T(8,128)(2,1)S(1)}, bf16[2,64,512]{2,1,0:T(8,128)(2,1)S(1)}, u32[]{:S(2)}, u32[]{:S(2)}) collective-permute-start(bf16[2,64,512]{2,1,0:T(8,128)(2,1)S(1)} %collective-permute-done.14), channel_id=1, source_target_pairs={{0,16},{1,49},{16,32},{17,1},{32,48},{33,17},{48,0},{49,33},{2,18}... | collective-permute-start | bytes 393224 | tf_op jit(solution)/shard_map/ppermute | solution.py:53
  56.4 17.5 %collective-permute-start.20 = (bf16[2,416,512]{2,1,0:T(8,128)(2,1)S(1)}, bf16[2,416,512]{2,1,0:T(8,128)(2,1)S(1)}, u32[]{:S(2)}, u32[]{:S(2)}) collective-permute-start(bf16[2,416,512]{2,1,0:T(8,128)(2,1)S(1)} %add_convert_fusion), channel_id=1, source_target_pairs={{0,2},{1,7},{2,4},{3,1},{4,6},{5,3},{6,0},{7,5},{8,10},{9,15},{10,... | collective-permute-start | bytes 2555912 | tf_op jit(solution)/shard_map/ppermute | solution.py:53
  65.6 1.7 %collective-permute-start.10 = (bf16[384,128]{1,0:T(8,128)(2,1)S(1)}, bf16[384,128]{1,0:T(8,128)(2,1)S(1)}, u32[]{:S(2)}, u32[]{:S(2)}) collective-permute-start(bf16[384,128]{1,0:T(8,128)(2,1)S(1)} %shrink.1), channel_id=1, source_target_pairs={{0,1},{1,0},{2,3},{3,2},{4,5},{5,4},{6,7},{7,6},{8,9},{9,8},{10,11... | collective-permute-start | bytes 294920 | tf_op jit(solution)/shard_map/ppermute | solution.py:38
  65.9 17.3 %collective-permute-start.25 = (bf16[2,352,512]{2,1,0:T(8,128)(2,1)S(1)}, bf16[2,352,512]{2,1,0:T(8,128)(2,1)S(1)}, u32[]{:S(2)}, u32[]{:S(2)}) collective-permute-start(bf16[2,352,512]{2,1,0:T(8,128)(2,1)S(1)} %add_convert_fusion.2), channel_id=1, source_target_pairs={{0,2},{1,7},{2,4},{3,1},{4,6},{5,3},{6,0},{7,5},{8,10},{9,15},{10,... | collective-permute-start | bytes 2162696 | tf_op jit(solution)/shard_map/ppermute | solution.py:53
  67.3 4.7 %collective-permute-start.11 = (bf16[384,128]{1,0:T(8,128)(2,1)S(1)}, bf16[384,128]{1,0:T(8,128)(2,1)S(1)}, u32[]{:S(2)}, u32[]{:S(2)}) collective-permute-start(bf16[384,128]{1,0:T(8,128)(2,1)S(1)} %add_convert_fusion.8), channel_id=1, source_target_pairs={{0,8},{8,0},{1,9},{9,1},{2,10},{10,2},{3,11},{11,3},{4,12},{12,4},... | collective-permute-start | bytes 294920 | tf_op jit(solution)/shard_map/ppermute | solution.py:38
  67.8 25.9 %copy-start.6 = (s32[12]{0:T(128)S(1)}, s32[12]{0:T(128)}, u32[]{:S(2)}) copy-start(s32[12]{0:T(128)} %count_ref.1) | copy-start | bytes 148
  67.8 15.5 %collective-permute-start.17 = (bf16[8,64,512]{2,1,0:T(8,128)(2,1)S(1)}, bf16[8,64,512]{2,1,0:T(8,128)(2,1)S(1)}, u32[]{:S(2)}, u32[]{:S(2)}) collective-permute-start(bf16[8,64,512]{2,1,0:T(8,128)(2,1)S(1)} %pad_maximum_fusion.rest_0_), channel_id=1, source_target_pairs={{0,64},{1,193},{64,128},{65,1},{128,192},{129,65},{192,0},{193,129... | collective-permute-start | bytes 1572872 | tf_op jit(solution)/shard_map/ppermute | solution.py:53
  68.2 23.8 %collective-permute-start.16 = (bf16[8,64,512]{2,1,0:T(8,128)(2,1)S(1)}, bf16[8,64,512]{2,1,0:T(8,128)(2,1)S(1)}, u32[]{:S(2)}, u32[]{:S(2)}) collective-permute-start(bf16[8,64,512]{2,1,0:T(8,128)(2,1)S(1)} %pad_maximum_fusion.rest_0_), channel_id=1, source_target_pairs={{0,192},{1,65},{64,0},{65,129},{128,64},{129,193},{192,128},{193,1... | collective-permute-start | bytes 1572872 | tf_op jit(solution)/shard_map/ppermute | solution.py:53
  72.1 13.7 %collective-permute-start.12 = (bf16[384,128]{1,0:T(8,128)(2,1)S(1)}, bf16[384,128]{1,0:T(8,128)(2,1)S(1)}, u32[]{:S(2)}, u32[]{:S(2)}) collective-permute-start(bf16[384,128]{1,0:T(8,128)(2,1)S(1)} %add_convert_fusion.7), channel_id=1, source_target_pairs={{0,2},{2,0},{4,6},{6,4},{1,3},{3,1},{5,7},{7,5},{8,10},{10,8},{12,... | collective-permute-start | bytes 294920 | tf_op jit(solution)/shard_map/ppermute | solution.py:43
  74.0 22.8 %collective-permute-start.22 = (bf16[1,416,512]{2,1,0:T(8,128)(2,1)S(1)}, bf16[1,416,512]{2,1,0:T(8,128)(2,1)S(1)}, u32[]{:S(2)}, u32[]{:S(2)}) collective-permute-start(bf16[1,416,512]{2,1,0:T(8,128)(2,1)S(1)} %add_convert_fusion.4), channel_id=1, source_target_pairs={{0,8},{8,0},{1,9},{9,1},{2,10},{10,2},{3,11},{11,3},{4,12},{12,4},... | collective-permute-start | bytes 1277960 | tf_op jit(solution)/shard_map/ppermute | solution.py:38
  83.2 10.4 %collective-permute-start.21 = (bf16[8,64,512]{2,1,0:T(8,128)(2,1)S(1)}, bf16[8,64,512]{2,1,0:T(8,128)(2,1)S(1)}, u32[]{:S(2)}, u32[]{:S(2)}) collective-permute-start(bf16[8,64,512]{2,1,0:T(8,128)(2,1)S(1)} %collective-permute-done.17.rest_3_), channel_id=1, source_target_pairs={{0,64},{1,193},{64,128},{65,1},{128,192},{129,65},{192,0},{193,129... | collective-permute-start | bytes 1572872 | tf_op jit(solution)/shard_map/ppermute | solution.py:53
  83.4 13.4 %collective-permute-start.26 = (bf16[1,352,512]{2,1,0:T(8,128)(2,1)S(1)}, bf16[1,352,512]{2,1,0:T(8,128)(2,1)S(1)}, u32[]{:S(2)}, u32[]{:S(2)}) collective-permute-start(bf16[1,352,512]{2,1,0:T(8,128)(2,1)S(1)} %add_convert_fusion.5), channel_id=1, source_target_pairs={{0,8},{8,0},{1,9},{9,1},{2,10},{10,2},{3,11},{11,3},{4,12},{12,4},... | collective-permute-start | bytes 1081352 | tf_op jit(solution)/shard_map/ppermute | solution.py:38
  85.8 6.2 %collective-permute-start.13 = (bf16[384,128]{1,0:T(8,128)(2,1)S(1)}, bf16[384,128]{1,0:T(8,128)(2,1)S(1)}, u32[]{:S(2)}, u32[]{:S(2)}) collective-permute-start(bf16[384,128]{1,0:T(8,128)(2,1)S(1)} %add_convert_fusion.6.s0), channel_id=1, source_target_pairs={{0,4},{2,6},{4,0},{6,2},{1,5},{3,7},{5,1},{7,3},{8,12},{10,14},{12... | collective-permute-start | bytes 294920 | tf_op jit(solution)/shard_map/ppermute | solution.py:43

commit v5 on v4

--- a/solution.py
+++ b/solution.py
@@ -179,32 +179,22 @@
     return dx, dz * 2 + (slot & 1)
 
 
-def fetch(tiles, slot_ref, adapter_ref, place_ref, buffers, held, sems):
+def fetch(tiles, slot_ref, adapter_ref, place_ref, buffers, held):
     for t in range(tiles):
         dx, at = locate(slot_ref, adapter_ref, place_ref, t)
         for k, ref in enumerate(buffers):
 
             @pl.when(dx == k)
             def _(ref=ref, at=at, t=t):
-                pltpu.make_async_copy(
-                    ref.at[at], held.at[pl.ds(t * TILE, TILE)], sems.at[t]
-                ).start()
-
-
-def wait_for(t, buffers, held, sems):
-    pltpu.make_async_copy(
-        buffers[0].at[0], held.at[pl.ds(t * TILE, TILE)], sems.at[t]
-    ).wait()
+                held[t * TILE : (t + 1) * TILE] = ref[at]
 
 
 def shrink_kernel(slot_ref, adapter_ref, place_ref, x_ref, *rest):
-    buffers, out_ref, held, sems = rest[:4], rest[4], rest[5], rest[6]
+    buffers, out_ref, held = rest[:4], rest[4], rest[5]
     tiles = adapter_ref.shape[0]
-    fetch(tiles, slot_ref, adapter_ref, place_ref, buffers, held, sems)
+    fetch(tiles, slot_ref, adapter_ref, place_ref, buffers, held)
     left = lax.broadcasted_iota(jnp.int32, (TILE, 2 * TILE), 1) < TILE
     for t in range(0, tiles, 2):
-        wait_for(t, buffers, held, sems)
-        wait_for(t + 1, buffers, held, sems)
         both = lax.dot_general(
             x_ref[t * TILE : (t + 2) * TILE],
             held[t * TILE : (t + 2) * TILE],
@@ -217,13 +207,11 @@
 
 
 def expand_kernel(slot_ref, adapter_ref, place_ref, count_ref, s0, s1, *rest):
-    buffers, out_ref, held, sems = rest[:4], rest[4], rest[5], rest[6]
+    buffers, out_ref, held = rest[:4], rest[4], rest[5]
     tiles = adapter_ref.shape[0]
-    fetch(tiles, slot_ref, adapter_ref, place_ref, buffers, held, sems)
+    fetch(tiles, slot_ref, adapter_ref, place_ref, buffers, held)
     left = lax.broadcasted_iota(jnp.int32, (TILE, 2 * TILE), 1) < TILE
     for t in range(0, tiles, 2):
-        wait_for(t, buffers, held, sems)
-        wait_for(t + 1, buffers, held, sems)
         at = pl.ds(t * TILE // 2, TILE)
         total = s0[at].astype(F32) + s1[at].astype(F32)
         factors = held[t * TILE : (t + 2) * TILE]
@@ -242,11 +230,10 @@
         out_shape=shape,
         in_specs=[pl.BlockSpec(memory_space=pltpu.SMEM)] * len(scalars)
         + [pl.BlockSpec(memory_space=pltpu.VMEM)] * len(arrays)
-        + [pl.BlockSpec(memory_space=pl.ANY)] * len(buffers),
+        + [pl.BlockSpec(memory_space=pltpu.VMEM)] * len(buffers),
         out_specs=pl.BlockSpec(memory_space=pltpu.VMEM),
         scratch_shapes=[
             pltpu.VMEM((tiles * TILE, width), BF16),
-            pltpu.SemaphoreType.DMA((tiles,)),
         ],
         compiler_params=params(12),
         cost_estimate=cost(2 * tiles * TILE * TILE * width, 6 * tiles * TILE * width),

time: 98.7 us -> 95.6 us (0.969)
  Pallas kernels: 21.9 us -> 18.1 us
    pallas_call x2, Pallas kernels: 6.41 us -> 2.6 us  [with_factors(): pl.pallas_call(kernel, out_shape=shape, in_specs=[pl.BlockSpec(memory_spa...]
    ppermute x18, waiting for transfers between devices: 26.6 us -> 28.7 us  [turn(): return lax.ppermute(value, (axis, 'c'), pairs)]
  transfers between devices with their start and end apart: 27 -> 27, of which waited for: 9 -> 11; matrix products, arithmetic and copies ran while one was open for 1% -> 1% of each run, Pallas kernels for 20% -> 17%
where the time goes in v5:
time: 95.6 us; the launch traced here: 95.4 us
  starting transfers between devices  36.4 us (38%)
  waiting for transfers between devices  34.5 us (36%)
  Pallas kernels  18.1 us (19%)
  local copies, waits for them, and re-layouts  4.85 us (5%)
  other arithmetic  1.2 us (1%)
    ppermute x18, waiting for transfers between devices, turn(): return lax.ppermute(value, (axis, 'c'), pairs)  28.7 us
    ppermute x18, starting transfers between devices, turn(): return lax.ppermute(value, (axis, 'c'), pairs)  28.6 us
    pallas_call x2, Pallas kernels, partials(): pl.pallas_call(functools.partial(partial_kernel, MINE + skip, outputs), o...  11.3 us
    ppermute x2, waiting for transfers between devices, swap(): return lax.ppermute(value, axis, [(i, i ^ bit) for i in range(size)])  4.33 us
    ppermute x7, starting transfers between devices, shift(): lax.ppermute(value, axis, [(i, (i + step) % size) for i in range(size)])  4.28 us
    unnamed x25, local copies, waits for them, and re-layouts  4.15 us
    ppermute x2, starting transfers between devices, swap(): return lax.ppermute(value, axis, [(i, i ^ bit) for i in range(size)])  3.54 us
    pallas_call x2, Pallas kernels, stage(): pl.pallas_call(functools.partial(stage_kernel, THEIRS + skip), out_shape=...  3.01 us
  transfers between devices with their start and end apart: 27, of which 11 were waited for; matrix products, arithmetic and copies ran while one was open for 1% of the time, Pallas kernels for 17%

profile of v5, /device:TPU:8, one launch (start us, length us, event | category | flops | bytes accessed | tf_op | source)
XLA Modules:
  0.0 95.4 jit_solution(16882610891021530356)
XLA Ops:
  0.0 0.7 dynamic-slice_bitcast_fusion.meta_ref.place_ref
  0.7 3.4 %copy-done = bf16[512,8192]{1,0:T(8,128)(2,1)S(1)} copy-done((bf16[512,8192]{1,0:T(8,128)(2,1)S(1)}, bf16[512,8192]{1,0:T(8,128)(2,1)}, u32[]{:S(2)}) %copy-start) | copy-done | bytes 8388632
  4.1 0.7 copy-done.2
  4.8 1.0 %stage.2 = bf16[2,512,512]{2,1,0:T(8,128)(2,1)S(1)} custom-call(s32[19]{0:T(128)S(1)} %dynamic-slice_bitcast_fusion.meta_ref.place_ref, f32[4,64]{1,0:T(4,128)S(1)} %copy-done.2, bf16[512,8192]{1,0:T(8,128)(2,1)S(1)} %copy-done), custom_call_target="tpu_custom_call" | custom-call | bytes 2097152 | tf_op jit(solution)/shard_map/stage/pallas_call | solution.py:101
  5.9 0.5 collective-permute-start
  6.4 2.0 %stage.3 = bf16[6,512,512]{2,1,0:T(8,128)(2,1)S(1)} custom-call(s32[19]{0:T(128)S(1)} %dynamic-slice_bitcast_fusion.meta_ref.place_ref, f32[4,64]{1,0:T(4,128)S(1)} %copy-done.2, bf16[512,8192]{1,0:T(8,128)(2,1)S(1)} %copy-done), custom_call_target="tpu_custom_call" | custom-call | bytes 6291456 | tf_op jit(solution)/shard_map/stage/pallas_call | solution.py:101
  8.4 1.3 %collective-permute-done.xs_ref = bf16[768,512]{1,0:T(8,128)(2,1)S(1)} collective-permute-done((bf16[768,512]{1,0:T(8,128)(2,1)S(1)}, bf16[768,512]{1,0:T(8,128)(2,1)S(1)}, u32[]{:S(2)}, u32[]{:S(2)}) %collective-permute-start) | collective-permute-done | bytes 786464 | tf_op jit(solution)/shard_map/ppermute | solution.py:38
  9.7 0.1 collective-permute-start.5
  9.9 3.3 %partials.2 = (bf16[2,416,512]{2,1,0:T(8,128)(2,1)S(1)}, bf16[2,352,512]{2,1,0:T(8,128)(2,1)S(1)}) custom-call(s32[19]{0:T(128)S(1)} %dynamic-slice_bitcast_fusion.meta_ref.place_ref, bf16[768,512]{1,0:T(8,128)(2,1)S(1)} %copy-done.1, bf16[768,512]{1,0:T(8,128)(2,1)S(1)} %collective-permute-done.xs_ref, bf16[512,8192]{1,0:T(8,128)(2,1)S(1)} %bitcast.4, ...), custom_call_target="tpu_custom_call" | custom-call | flops 1610612736 | bytes 3670016 | tf_op jit(solution)/shard_map/partials/pallas_call | solution.py:143
  13.2 6.4 %collective-permute-start.2 = (bf16[2,64,512]{2,1,0:T(8,128)(2,1)S(1)}, bf16[2,64,512]{2,1,0:T(8,128)(2,1)S(1)}, u32[]{:S(2)}, u32[]{:S(2)}) collective-permute-start(bf16[2,64,512]{2,1,0:T(8,128)(2,1)S(1)} %bitcast.5), channel_id=1, source_target_pairs={{0,48},{1,17},{16,0},{17,33},{32,16},{33,49},{48,32},{49,1},{2,50}... | collective-permute-start | bytes 393224 | tf_op jit(solution)/shard_map/ppermute | solution.py:53
  19.6 1.0 %collective-permute-start.3 = (bf16[2,64,512]{2,1,0:T(8,128)(2,1)S(1)}, bf16[2,64,512]{2,1,0:T(8,128)(2,1)S(1)}, u32[]{:S(2)}, u32[]{:S(2)}) collective-permute-start(bf16[2,64,512]{2,1,0:T(8,128)(2,1)S(1)} %bitcast.6), channel_id=1, source_target_pairs={{0,32},{1,33},{16,48},{17,49},{32,0},{33,1},{48,16},{49,17},{2,34}... | collective-permute-start | bytes 393224 | tf_op jit(solution)/shard_map/ppermute | solution.py:53
  20.6 2.8 %collective-permute-start.4 = (bf16[2,64,512]{2,1,0:T(8,128)(2,1)S(1)}, bf16[2,64,512]{2,1,0:T(8,128)(2,1)S(1)}, u32[]{:S(2)}, u32[]{:S(2)}) collective-permute-start(bf16[2,64,512]{2,1,0:T(8,128)(2,1)S(1)} %bitcast.7), channel_id=1, source_target_pairs={{0,16},{1,49},{16,32},{17,1},{32,48},{33,17},{48,0},{49,33},{2,18}... | collective-permute-start | bytes 393224 | tf_op jit(solution)/shard_map/ppermute | solution.py:53
  23.4 1.6 %collective-permute-start.18 = (bf16[2,416,512]{2,1,0:T(8,128)(2,1)S(1)}, bf16[2,416,512]{2,1,0:T(8,128)(2,1)S(1)}, u32[]{:S(2)}, u32[]{:S(2)}) collective-permute-start(bf16[2,416,512]{2,1,0:T(8,128)(2,1)S(1)} %get-tuple-element.25), channel_id=1, source_target_pairs={{0,2},{1,7},{2,4},{3,1},{4,6},{5,3},{6,0},{7,5},{8,10},{9,15},{10,... | collective-permute-start | bytes 2555912 | tf_op jit(solution)/shard_map/ppermute | solution.py:53
  25.0 2.7 %collective-permute-start.6 = (bf16[2,64,512]{2,1,0:T(8,128)(2,1)S(1)}, bf16[2,64,512]{2,1,0:T(8,128)(2,1)S(1)}, u32[]{:S(2)}, u32[]{:S(2)}) collective-permute-start(bf16[2,64,512]{2,1,0:T(8,128)(2,1)S(1)} %copy-done.8), channel_id=1, source_target_pairs={{0,16},{1,49},{16,32},{17,1},{32,48},{33,17},{48,0},{49,33},{2,18}... | collective-permute-start | bytes 393224 | tf_op jit(solution)/shard_map/ppermute | solution.py:53
  27.7 8.0 %partials.3 = (bf16[2,416,512]{2,1,0:T(8,128)(2,1)S(1)}, bf16[2,352,512]{2,1,0:T(8,128)(2,1)S(1)}, bf16[2,416,512]{2,1,0:T(8,128)(2,1)S(1)}, bf16[2,352,512]{2,1...) custom-call(s32[19]{0:T(128)S(1)} %dynamic-slice_bitcast_fusion.meta_ref.place_ref, ...), custom_call_target="tpu_custom_call" | custom-call | flops 4831838208 | bytes 11010048 | tf_op jit(solution)/shard_map/partials/pallas_call | solution.py:143
  35.6 1.4 %collective-permute-start.23 = (bf16[2,352,512]{2,1,0:T(8,128)(2,1)S(1)}, bf16[2,352,512]{2,1,0:T(8,128)(2,1)S(1)}, u32[]{:S(2)}, u32[]{:S(2)}) collective-permute-start(bf16[2,352,512]{2,1,0:T(8,128)(2,1)S(1)} %get-tuple-element.44), channel_id=1, source_target_pairs={{0,2},{1,7},{2,4},{3,1},{4,6},{5,3},{6,0},{7,5},{8,10},{9,15},{10,... | collective-permute-start | bytes 2162696 | tf_op jit(solution)/shard_map/ppermute | solution.py:53
  37.1 2.8 %collective-permute-start.7 = (bf16[8,64,512]{2,1,0:T(8,128)(2,1)S(1)}, bf16[8,64,512]{2,1,0:T(8,128)(2,1)S(1)}, u32[]{:S(2)}, u32[]{:S(2)}) collective-permute-start(bf16[8,64,512]{2,1,0:T(8,128)(2,1)S(1)} %constant_dynamic-update-slice_fusion.rest_0_), channel_id=1, source_target_pairs={{0,192},{1,65},{64,0},{65,129},{128,64},{129,193},{192,128},{193,1... | collective-permute-start | bytes 1572872 | tf_op jit(solution)/shard_map/ppermute | solution.py:53
  39.9 0.2 add_convert_fusion.1
  40.2 0.3 collective-permute-start.19
  40.5 0.2 collective-permute-start.14
  40.7 8.1 %collective-permute-done.14 = bf16[2,64,512]{2,1,0:T(8,128)(2,1)S(1)} collective-permute-done((bf16[2,64,512]{2,1,0:T(8,128)(2,1)S(1)}, bf16[2,64,512]{2,1,0:T(8,128)(2,1)S(1)}, u32[]{:S(2)}, u32[]{:S(2)}) %collective-permute-start.14) | collective-permute-done | bytes 131104 | tf_op jit(solution)/shard_map/ppermute | solution.py:53
  48.8 1.5 %collective-permute-done.7.rest_1_ = bf16[8,64,512]{2,1,0:T(8,128)(2,1)S(1)} collective-permute-done((bf16[8,64,512]{2,1,0:T(8,128)(2,1)S(1)}, bf16[8,64,512]{2,1,0:T(8,128)(2,1)S(1)}, u32[]{:S(2)}, u32[]{:S(2)}) %collective-permute-start.7) | collective-permute-done | bytes 524320 | tf_op jit(solution)/shard_map/ppermute | solution.py:53
  50.3 0.2 add_convert_fusion.3
  50.5 1.3 %collective-permute-start.24 = (bf16[2,352,512]{2,1,0:T(8,128)(2,1)S(1)}, bf16[2,352,512]{2,1,0:T(8,128)(2,1)S(1)}, u32[]{:S(2)}, u32[]{:S(2)}) collective-permute-start(bf16[2,352,512]{2,1,0:T(8,128)(2,1)S(1)} %add_convert_fusion.3), channel_id=1, source_target_pairs={{0,2},{1,7},{2,4},{3,1},{4,6},{5,3},{6,0},{7,5},{8,10},{9,15},{10,... | collective-permute-start | bytes 2162696 | tf_op jit(solution)/shard_map/ppermute | solution.py:53
  51.9 1.5 %collective-permute-start.9 = (bf16[8,64,512]{2,1,0:T(8,128)(2,1)S(1)}, bf16[8,64,512]{2,1,0:T(8,128)(2,1)S(1)}, u32[]{:S(2)}, u32[]{:S(2)}) collective-permute-start(bf16[8,64,512]{2,1,0:T(8,128)(2,1)S(1)} %collective-permute-done.8.rest_3_), channel_id=1, source_target_pairs={{0,64},{1,193},{64,128},{65,1},{128,192},{129,65},{192,0},{193,129... | collective-permute-start | bytes 1572872 | tf_op jit(solution)/shard_map/ppermute | solution.py:53
  53.4 0.6 collective-permute-start.15
  54.0 2.1 %collective-permute-done.19 = bf16[2,416,512]{2,1,0:T(8,128)(2,1)S(1)} collective-permute-done((bf16[2,416,512]{2,1,0:T(8,128)(2,1)S(1)}, bf16[2,416,512]{2,1,0:T(8,128)(2,1)S(1)}, u32[]{:S(2)}, u32[]{:S(2)}) %collective-permute-start.19) | collective-permute-done | bytes 852000 | tf_op jit(solution)/shard_map/ppermute | solution.py:53
  56.1 0.2 add_convert_fusion
  56.4 1.4 %collective-permute-start.20 = (bf16[2,416,512]{2,1,0:T(8,128)(2,1)S(1)}, bf16[2,416,512]{2,1,0:T(8,128)(2,1)S(1)}, u32[]{:S(2)}, u32[]{:S(2)}) collective-permute-start(bf16[2,416,512]{2,1,0:T(8,128)(2,1)S(1)} %add_convert_fusion), channel_id=1, source_target_pairs={{0,2},{1,7},{2,4},{3,1},{4,6},{5,3},{6,0},{7,5},{8,10},{9,15},{10,... | collective-permute-start | bytes 2555912 | tf_op jit(solution)/shard_map/ppermute | solution.py:53
  57.7 4.6 %collective-permute-done.9.rest_2_ = bf16[8,64,512]{2,1,0:T(8,128)(2,1)S(1)} collective-permute-done((bf16[8,64,512]{2,1,0:T(8,128)(2,1)S(1)}, bf16[8,64,512]{2,1,0:T(8,128)(2,1)S(1)}, u32[]{:S(2)}, u32[]{:S(2)}) %collective-permute-start.9) | collective-permute-done | bytes 524320 | tf_op jit(solution)/shard_map/ppermute | solution.py:53
  62.3 1.3 %shrink.1 = bf16[384,128]{1,0:T(8,128)(2,1)S(1)} custom-call(s32[32]{0:T(128)S(1)} %copy-done.4, s32[12]{0:T(128)S(1)} %copy-done.5, s32[19]{0:T(128)S(1)} %dynamic-slice_bitcast_fusion.meta_ref.place_ref, bf16[768,512]{1,0:T(8,128)(2,1)S(1)} %copy-done.1, bf16[8,64,512]{2,1,0:T(8,128)(2,1)S(1)} %constant_dynamic-update-slice_fusion.rest_0_, ...), custom_call_target="tpu_custom_call" | custom-call | flops 50331648 | bytes 2359296 | tf_op jit(solution)/shard_map/shrink/pallas_call | solution.py:228
  63.7 0.2 collective-permute-done.24
  63.9 0.2 add_convert_fusion.2
  64.1 1.4 %collective-permute-start.25 = (bf16[2,352,512]{2,1,0:T(8,128)(2,1)S(1)}, bf16[2,352,512]{2,1,0:T(8,128)(2,1)S(1)}, u32[]{:S(2)}, u32[]{:S(2)}) collective-permute-start(bf16[2,352,512]{2,1,0:T(8,128)(2,1)S(1)} %add_convert_fusion.2), channel_id=1, source_target_pairs={{0,2},{1,7},{2,4},{3,1},{4,6},{5,3},{6,0},{7,5},{8,10},{9,15},{10,... | collective-permute-start | bytes 2162696 | tf_op jit(solution)/shard_map/ppermute | solution.py:53
  65.4 1.1 %collective-permute-start.11 = (bf16[384,128]{1,0:T(8,128)(2,1)S(1)}, bf16[384,128]{1,0:T(8,128)(2,1)S(1)}, u32[]{:S(2)}, u32[]{:S(2)}) collective-permute-start(bf16[384,128]{1,0:T(8,128)(2,1)S(1)} %add_convert_fusion.8), channel_id=1, source_target_pairs={{0,8},{8,0},{1,9},{9,1},{2,10},{10,2},{3,11},{11,3},{4,12},{12,4},... | collective-permute-start | bytes 294920 | tf_op jit(solution)/shard_map/ppermute | solution.py:38
  66.6 1.6 %collective-permute-start.17 = (bf16[8,64,512]{2,1,0:T(8,128)(2,1)S(1)}, bf16[8,64,512]{2,1,0:T(8,128)(2,1)S(1)}, u32[]{:S(2)}, u32[]{:S(2)}) collective-permute-start(bf16[8,64,512]{2,1,0:T(8,128)(2,1)S(1)} %pad_maximum_fusion.rest_0_), channel_id=1, source_target_pairs={{0,64},{1,193},{64,128},{65,1},{128,192},{129,65},{192,0},{193,129... | collective-permute-start | bytes 1572872 | tf_op jit(solution)/shard_map/ppermute | solution.py:53
  68.2 1.7 %collective-permute-start.16 = (bf16[8,64,512]{2,1,0:T(8,128)(2,1)S(1)}, bf16[8,64,512]{2,1,0:T(8,128)(2,1)S(1)}, u32[]{:S(2)}, u32[]{:S(2)}) collective-permute-start(bf16[8,64,512]{2,1,0:T(8,128)(2,1)S(1)} %pad_maximum_fusion.rest_0_), channel_id=1, source_target_pairs={{0,192},{1,65},{64,0},{65,129},{128,64},{129,193},{192,128},{193,1... | collective-permute-start | bytes 1572872 | tf_op jit(solution)/shard_map/ppermute | solution.py:53
  69.9 0.2 collective-permute-done.11
  70.2 1.7 %collective-permute-start.12 = (bf16[384,128]{1,0:T(8,128)(2,1)S(1)}, bf16[384,128]{1,0:T(8,128)(2,1)S(1)}, u32[]{:S(2)}, u32[]{:S(2)}) collective-permute-start(bf16[384,128]{1,0:T(8,128)(2,1)S(1)} %add_convert_fusion.7), channel_id=1, source_target_pairs={{0,2},{2,0},{4,6},{6,4},{1,3},{3,1},{5,7},{7,5},{8,10},{10,8},{12,... | collective-permute-start | bytes 294920 | tf_op jit(solution)/shard_map/ppermute | solution.py:43
  71.8 1.5 %collective-permute-done.20.rest_1_ = bf16[2,416,512]{2,1,0:T(8,128)(2,1)S(1)} collective-permute-done((bf16[2,416,512]{2,1,0:T(8,128)(2,1)S(1)}, bf16[2,416,512]{2,1,0:T(8,128)(2,1)S(1)}, u32[]{:S(2)}, u32[]{:S(2)}) %collective-permute-start.20) | collective-permute-done | bytes 852000 | tf_op jit(solution)/shard_map/ppermute | solution.py:53
  73.4 1.1 %collective-permute-start.22 = (bf16[1,416,512]{2,1,0:T(8,128)(2,1)S(1)}, bf16[1,416,512]{2,1,0:T(8,128)(2,1)S(1)}, u32[]{:S(2)}, u32[]{:S(2)}) collective-permute-start(bf16[1,416,512]{2,1,0:T(8,128)(2,1)S(1)} %add_convert_fusion.4), channel_id=1, source_target_pairs={{0,8},{8,0},{1,9},{9,1},{2,10},{10,2},{3,11},{11,3},{4,12},{12,4},... | collective-permute-start | bytes 1277960 | tf_op jit(solution)/shard_map/ppermute | solution.py:38
  74.5 7.9 %collective-permute-done.17.rest_3_ = bf16[8,64,512]{2,1,0:T(8,128)(2,1)S(1)} collective-permute-done((bf16[8,64,512]{2,1,0:T(8,128)(2,1)S(1)}, bf16[8,64,512]{2,1,0:T(8,128)(2,1)S(1)}, u32[]{:S(2)}, u32[]{:S(2)}) %collective-permute-start.17) | collective-permute-done | bytes 524320 | tf_op jit(solution)/shard_map/ppermute | solution.py:53
  82.6 1.3 %collective-permute-start.26 = (bf16[1,352,512]{2,1,0:T(8,128)(2,1)S(1)}, bf16[1,352,512]{2,1,0:T(8,128)(2,1)S(1)}, u32[]{:S(2)}, u32[]{:S(2)}) collective-permute-start(bf16[1,352,512]{2,1,0:T(8,128)(2,1)S(1)} %add_convert_fusion.5), channel_id=1, source_target_pairs={{0,8},{8,0},{1,9},{9,1},{2,10},{10,2},{3,11},{11,3},{4,12},{12,4},... | collective-permute-start | bytes 1081352 | tf_op jit(solution)/shard_map/ppermute | solution.py:38
  83.9 1.9 %collective-permute-start.13 = (bf16[384,128]{1,0:T(8,128)(2,1)S(1)}, bf16[384,128]{1,0:T(8,128)(2,1)S(1)}, u32[]{:S(2)}, u32[]{:S(2)}) collective-permute-start(bf16[384,128]{1,0:T(8,128)(2,1)S(1)} %add_convert_fusion.6.s0), channel_id=1, source_target_pairs={{0,4},{2,6},{4,0},{6,2},{1,5},{3,7},{5,1},{7,3},{8,12},{10,14},{12... | collective-permute-start | bytes 294920 | tf_op jit(solution)/shard_map/ppermute | solution.py:43
  85.8 4.3 %collective-permute-done.13.s1 = bf16[384,128]{1,0:T(8,128)(2,1)S(1)} collective-permute-done((bf16[384,128]{1,0:T(8,128)(2,1)S(1)}, bf16[384,128]{1,0:T(8,128)(2,1)S(1)}, u32[]{:S(2)}, u32[]{:S(2)}) %collective-permute-start.13) | collective-permute-done | bytes 98336 | tf_op jit(solution)/shard_map/ppermute | solution.py:43
  90.1 2.7 %collective-permute-done.21.rest_2_ = bf16[8,64,512]{2,1,0:T(8,128)(2,1)S(1)} collective-permute-done((bf16[8,64,512]{2,1,0:T(8,128)(2,1)S(1)}, bf16[8,64,512]{2,1,0:T(8,128)(2,1)S(1)}, u32[]{:S(2)}, u32[]{:S(2)}) %collective-permute-start.21) | collective-permute-done | bytes 524320 | tf_op jit(solution)/shard_map/ppermute | solution.py:53
  92.9 1.3 %expand.1.delta_ref = f32[768,512]{1,0:T(8,128)S(1)} custom-call(s32[32]{0:T(128)S(1)} %copy-done.4, s32[12]{0:T(128)S(1)} %copy-done.5, s32[19]{0:T(128)S(1)} %dynamic-slice_bitcast_fusion.meta_ref.place_ref, s32[12]{0:T(128)S(1)} %copy-done.6, bf16[384,128]{1,0:T(8,128)(2,1)S(1)} %add_convert_fusion.6.s0, bf16[384,128]{1,0:T(8,128)(2,1)S(1)} %collective-permute-done.13.s1, ...), custom_call_target="tpu_custom_call" | custom-call | flops 50331648 | bytes 2359296 | tf_op jit(solution)/shard_map/expand/pallas_call | solution.py:228
  94.2 1.2 %finish.1 = bf16[768,512]{1,0:T(8,128)(2,1)} custom-call(f32[768,512]{1,0:T(8,128)S(1)} %expand.1.delta_ref, bf16[2,416,512]{2,1,0:T(8,128)(2,1)S(1)} %get-tuple-element.39.rest_0_, bf16[2,416,512]{2,1,0:T(8,128)(2,1)S(1)} %collective-permute-done.20.rest_1_, bf16[1,416,512]{2,1,0:T(8,128)(2,1)S(1)} %collective-permute-done.22.rest_2_, ...), custom_call_target="tpu_custom_call" | custom-call | bytes 5505024 | tf_op jit(solution)/shard_map/finish/pallas_call | solution.py:359
  (51 shorter events, 0.7 us)
Async XLA Ops:
  0.7 3.4 %copy-start = (bf16[512,8192]{1,0:T(8,128)(2,1)S(1)}, bf16[512,8192]{1,0:T(8,128)(2,1)}, u32[]{:S(2)}) copy-start(bf16[512,8192]{1,0:T(8,128)(2,1)} %w_ref.7) | copy-start | bytes 25165828
  4.1 0.7 copy-start.2
  4.8 1.2 %copy-start.1 = (bf16[768,512]{1,0:T(8,128)(2,1)S(1)}, bf16[768,512]{1,0:T(8,128)(2,1)}, u32[]{:S(2)}) copy-start(bf16[768,512]{1,0:T(8,128)(2,1)} %x_ref.5) | copy-start | bytes 2359300
  4.8 5.1 %slice-start = ((s8[8388608]{0:T(1024)(128)(4,1)}), s8[4194304]{0:T(1024)(128)(4,1)S(1)}, s32[]{:S(2)}) async-start(s8[8388608]{0:T(1024)(128)(4,1)} %bitcast.3), calls=%async_computation | async-start | bytes 8388608
  5.8 4.0 %slice-start.1 = ((s8[8388608]{0:T(1024)(128)(4,1)}), s8[4194304]{0:T(1024)(128)(4,1)S(1)}, s32[]{:S(2)}) async-start(s8[8388608]{0:T(1024)(128)(4,1)} %bitcast.3), calls=%async_computation.1 | async-start | bytes 8388608
  5.8 4.0 %copy-start.3 = (f32[4,64]{1,0:T(4,128)S(1)}, f32[4,64]{1,0:T(4,128)}, u32[]{:S(2)}) copy-start(f32[4,64]{1,0:T(4,128)} %s_ref.3) | copy-start | bytes 3076
  5.8 3.9 %collective-permute-start.1 = (bf16[2,512,512]{2,1,0:T(8,128)(2,1)S(1)}, bf16[2,512,512]{2,1,0:T(8,128)(2,1)S(1)}, u32[]{:S(2)}, u32[]{:S(2)}) collective-permute-start(bf16[2,512,512]{2,1,0:T(8,128)(2,1)S(1)} %stage.2), channel_id=1, source_target_pairs={{0,1},{1,0},{2,3},{3,2},{4,5},{5,4},{6,7},{7,6},{8,9},{9,8},{10,11... | collective-permute-start | bytes 3145736 | tf_op jit(solution)/shard_map/ppermute | solution.py:38
  5.9 3.8 %collective-permute-start = (bf16[768,512]{1,0:T(8,128)(2,1)S(1)}, bf16[768,512]{1,0:T(8,128)(2,1)S(1)}, u32[]{:S(2)}, u32[]{:S(2)}) collective-permute-start(bf16[768,512]{1,0:T(8,128)(2,1)S(1)} %copy-done.1), channel_id=1, source_target_pairs={{0,1},{1,0},{2,3},{3,2},{4,5},{5,4},{6,7},{7,6},{8,9},{9,8},{10,11... | collective-permute-start | bytes 2359304 | tf_op jit(solution)/shard_map/ppermute | solution.py:38
  8.4 4.8 %copy-start.7 = (bf16[2,512,64]{1,2,0:T(8,128)(2,1)S(1)}, bf16[2,512,64]{1,2,0:T(8,128)(2,1)}, u32[]{:S(2)}) copy-start(bf16[2,512,64]{1,2,0:T(8,128)(2,1)} %param.12) | copy-start | bytes 393220
  8.4 16.6 %copy-start.8 = (bf16[2,64,512]{2,1,0:T(8,128)(2,1)S(1)}, bf16[2,64,512]{2,1,0:T(8,128)(2,1)}, u32[]{:S(2)}) copy-start(bf16[2,64,512]{2,1,0:T(8,128)(2,1)} %param.13) | copy-start | bytes 393220
  9.7 15.3 %collective-permute-start.5 = (bf16[6,512,512]{2,1,0:T(8,128)(2,1)S(1)}, bf16[6,512,512]{2,1,0:T(8,128)(2,1)S(1)}, u32[]{:S(2)}, u32[]{:S(2)}) collective-permute-start(bf16[6,512,512]{2,1,0:T(8,128)(2,1)S(1)} %stage.3), channel_id=1, source_target_pairs={{0,1},{1,0},{2,3},{3,2},{4,5},{5,4},{6,7},{7,6},{8,9},{9,8},{10,11... | collective-permute-start | bytes 9437192 | tf_op jit(solution)/shard_map/ppermute | solution.py:38
  13.2 22.4 %collective-permute-start.2 = (bf16[2,64,512]{2,1,0:T(8,128)(2,1)S(1)}, bf16[2,64,512]{2,1,0:T(8,128)(2,1)S(1)}, u32[]{:S(2)}, u32[]{:S(2)}) collective-permute-start(bf16[2,64,512]{2,1,0:T(8,128)(2,1)S(1)} %bitcast.5), channel_id=1, source_target_pairs={{0,48},{1,17},{16,0},{17,33},{32,16},{33,49},{48,32},{49,1},{2,50}... | collective-permute-start | bytes 393224 | tf_op jit(solution)/shard_map/ppermute | solution.py:53
  19.6 17.4 %collective-permute-start.3 = (bf16[2,64,512]{2,1,0:T(8,128)(2,1)S(1)}, bf16[2,64,512]{2,1,0:T(8,128)(2,1)S(1)}, u32[]{:S(2)}, u32[]{:S(2)}) collective-permute-start(bf16[2,64,512]{2,1,0:T(8,128)(2,1)S(1)} %bitcast.6), channel_id=1, source_target_pairs={{0,32},{1,33},{16,48},{17,49},{32,0},{33,1},{48,16},{49,17},{2,34}... | collective-permute-start | bytes 393224 | tf_op jit(solution)/shard_map/ppermute | solution.py:53
  20.6 16.4 %collective-permute-start.4 = (bf16[2,64,512]{2,1,0:T(8,128)(2,1)S(1)}, bf16[2,64,512]{2,1,0:T(8,128)(2,1)S(1)}, u32[]{:S(2)}, u32[]{:S(2)}) collective-permute-start(bf16[2,64,512]{2,1,0:T(8,128)(2,1)S(1)} %bitcast.7), channel_id=1, source_target_pairs={{0,16},{1,49},{16,32},{17,1},{32,48},{33,17},{48,0},{49,33},{2,18}... | collective-permute-start | bytes 393224 | tf_op jit(solution)/shard_map/ppermute | solution.py:53
  23.4 16.5 %collective-permute-start.18 = (bf16[2,416,512]{2,1,0:T(8,128)(2,1)S(1)}, bf16[2,416,512]{2,1,0:T(8,128)(2,1)S(1)}, u32[]{:S(2)}, u32[]{:S(2)}) collective-permute-start(bf16[2,416,512]{2,1,0:T(8,128)(2,1)S(1)} %get-tuple-element.25), channel_id=1, source_target_pairs={{0,2},{1,7},{2,4},{3,1},{4,6},{5,3},{6,0},{7,5},{8,10},{9,15},{10,... | collective-permute-start | bytes 2555912 | tf_op jit(solution)/shard_map/ppermute | solution.py:53
  25.0 12.0 %collective-permute-start.6 = (bf16[2,64,512]{2,1,0:T(8,128)(2,1)S(1)}, bf16[2,64,512]{2,1,0:T(8,128)(2,1)S(1)}, u32[]{:S(2)}, u32[]{:S(2)}) collective-permute-start(bf16[2,64,512]{2,1,0:T(8,128)(2,1)S(1)} %copy-done.8), channel_id=1, source_target_pairs={{0,16},{1,49},{16,32},{17,1},{32,48},{33,17},{48,0},{49,33},{2,18}... | collective-permute-start | bytes 393224 | tf_op jit(solution)/shard_map/ppermute | solution.py:53
  35.6 14.7 %collective-permute-start.23 = (bf16[2,352,512]{2,1,0:T(8,128)(2,1)S(1)}, bf16[2,352,512]{2,1,0:T(8,128)(2,1)S(1)}, u32[]{:S(2)}, u32[]{:S(2)}) collective-permute-start(bf16[2,352,512]{2,1,0:T(8,128)(2,1)S(1)} %get-tuple-element.44), channel_id=1, source_target_pairs={{0,2},{1,7},{2,4},{3,1},{4,6},{5,3},{6,0},{7,5},{8,10},{9,15},{10,... | collective-permute-start | bytes 2162696 | tf_op jit(solution)/shard_map/ppermute | solution.py:53
  37.1 13.2 %collective-permute-start.7 = (bf16[8,64,512]{2,1,0:T(8,128)(2,1)S(1)}, bf16[8,64,512]{2,1,0:T(8,128)(2,1)S(1)}, u32[]{:S(2)}, u32[]{:S(2)}) collective-permute-start(bf16[8,64,512]{2,1,0:T(8,128)(2,1)S(1)} %constant_dynamic-update-slice_fusion.rest_0_), channel_id=1, source_target_pairs={{0,192},{1,65},{64,0},{65,129},{128,64},{129,193},{192,128},{193,1... | collective-permute-start | bytes 1572872 | tf_op jit(solution)/shard_map/ppermute | solution.py:53
  39.9 10.4 %collective-permute-start.8 = (bf16[8,64,512]{2,1,0:T(8,128)(2,1)S(1)}, bf16[8,64,512]{2,1,0:T(8,128)(2,1)S(1)}, u32[]{:S(2)}, u32[]{:S(2)}) collective-permute-start(bf16[8,64,512]{2,1,0:T(8,128)(2,1)S(1)} %constant_dynamic-update-slice_fusion.rest_0_), channel_id=1, source_target_pairs={{0,64},{1,193},{64,128},{65,1},{128,192},{129,65},{192,0},{193,129... | collective-permute-start | bytes 1572872 | tf_op jit(solution)/shard_map/ppermute | solution.py:53
  40.2 16.0 %collective-permute-start.19 = (bf16[2,416,512]{2,1,0:T(8,128)(2,1)S(1)}, bf16[2,416,512]{2,1,0:T(8,128)(2,1)S(1)}, u32[]{:S(2)}, u32[]{:S(2)}) collective-permute-start(bf16[2,416,512]{2,1,0:T(8,128)(2,1)S(1)} %add_convert_fusion.1), channel_id=1, source_target_pairs={{0,2},{1,7},{2,4},{3,1},{4,6},{5,3},{6,0},{7,5},{8,10},{9,15},{10,... | collective-permute-start | bytes 2555912 | tf_op jit(solution)/shard_map/ppermute | solution.py:53
  40.5 8.3 %collective-permute-start.14 = (bf16[2,64,512]{2,1,0:T(8,128)(2,1)S(1)}, bf16[2,64,512]{2,1,0:T(8,128)(2,1)S(1)}, u32[]{:S(2)}, u32[]{:S(2)}) collective-permute-start(bf16[2,64,512]{2,1,0:T(8,128)(2,1)S(1)} %collective-permute-done.6), channel_id=1, source_target_pairs={{0,16},{1,49},{16,32},{17,1},{32,48},{33,17},{48,0},{49,33},{2,18}... | collective-permute-start | bytes 393224 | tf_op jit(solution)/shard_map/ppermute | solution.py:53
  50.5 11.8 %copy-start.4 = (s32[32]{0:T(128)S(1)}, s32[32]{0:T(128)}, u32[]{:S(2)}) copy-start(s32[32]{0:T(128)} %slot_ref.3) | copy-start | bytes 388
  50.5 11.8 %copy-start.5 = (s32[12]{0:T(128)S(1)}, s32[12]{0:T(128)}, u32[]{:S(2)}) copy-start(s32[12]{0:T(128)} %adapter_ref.3) | copy-start | bytes 148
  50.5 13.3 %collective-permute-start.24 = (bf16[2,352,512]{2,1,0:T(8,128)(2,1)S(1)}, bf16[2,352,512]{2,1,0:T(8,128)(2,1)S(1)}, u32[]{:S(2)}, u32[]{:S(2)}) collective-permute-start(bf16[2,352,512]{2,1,0:T(8,128)(2,1)S(1)} %add_convert_fusion.3), channel_id=1, source_target_pairs={{0,2},{1,7},{2,4},{3,1},{4,6},{5,3},{6,0},{7,5},{8,10},{9,15},{10,... | collective-permute-start | bytes 2162696 | tf_op jit(solution)/shard_map/ppermute | solution.py:53
  51.9 10.4 %collective-permute-start.9 = (bf16[8,64,512]{2,1,0:T(8,128)(2,1)S(1)}, bf16[8,64,512]{2,1,0:T(8,128)(2,1)S(1)}, u32[]{:S(2)}, u32[]{:S(2)}) collective-permute-start(bf16[8,64,512]{2,1,0:T(8,128)(2,1)S(1)} %collective-permute-done.8.rest_3_), channel_id=1, source_target_pairs={{0,64},{1,193},{64,128},{65,1},{128,192},{129,65},{192,0},{193,129... | collective-permute-start | bytes 1572872 | tf_op jit(solution)/shard_map/ppermute | solution.py:53
  53.4 13.2 %collective-permute-start.15 = (bf16[2,64,512]{2,1,0:T(8,128)(2,1)S(1)}, bf16[2,64,512]{2,1,0:T(8,128)(2,1)S(1)}, u32[]{:S(2)}, u32[]{:S(2)}) collective-permute-start(bf16[2,64,512]{2,1,0:T(8,128)(2,1)S(1)} %collective-permute-done.14), channel_id=1, source_target_pairs={{0,16},{1,49},{16,32},{17,1},{32,48},{33,17},{48,0},{49,33},{2,18}... | collective-permute-start | bytes 393224 | tf_op jit(solution)/shard_map/ppermute | solution.py:53
  56.4 17.0 %collective-permute-start.20 = (bf16[2,416,512]{2,1,0:T(8,128)(2,1)S(1)}, bf16[2,416,512]{2,1,0:T(8,128)(2,1)S(1)}, u32[]{:S(2)}, u32[]{:S(2)}) collective-permute-start(bf16[2,416,512]{2,1,0:T(8,128)(2,1)S(1)} %add_convert_fusion), channel_id=1, source_target_pairs={{0,2},{1,7},{2,4},{3,1},{4,6},{5,3},{6,0},{7,5},{8,10},{9,15},{10,... | collective-permute-start | bytes 2555912 | tf_op jit(solution)/shard_map/ppermute | solution.py:53
  63.6 1.8 %collective-permute-start.10 = (bf16[384,128]{1,0:T(8,128)(2,1)S(1)}, bf16[384,128]{1,0:T(8,128)(2,1)S(1)}, u32[]{:S(2)}, u32[]{:S(2)}) collective-permute-start(bf16[384,128]{1,0:T(8,128)(2,1)S(1)} %shrink.1), channel_id=1, source_target_pairs={{0,1},{1,0},{2,3},{3,2},{4,5},{5,4},{6,7},{7,6},{8,9},{9,8},{10,11... | collective-permute-start | bytes 294920 | tf_op jit(solution)/shard_map/ppermute | solution.py:38
  64.1 18.4 %collective-permute-start.25 = (bf16[2,352,512]{2,1,0:T(8,128)(2,1)S(1)}, bf16[2,352,512]{2,1,0:T(8,128)(2,1)S(1)}, u32[]{:S(2)}, u32[]{:S(2)}) collective-permute-start(bf16[2,352,512]{2,1,0:T(8,128)(2,1)S(1)} %add_convert_fusion.2), channel_id=1, source_target_pairs={{0,2},{1,7},{2,4},{3,1},{4,6},{5,3},{6,0},{7,5},{8,10},{9,15},{10,... | collective-permute-start | bytes 2162696 | tf_op jit(solution)/shard_map/ppermute | solution.py:53
  65.4 4.7 %collective-permute-start.11 = (bf16[384,128]{1,0:T(8,128)(2,1)S(1)}, bf16[384,128]{1,0:T(8,128)(2,1)S(1)}, u32[]{:S(2)}, u32[]{:S(2)}) collective-permute-start(bf16[384,128]{1,0:T(8,128)(2,1)S(1)} %add_convert_fusion.8), channel_id=1, source_target_pairs={{0,8},{8,0},{1,9},{9,1},{2,10},{10,2},{3,11},{11,3},{4,12},{12,4},... | collective-permute-start | bytes 294920 | tf_op jit(solution)/shard_map/ppermute | solution.py:38
  66.6 26.2 %copy-start.6 = (s32[12]{0:T(128)S(1)}, s32[12]{0:T(128)}, u32[]{:S(2)}) copy-start(s32[12]{0:T(128)} %count_ref.1) | copy-start | bytes 148
  66.6 15.8 %collective-permute-start.17 = (bf16[8,64,512]{2,1,0:T(8,128)(2,1)S(1)}, bf16[8,64,512]{2,1,0:T(8,128)(2,1)S(1)}, u32[]{:S(2)}, u32[]{:S(2)}) collective-permute-start(bf16[8,64,512]{2,1,0:T(8,128)(2,1)S(1)} %pad_maximum_fusion.rest_0_), channel_id=1, source_target_pairs={{0,64},{1,193},{64,128},{65,1},{128,192},{129,65},{192,0},{193,129... | collective-permute-start | bytes 1572872 | tf_op jit(solution)/shard_map/ppermute | solution.py:53
  68.2 21.9 %collective-permute-start.16 = (bf16[8,64,512]{2,1,0:T(8,128)(2,1)S(1)}, bf16[8,64,512]{2,1,0:T(8,128)(2,1)S(1)}, u32[]{:S(2)}, u32[]{:S(2)}) collective-permute-start(bf16[8,64,512]{2,1,0:T(8,128)(2,1)S(1)} %pad_maximum_fusion.rest_0_), channel_id=1, source_target_pairs={{0,192},{1,65},{64,0},{65,129},{128,64},{129,193},{192,128},{193,1... | collective-permute-start | bytes 1572872 | tf_op jit(solution)/shard_map/ppermute | solution.py:53
  70.2 13.7 %collective-permute-start.12 = (bf16[384,128]{1,0:T(8,128)(2,1)S(1)}, bf16[384,128]{1,0:T(8,128)(2,1)S(1)}, u32[]{:S(2)}, u32[]{:S(2)}) collective-permute-start(bf16[384,128]{1,0:T(8,128)(2,1)S(1)} %add_convert_fusion.7), channel_id=1, source_target_pairs={{0,2},{2,0},{4,6},{6,4},{1,3},{3,1},{5,7},{7,5},{8,10},{10,8},{12,... | collective-permute-start | bytes 294920 | tf_op jit(solution)/shard_map/ppermute | solution.py:43
  73.4 20.7 %collective-permute-start.22 = (bf16[1,416,512]{2,1,0:T(8,128)(2,1)S(1)}, bf16[1,416,512]{2,1,0:T(8,128)(2,1)S(1)}, u32[]{:S(2)}, u32[]{:S(2)}) collective-permute-start(bf16[1,416,512]{2,1,0:T(8,128)(2,1)S(1)} %add_convert_fusion.4), channel_id=1, source_target_pairs={{0,8},{8,0},{1,9},{9,1},{2,10},{10,2},{3,11},{11,3},{4,12},{12,4},... | collective-permute-start | bytes 1277960 | tf_op jit(solution)/shard_map/ppermute | solution.py:38
  82.5 10.4 %collective-permute-start.21 = (bf16[8,64,512]{2,1,0:T(8,128)(2,1)S(1)}, bf16[8,64,512]{2,1,0:T(8,128)(2,1)S(1)}, u32[]{:S(2)}, u32[]{:S(2)}) collective-permute-start(bf16[8,64,512]{2,1,0:T(8,128)(2,1)S(1)} %collective-permute-done.17.rest_3_), channel_id=1, source_target_pairs={{0,64},{1,193},{64,128},{65,1},{128,192},{129,65},{192,0},{193,129... | collective-permute-start | bytes 1572872 | tf_op jit(solution)/shard_map/ppermute | solution.py:53
  82.6 11.6 %collective-permute-start.26 = (bf16[1,352,512]{2,1,0:T(8,128)(2,1)S(1)}, bf16[1,352,512]{2,1,0:T(8,128)(2,1)S(1)}, u32[]{:S(2)}, u32[]{:S(2)}) collective-permute-start(bf16[1,352,512]{2,1,0:T(8,128)(2,1)S(1)} %add_convert_fusion.5), channel_id=1, source_target_pairs={{0,8},{8,0},{1,9},{9,1},{2,10},{10,2},{3,11},{11,3},{4,12},{12,4},... | collective-permute-start | bytes 1081352 | tf_op jit(solution)/shard_map/ppermute | solution.py:38
  83.9 6.2 %collective-permute-start.13 = (bf16[384,128]{1,0:T(8,128)(2,1)S(1)}, bf16[384,128]{1,0:T(8,128)(2,1)S(1)}, u32[]{:S(2)}, u32[]{:S(2)}) collective-permute-start(bf16[384,128]{1,0:T(8,128)(2,1)S(1)} %add_convert_fusion.6.s0), channel_id=1, source_target_pairs={{0,4},{2,6},{4,0},{6,2},{1,5},{3,7},{5,1},{7,3},{8,12},{10,14},{12... | collective-permute-start | bytes 294920 | tf_op jit(solution)/shard_map/ppermute | solution.py:43
